TPU v7x, 128 devices: a whole 4x4x4 slice. The times are simulated.
128 devices in a mesh: wide: 16 (over x_hi, z, core), narrow: 8 (over y, x_lo).
Axes of the slice: x: 4 (x_hi: 2, x_lo: 2; x = x_hi * 2 + x_lo), y: 4, z: 4, core: 2. Of those that a mesh axis runs over, the one named last changes fastest.
Arguments:
- velocity: float32 [3, 128, 128, 512], P(None, 'wide', 'narrow'), may hold values from -4 to 4
- bfield: float32 [128, 128, 512], P('wide', 'narrow'), may hold values from 1 to 3
Outputs:
- force: float32 [3, 128, 128, 512], P(None, 'wide', 'narrow')
- pressure: float32 [128, 128, 512], P('wide', 'narrow')
All inputs are finite; a program needn't handle non-finite values.
Results may differ from a plain program's by a relative error of at most 0.00023.
Values sent between devices are 32-bit elements; how exact they have to be, the bound alone decides.
No kernel may reach another device: no remote copies, remote signals or barrier semaphores. Data moves between devices by JAX's collectives and lax.ppermute only.
A program may use at most 128 MiB of HBM per device.

v0:
```python
import ml_dtypes
import jax
import jax.numpy as jnp
import numpy as np
from jax import lax
from jax.experimental import pallas as pl
from jax.experimental.pallas import tpu as pltpu
from jax.sharding import PartitionSpec as P

F32 = jnp.float32
BF16 = jnp.bfloat16
MIB = 2**20


def legendre_pair(degree, points):
    below, current = np.ones(points.shape), points * 1.0
    for step in range(2, degree + 1):
        below, current = current, ((2 * step - 1) * points * current - (step - 1) * below) / step
    return current, below


def tables_1d():
    points = np.cos(np.pi * np.arange(8) / 7)
    for _ in range(60):
        top, below = legendre_pair(7, points)
        points = points - (points * top - below) / (8 * top)
    points = np.sort(points)
    top, below = legendre_pair(7, points)
    w = 2.0 / (56 * top**2)
    spacing = points[:, None] - points[None, :] + np.eye(8)
    deriv = top[:, None] / (top[None, :] * spacing) * (1.0 - np.eye(8))
    deriv[0, 0], deriv[-1, -1] = -14.0, 14.0
    gauss = np.cos(np.pi * (np.arange(12) + 0.75) / 12.5)
    for _ in range(60):
        top, below = legendre_pair(12, gauss)
        gauss = gauss - top / (12 * (gauss * top - below) / (gauss**2 - 1.0))
    top, below = legendre_pair(12, gauss)
    slope = 12 * (gauss * top - below) / (gauss**2 - 1.0)
    v = 2.0 / ((1.0 - gauss**2) * slope**2)
    interp = np.ones((12, 8))
    for col in range(8):
        for other in range(8):
            if other != col:
                interp[:, col] *= (gauss - points[other]) / (points[col] - points[other])
    stiff = deriv.T @ (w[:, None] * deriv)
    wide_stiff, wide_mass = np.zeros((22, 22)), np.zeros(22)
    for el in range(3):
        r = 7 * el
        wide_stiff[r : r + 8, r : r + 8] += stiff
        wide_mass[r : r + 8] += w
    scale = 1.0 / np.sqrt(wide_mass[6:16])
    lam, vec = np.linalg.eigh(scale[:, None] * wide_stiff[6:16, 6:16] * scale[None, :])
    return interp, interp @ deriv, deriv, stiff, w, scale[:, None] * vec, lam, v


def hi_lo(m):
    hi = m.astype(ml_dtypes.bfloat16)
    return hi, (m - hi.astype(np.float64)).astype(ml_dtypes.bfloat16)


def left_const(m):
    hi, lo = hi_lo(m)
    return np.concatenate([hi, hi, lo], axis=1)


def right_const(m):
    hi, lo = hi_lo(m)
    return np.concatenate([hi, hi, lo], axis=0)


def block_diag(m, count):
    return np.kron(np.eye(count), m)


def own(z, x):
    return 16 * z + x


def local_rows(terms, xs):
    out = np.zeros((8 * len(xs), 128))
    for k, x in enumerate(xs):
        el, j = divmod(x, 8)
        for z in range(8):
            for zm, xm in terms:
                for z2 in range(8):
                    for j2 in range(8):
                        out[8 * k + z, own(z2, 8 * el + j2)] += zm[z, z2] * xm[j, j2]
    return out


def extended_rows(terms):
    local = local_rows(terms, range(16)).reshape(16, 8, 128)
    out = np.zeros((144, 144))
    for x in range(16):
        for z in range(8):
            out[own(z, x), :128] = local[x, z]
            if x in (7, 8):
                out[own(z, x), :128] += local[15 - x, z]
    for z in range(8):
        for zm, xm in terms:
            for z2 in range(8):
                out[own(z, 0), 128 + z2] += zm[z, z2] * xm[7, 7]
                out[128 + z, 128 + z2] += zm[z, z2] * xm[6, 7]
                out[own(z, 15), 136 + z2] += zm[z, z2] * xm[0, 0]
                out[136 + z, 136 + z2] += zm[z, z2] * xm[1, 0]
    return out


def box_rows(vec):
    nodes = np.zeros((10, 2, 10, 240))

    def put(zk, el, xk, z, place):
        if xk == 0 and el == 0:
            x = "l"
        elif xk == 9 and el == 1:
            x = "r"
        else:
            x = 8 * el + (-2 if xk == 0 else 9 if xk == 9 else xk - 1)
        side = {"l": 0, "r": 8}.get(x)
        if place == "own":
            row = own(z, x) if side is None else 128 + side + z
        elif place == "below":
            row = 144 + ((z - 6) * 16 + x if side is None else 32 + side + z)
        else:
            row = 192 + (z * 16 + x if side is None else 32 + side + z)
        nodes[zk, el, xk, row] += 1.0

    for el in range(2):
        for xk in range(10):
            put(0, el, xk, 6, "below")
            put(1, el, xk, 7, "below")
            put(8, el, xk, 0, "above")
            put(9, el, xk, 1, "above")
            for z in range(8):
                put(z + 1, el, xk, z, "own")
    into = np.einsum("zi,xj,zexr->iejr", vec, vec, nodes).reshape(200, 240)
    back = np.zeros((8, 16, 10, 2, 10))
    inner = vec[1:9]
    for z in range(8):
        for x in range(16):
            el, j = divmod(x, 8)
            block = inner[z][:, None] * inner[j][None, :]
            if x in (7, 8):
                back[z, x, :, el] += 0.5 * block
                back[z, x, :, 1 - el] += 0.5 * inner[z][:, None] * inner[7 - j][None, :]
            else:
                back[z, x, :, el] += block
    back = back.reshape(128, 200)
    return np.pad(into, ((0, 8), (0, 0))), np.pad(back, ((0, 0), (0, 8)))


def box_lanes(vec, count):
    into = np.zeros((8 * count, 10 * count))
    back = np.zeros((10 * count, 8 * count))
    for e in range(count):
        spots = [8 * e - 2] + list(range(8 * e, 8 * e + 8)) + [8 * e + 9]
        for k, y in enumerate(spots):
            if 0 <= y < 8 * count:
                into[y, 10 * e : 10 * e + 10] += vec[k]
        for j in range(8):
            col = vec[j + 1]
            y = 8 * e + j
            if j == 0 and e > 0:
                back[10 * e : 10 * e + 10, [y - 1, y]] += 0.5 * col[:, None]
            elif j == 7 and e < count - 1:
                back[10 * e : 10 * e + 10, [y, y + 1]] += 0.5 * col[:, None]
            else:
                back[10 * e : 10 * e + 10, y] += col
    return into, back


def constants():
    interp, slopes, deriv, stiff, w, vec, lam, v = tables_1d()
    eye2 = np.eye(2)
    zx = lambda a, b: np.kron(a, np.kron(eye2, b))
    c = {}
    c["y_in"] = right_const(
        np.concatenate([block_diag(interp.T, 32), block_diag(slopes.T, 32)], axis=1)
    )
    c["zx_in"] = left_const(
        np.concatenate([zx(interp, interp), zx(slopes, interp), zx(interp, slopes)], axis=0)
    )
    test = v[:, None] * interp
    back = zx(test.T, test.T).reshape(8, 16, 288)
    pair = back[:, 7] + back[:, 8]
    back[:, 7], back[:, 8] = pair, pair
    c["zx_out"] = left_const(back.reshape(128, 288))
    c["y_out"] = right_const(block_diag(test, 32))
    wm, wd = np.diag(w), w[:, None] * deriv
    parts = ([(wd, wm)], [(wm, wd)], [(wm, wm)])
    sides = (14, 15, 1, 0)
    c["div_msg01"] = left_const(np.concatenate([local_rows(t, sides) for t in parts[:2]], 1))
    c["div_msg2"] = left_const(local_rows(parts[2], sides))
    c["div01"] = left_const(np.concatenate([extended_rows(t) for t in parts[:2]], 1))
    c["div2"] = left_const(extended_rows(parts[2]))
    kterms = [(stiff, wm), (wm, stiff)]
    c["st_msg"] = left_const(
        np.concatenate([local_rows(kterms, sides), local_rows(parts[2], sides)], 0)
    )
    c["st"] = left_const(np.concatenate([extended_rows(kterms), extended_rows(parts[2])], 0))
    c["wd_y"] = right_const(block_diag(wd.T, 32))
    c["k_y"] = right_const(block_diag(stiff.T, 32))
    c["w_y"] = np.tile(w, 64)[None].astype(np.float32)
    into, back = box_rows(vec)
    c["box_in"], c["box_out"] = left_const(into), left_const(back)
    into, back = box_lanes(vec, 64)
    c["ybox_in"], c["ybox_out"] = right_const(into), right_const(back)
    inv = 1.0 / (lam[:, None, None, None] + lam[None, None, :, None] + lam)
    inv = np.broadcast_to(inv[:, :, :, None, :], (10, 1, 10, 64, 10))
    inv = np.broadcast_to(inv, (10, 2, 10, 64, 10)).reshape(200, 640)
    c["inv"] = np.pad(inv, ((0, 8), (0, 0))).astype(np.float32)
    return c


def split(x):
    hi = x.astype(BF16)
    return hi, (x - hi.astype(F32)).astype(BF16)


def rmul(x, const):
    hi, lo = split(x)
    return jnp.dot(jnp.concatenate([hi, lo, hi], axis=1), const, preferred_element_type=F32)


def lmul(const, x):
    hi, lo = split(x)
    return jnp.dot(const, jnp.concatenate([hi, lo, hi], axis=0), preferred_element_type=F32)


def rmul_halves(x, const):
    return jnp.concatenate([rmul(x[:, :256], const), rmul(x[:, 256:], const)], axis=1)


def dss_lanes(x):
    lane = lax.broadcasted_iota(jnp.int32, x.shape, 1)
    n = x.shape[1]
    up = jnp.where((lane % 8 == 7) & (lane < n - 1), pltpu.roll(x, n - 1, 1), 0.0)
    down = jnp.where((lane % 8 == 0) & (lane > 0), pltpu.roll(x, 1, 1), 0.0)
    return x + up + down


def flags():
    z, x = lax.axis_index("wide"), lax.axis_index("narrow")
    nz, nx = lax.axis_size("wide"), lax.axis_size("narrow")
    as_flag = lambda t: t.astype(F32)
    return as_flag(z > 0), as_flag(z < nz - 1), as_flag(x > 0), as_flag(x < nx - 1)


def force_kernel(v_ref, b_ref, y_in, zx_in, zx_out, y_out, f_ref, up_ref, down_ref):
    v = v_ref[...].reshape(384, 512)
    b = b_ref[...].reshape(128, 512)
    halves = []
    for h in range(2):
        cut = slice(256 * h, 256 * h + 256)
        first = rmul(v[:, cut], y_in[...])
        bq = lmul(zx_in[:288, :], rmul(b[:, cut], y_in[:, :384]))
        u, gz, gx, gy = [], [], [], []
        for c in range(3):
            rows = slice(128 * c, 128 * c + 128)
            most = lmul(zx_in[...], first[rows, :384])
            u.append(most[:288])
            gz.append(most[288:576])
            gx.append(most[576:])
            gy.append(lmul(zx_in[:288, :], first[rows, 384:]))
        b2 = bq * bq
        back = []
        for c in range(3):
            conv = u[0] * gz[c] + u[1] * gx[c] + u[2] * gy[c]
            if c != 1:
                conv = conv + b2 * u[c]
            back.append(lmul(zx_out[...], -conv))
        halves.append(rmul(jnp.concatenate(back, axis=0), y_out[...]))
    f = dss_lanes(jnp.concatenate(halves, axis=1))
    f_ref[...] = f
    for c in range(3):
        up_ref[16 * c : 16 * c + 16] = f[128 * c + 112 : 128 * c + 128]
        down_ref[16 * c : 16 * c + 16] = f[128 * c : 128 * c + 16]


def edge(ref, base, x):
    return jnp.concatenate([ref[base + x + 16 * z : base + x + 16 * z + 1] for z in range(8)], axis=0)


def add_edge(ref, base, x, rows):
    for z in range(8):
        ref[base + x + 16 * z : base + x + 16 * z + 1] += rows[z : z + 1]


def div_msg_kernel(f_ref, fb_ref, fa_ref, m01, m2, wd_y, w_y, fz_ref, r_ref, l_ref):
    has_b, has_a, _, _ = flags()
    fz_ref[...] = f_ref[...]
    for c in range(3):
        piece = slice(16 * c, 16 * c + 16)
        fz_ref[128 * c : 128 * c + 16] += fb_ref[piece] * has_b
        fz_ref[128 * c + 112 : 128 * c + 128] += fa_ref[piece] * has_a
    f = fz_ref[...]
    s = lmul(m01[...], f[:256]) * w_y[...] + rmul_halves(lmul(m2[...], f[256:]), wd_y[...])
    r_ref[:16] = s[:16]
    l_ref[:16] = s[16:]
    for c in range(3):
        r_ref[16 + 8 * c : 24 + 8 * c] = edge(fz_ref, 128 * c, 15)
        l_ref[16 + 8 * c : 24 + 8 * c] = edge(fz_ref, 128 * c, 0)


def extend_into(s, from_l, from_r, out_ref, acc_ref):
    acc_ref[...] = s
    add_edge(acc_ref, 0, 0, from_l[8:16])
    add_edge(acc_ref, 0, 15, from_r[8:16])
    acc_ref[128:136] += from_l[:8]
    acc_ref[136:144] += from_r[:8]
    return dss_lanes(acc_ref[...])


def layers_out(s, up_ref, down_ref):
    up_ref[:32] = s[96:128]
    up_ref[32:] = s[128:]
    down_ref[:32] = s[:32]
    down_ref[32:] = s[128:]


def div_kernel(
    fz_ref, ml_ref, mr_ref, m01, m2, wd_y, w_y, f_ref, s_ref, up_ref, down_ref, acc_ref
):
    _, _, has_l, has_r = flags()
    ml, mr = ml_ref[...] * has_l, mr_ref[...] * has_r
    f_ref[...] = fz_ref[...]
    rows = []
    for c in range(3):
        base = 128 * c
        add_edge(f_ref, base, 0, ml[16 + 8 * c : 24 + 8 * c])
        add_edge(f_ref, base, 15, mr[16 + 8 * c : 24 + 8 * c])
        rows += [
            f_ref[base : base + 128],
            edge(fz_ref, base, 0) * has_l,
            edge(fz_ref, base, 15) * has_r,
        ]
    f01 = jnp.concatenate(rows[:6], axis=0)
    f2 = jnp.concatenate(rows[6:], axis=0)
    s = lmul(m01[...], f01) * w_y[...] + rmul_halves(lmul(m2[...], f2), wd_y[...])
    s = extend_into(s, ml, mr, s_ref, acc_ref)
    s_ref[...] = s
    layers_out(s, up_ref, down_ref)


def box_kernel(s_ref, sb_ref, sa_ref, box_in, ybox_in, inv, box_out, ybox_out, g_ref, up_ref, down_ref):
    has_b, has_a, has_l, has_r = flags()
    s = jnp.concatenate([s_ref[...], sb_ref[...] * has_b, sa_ref[...] * has_a], axis=0)
    t = rmul(lmul(box_in[...], s), ybox_in[...]) * inv[...]
    g = rmul(lmul(box_out[...], t), ybox_out[...])
    row = lax.broadcasted_iota(jnp.int32, (128, 1), 0)
    z, x = row // 16, row % 16
    weight = 1.0 - 0.5 * jnp.where(z == 0, has_b, jnp.where(z == 7, has_a, 0.0))
    weight = weight * (1.0 - 0.5 * jnp.where(x == 0, has_l, jnp.where(x == 15, has_r, 0.0)))
    g = g * weight
    g_ref[...] = g
    up_ref[...] = g[112:]
    down_ref[...] = g[:16]


def join_z(g_ref, gb_ref, ga_ref, out_ref):
    has_b, has_a, _, _ = flags()
    out_ref[...] = g_ref[...]
    out_ref[:16] += gb_ref[...] * has_b
    out_ref[112:] += ga_ref[...] * has_a


def stiff_msg_kernel(g_ref, gb_ref, ga_ref, st_msg, k_y, w_y, gz_ref, r_ref, l_ref):
    join_z(g_ref, gb_ref, ga_ref, gz_ref)
    both = lmul(st_msg[...], gz_ref[...])
    s = both[:32] * w_y[...] + rmul_halves(both[32:], k_y[...])
    r_ref[:16] = s[:16]
    l_ref[:16] = s[16:]
    r_ref[16:] = edge(gz_ref, 0, 15)
    l_ref[16:] = edge(gz_ref, 0, 0)


def stiff_kernel(
    gz_ref, ml_ref, mr_ref, s_ref, st, k_y, w_y, p_ref, res_ref, up_ref, down_ref, acc_ref
):
    _, _, has_l, has_r = flags()
    ml, mr = ml_ref[...] * has_l, mr_ref[...] * has_r
    p_ref[...] = gz_ref[...]
    add_edge(p_ref, 0, 0, ml[16:])
    add_edge(p_ref, 0, 15, mr[16:])
    rows = [p_ref[...], edge(gz_ref, 0, 0) * has_l, edge(gz_ref, 0, 15) * has_r]
    both = lmul(st[...], jnp.concatenate(rows, axis=0))
    s = both[:144] * w_y[...] + rmul_halves(both[144:], k_y[...])
    res = s_ref[...] - extend_into(s, ml, mr, res_ref, acc_ref)
    res_ref[...] = res
    layers_out(res, up_ref, down_ref)


def last_z_kernel(g_ref, gb_ref, ga_ref, p_ref, out_ref, r_ref, l_ref):
    join_z(g_ref, gb_ref, ga_ref, out_ref)
    r_ref[...] = edge(out_ref, 0, 15)
    l_ref[...] = edge(out_ref, 0, 0)
    out_ref[...] += p_ref[...]


def last_x_kernel(g_ref, ml_ref, mr_ref, out_ref):
    _, _, has_l, has_r = flags()
    out_ref[...] = g_ref[...]
    add_edge(out_ref, 0, 0, ml_ref[...] * has_l)
    add_edge(out_ref, 0, 15, mr_ref[...] * has_r)


def call(kernel, name, outs, *args, scratch=(), vmem=16):
    shape = lambda rows: jax.ShapeDtypeStruct(rows if isinstance(rows, tuple) else (rows, 512), F32)
    spec = pl.BlockSpec(memory_space=pltpu.VMEM)
    return pl.pallas_call(
        kernel,
        out_shape=[shape(o) for o in outs],
        in_specs=[spec] * len(args),
        out_specs=[spec] * len(outs),
        scratch_shapes=[pltpu.VMEM((rows, 512), F32) for rows in scratch],
        compiler_params=pltpu.CompilerParams(vmem_limit_bytes=vmem * MIB),
        name=name,
    )(*args)


def exchange(axis, forward, backward):
    n = lax.axis_size(axis)
    ahead = [(i, (i + 1) % n) for i in range(n)]
    behind = [(j, i) for i, j in ahead]
    return lax.ppermute(forward, axis, ahead), lax.ppermute(backward, axis, behind)


def shards(velocity, bfield):
    c = {name: jnp.asarray(value) for name, value in constants().items()}
    consts = lambda *names: [c[name] for name in names]
    f, up, down = call(
        force_kernel,
        "force",
        (384, 48, 48),
        velocity,
        bfield,
        *consts("y_in", "zx_in", "zx_out", "y_out"),
        vmem=40,
    )
    below, above = exchange("wide", up, down)
    fz, right, left = call(
        div_msg_kernel,
        "div_msg",
        (384, 40, 40),
        f,
        below,
        above,
        *consts("div_msg01", "div_msg2", "wd_y", "w_y"),
    )
    from_l, from_r = exchange("narrow", right, left)
    force, s, up, down = call(
        div_kernel,
        "div",
        (384, 144, 48, 48),
        fz,
        from_l,
        from_r,
        *consts("div01", "div2", "wd_y", "w_y"),
        scratch=(144,),
    )
    box = consts("box_in", "ybox_in", "inv", "box_out", "ybox_out")
    below, above = exchange("wide", up, down)
    g, up, down = call(box_kernel, "box_first", (128, 16, 16), s, below, above, *box)
    below, above = exchange("wide", up, down)
    gz, right, left = call(
        stiff_msg_kernel,
        "stiff_msg",
        (128, 24, 24),
        g,
        below,
        above,
        *consts("st_msg", "k_y", "w_y"),
    )
    from_l, from_r = exchange("narrow", right, left)
    first, res, up, down = call(
        stiff_kernel,
        "stiff",
        (128, 144, 48, 48),
        gz,
        from_l,
        from_r,
        s,
        *consts("st", "k_y", "w_y"),
        scratch=(144,),
    )
    below, above = exchange("wide", up, down)
    g, up, down = call(box_kernel, "box_second", (128, 16, 16), res, below, above, *box)
    below, above = exchange("wide", up, down)
    total, right, left = call(last_z_kernel, "last_z", (128, 8, 8), g, below, above, first)
    from_l, from_r = exchange("narrow", right, left)
    (pressure,) = call(last_x_kernel, "last_x", (128,), total, from_l, from_r)
    return force.reshape(3, 8, 16, 512), pressure.reshape(8, 16, 512)


def solution(mesh):
    placed = (P(None, "wide", "narrow", None), P("wide", "narrow", None))
    return jax.shard_map(
        shards, mesh=mesh, in_specs=placed, out_specs=placed, check_vma=False
    )
```

profile of v0, /device:TPU:6, one launch (start us, length us, event | category | flops | bytes accessed | tf_op | source)
XLA Modules:
  0.0 78.0 jit_solution(336222128041316361)
XLA Ops:
  0.6 0.0 copy-start.4
  0.6 0.0 copy-start.6
  0.7 1.3 %copy-done.6 = bf16[768,768]{1,0:T(8,128)(2,1)S(1)} copy-done((bf16[768,768]{1,0:T(8,128)(2,1)S(1)}, bf16[768,768]{1,0:T(8,128)(2,1)}, u32[]{:S(2)}) %copy-start.6) | copy-done | bytes 1179672
  2.0 1.1 %copy-done.7 = f32[3,8,16,512]{3,2,1,0:T(8,128)S(1)} copy-done((f32[3,8,16,512]{3,2,1,0:T(8,128)S(1)}, f32[3,8,16,512]{3,2,1,0:T(8,128)}, u32[]{:S(2)}) %copy-start.7) | copy-done | bytes 786456
  3.1 1.1 %copy-done.8 = bf16[864,384]{1,0:T(8,128)(2,1)S(1)} copy-done((bf16[864,384]{1,0:T(8,128)(2,1)S(1)}, bf16[864,384]{1,0:T(8,128)(2,1)}, u32[]{:S(2)}) %copy-start.8) | copy-done | bytes 663576
  4.2 1.1 %copy-done.10 = bf16[1152,256]{1,0:T(8,128)(2,1)S(1)} copy-done((bf16[1152,256]{1,0:T(8,128)(2,1)S(1)}, bf16[1152,256]{1,0:T(8,128)(2,1)}, u32[]{:S(2)}) %copy-start.10) | copy-done | bytes 589848
  5.3 0.9 %copy-done.12 = f32[8,16,512]{2,1,0:T(8,128)S(1)} copy-done((f32[8,16,512]{2,1,0:T(8,128)S(1)}, f32[8,16,512]{2,1,0:T(8,128)}, u32[]{:S(2)}) %copy-start.12) | copy-done | bytes 262168
  6.2 0.9 %copy-done.14 = bf16[128,864]{1,0:T(8,128)(2,1)S(1)} copy-done((bf16[128,864]{1,0:T(8,128)(2,1)S(1)}, bf16[128,864]{1,0:T(8,128)(2,1)}, u32[]{:S(2)}) %copy-start.14) | copy-done | bytes 221208
  7.2 0.0 copy-start.15
  7.2 0.0 copy-start.1
  7.2 7.2 %force.1 = (f32[384,512]{1,0:T(8,128)S(1)}, f32[48,512]{1,0:T(8,128)S(1)}, f32[48,512]{1,0:T(8,128)S(1)}) custom-call(f32[3,8,16,512]{3,2,1,0:T(8,128)S(1)} %copy-done.7, f32[8,16,512]{2,1,0:T(8,128)S(1)} %copy-done.12, bf16[768,768]{1,0:T(8,128)(2,1)S(1)} %copy-done.6, bf16[864,384]{1,0:T(8,128)(2,1)S(1)} %copy-done.8, bf16[128,864]{1,0:T(8,128)(2,1)S(1)} %copy-done.14, ...), custom_call_target="tpu_custom_call" | custom-call | tf_op jit(solution)/shard_map/force/pallas_call | solution.py:410
  14.4 0.0 copy-start
  14.4 0.0 copy-start.2
  14.5 0.0 copy-start.5
  14.5 0.0 copy-start.9
  14.5 0.1 collective-permute-start
  14.6 5.3 %collective-permute-start.1 = (f32[48,512]{1,0:T(8,128)S(1)}, f32[48,512]{1,0:T(8,128)S(1)}, u32[]{:S(2)}, u32[]{:S(2)}) collective-permute-start(f32[48,512]{1,0:T(8,128)S(1)} %get-tuple-element.30), channel_id=1, source_target_pairs={{8,0},{16,8},{24,16},{32,24},{40,32},{48,40},{56,48},{64,56},{72,6... | collective-permute-start | bytes 294920 | tf_op jit(solution)/shard_map/ppermute | solution.py:425
  19.9 2.3 %collective-permute-done.fb_ref = f32[48,512]{1,0:T(8,128)S(1)} collective-permute-done((f32[48,512]{1,0:T(8,128)S(1)}, f32[48,512]{1,0:T(8,128)S(1)}, u32[]{:S(2)}, u32[]{:S(2)}) %collective-permute-start) | collective-permute-done | bytes 98336 | tf_op jit(solution)/shard_map/ppermute | solution.py:425
  22.2 0.0 collective-permute-done.1.fa_ref
  22.2 0.0 copy-done.4
  22.2 0.0 copy-done.16
  22.2 0.0 copy-done.18
  22.2 0.0 copy-done.19
  22.2 0.6 div_msg.1
  22.9 1.9 %collective-permute-start.2 = (f32[40,512]{1,0:T(8,128)S(1)}, f32[40,512]{1,0:T(8,128)S(1)}, u32[]{:S(2)}, u32[]{:S(2)}) collective-permute-start(f32[40,512]{1,0:T(8,128)S(1)} %get-tuple-element.32), channel_id=1, source_target_pairs={{0,1},{1,2},{2,3},{3,4},{4,5},{5,6},{6,7},{7,0},{8,9},{9,10},{10,1... | collective-permute-start | bytes 245768 | tf_op jit(solution)/shard_map/ppermute | solution.py:425
  24.7 0.2 collective-permute-start.3
  24.9 3.0 %collective-permute-done.2.ml_ref = f32[40,512]{1,0:T(8,128)S(1)} collective-permute-done((f32[40,512]{1,0:T(8,128)S(1)}, f32[40,512]{1,0:T(8,128)S(1)}, u32[]{:S(2)}, u32[]{:S(2)}) %collective-permute-start.2) | collective-permute-done | bytes 81952 | tf_op jit(solution)/shard_map/ppermute | solution.py:425
  27.9 2.2 %collective-permute-done.3.mr_ref = f32[40,512]{1,0:T(8,128)S(1)} collective-permute-done((f32[40,512]{1,0:T(8,128)S(1)}, f32[40,512]{1,0:T(8,128)S(1)}, u32[]{:S(2)}, u32[]{:S(2)}) %collective-permute-start.3) | collective-permute-done | bytes 81952 | tf_op jit(solution)/shard_map/ppermute | solution.py:425
  30.1 0.0 copy-done.13
  30.1 0.0 copy-done.15
  30.1 1.2 %div.1 = (f32[384,512]{1,0:T(8,128)}, f32[144,512]{1,0:T(8,128)S(1)}, f32[48,512]{1,0:T(8,128)S(1)}, f32[48,512]{1,0:T(8,128)S(1)}) custom-call(f32[384,512]{1,0:T(8,128)S(1)} %get-tuple-element.31.fz_ref, f32[40,512]{1,0:T(8,128)S(1)} %collective-permute-done.2.ml_ref, f32[40,512]{1,0:T(8,128)S(1)} %collective-permute-done.3.mr_ref, ...), custom_call_target="tpu_custom_call" | custom-call | tf_op jit(solution)/shard_map/div/pallas_call | solution.py:410
  31.2 0.0 collective-permute-start.4
  31.3 5.4 %collective-permute-start.5 = (f32[48,512]{1,0:T(8,128)S(1)}, f32[48,512]{1,0:T(8,128)S(1)}, u32[]{:S(2)}, u32[]{:S(2)}) collective-permute-start(f32[48,512]{1,0:T(8,128)S(1)} %get-tuple-element.37), channel_id=1, source_target_pairs={{8,0},{16,8},{24,16},{32,24},{40,32},{48,40},{56,48},{64,56},{72,6... | collective-permute-start | bytes 294920 | tf_op jit(solution)/shard_map/ppermute | solution.py:425
  36.6 2.3 %collective-permute-done.4.sb_ref = f32[48,512]{1,0:T(8,128)S(1)} collective-permute-done((f32[48,512]{1,0:T(8,128)S(1)}, f32[48,512]{1,0:T(8,128)S(1)}, u32[]{:S(2)}, u32[]{:S(2)}) %collective-permute-start.4) | collective-permute-done | bytes 98336 | tf_op jit(solution)/shard_map/ppermute | solution.py:425
  38.9 0.0 collective-permute-done.5.sa_ref
  38.9 0.0 copy-start.3
  39.0 0.0 copy-start.17
  39.0 0.0 copy-start.11
  39.0 1.5 %box_first.1 = (f32[128,512]{1,0:T(8,128)S(1)}, f32[16,512]{1,0:T(8,128)S(1)}, f32[16,512]{1,0:T(8,128)S(1)}) custom-call(f32[144,512]{1,0:T(8,128)S(1)} %get-tuple-element.35.s_ref, f32[48,512]{1,0:T(8,128)S(1)} %collective-permute-done.4.sb_ref, f32[48,512]{1,0:T(8,128)S(1)} %collective-permute-done.5.sa_ref, bf16[208,720]{1,0:T(8,128)(2,1)S(1)} %copy-done.5, ...), custom_call_target="tpu_custom_call" | custom-call | tf_op jit(solution)/shard_map/box_first/pallas_call | solution.py:410
  40.5 0.1 collective-permute-start.6
  40.6 5.6 %collective-permute-start.7 = (f32[16,512]{1,0:T(8,128)S(1)}, f32[16,512]{1,0:T(8,128)S(1)}, u32[]{:S(2)}, u32[]{:S(2)}) collective-permute-start(f32[16,512]{1,0:T(8,128)S(1)} %get-tuple-element.40), channel_id=1, source_target_pairs={{8,0},{16,8},{24,16},{32,24},{40,32},{48,40},{56,48},{64,56},{72,6... | collective-permute-start | bytes 98312 | tf_op jit(solution)/shard_map/ppermute | solution.py:425
  46.2 1.3 %collective-permute-done.6.gb_ref = f32[16,512]{1,0:T(8,128)S(1)} collective-permute-done((f32[16,512]{1,0:T(8,128)S(1)}, f32[16,512]{1,0:T(8,128)S(1)}, u32[]{:S(2)}, u32[]{:S(2)}) %collective-permute-start.6) | collective-permute-done | bytes 32800 | tf_op jit(solution)/shard_map/ppermute | solution.py:425
  47.5 0.3 collective-permute-done.7.ga_ref
  47.8 0.4 stiff_msg.1
  48.2 1.0 %collective-permute-start.8 = (f32[24,512]{1,0:T(8,128)S(1)}, f32[24,512]{1,0:T(8,128)S(1)}, u32[]{:S(2)}, u32[]{:S(2)}) collective-permute-start(f32[24,512]{1,0:T(8,128)S(1)} %get-tuple-element.42), channel_id=1, source_target_pairs={{0,1},{1,2},{2,3},{3,4},{4,5},{5,6},{6,7},{7,0},{8,9},{9,10},{10,1... | collective-permute-start | bytes 147464 | tf_op jit(solution)/shard_map/ppermute | solution.py:425
  49.2 1.0 %collective-permute-start.9 = (f32[24,512]{1,0:T(8,128)S(1)}, f32[24,512]{1,0:T(8,128)S(1)}, u32[]{:S(2)}, u32[]{:S(2)}) collective-permute-start(f32[24,512]{1,0:T(8,128)S(1)} %get-tuple-element.43), channel_id=1, source_target_pairs={{1,0},{2,1},{3,2},{4,3},{5,4},{6,5},{7,6},{0,7},{9,8},{10,9},{11,1... | collective-permute-start | bytes 147464 | tf_op jit(solution)/shard_map/ppermute | solution.py:425
  50.2 2.1 %collective-permute-done.8.ml_ref = f32[24,512]{1,0:T(8,128)S(1)} collective-permute-done((f32[24,512]{1,0:T(8,128)S(1)}, f32[24,512]{1,0:T(8,128)S(1)}, u32[]{:S(2)}, u32[]{:S(2)}) %collective-permute-start.8) | collective-permute-done | bytes 49184 | tf_op jit(solution)/shard_map/ppermute | solution.py:425
  52.3 1.9 %collective-permute-done.9.mr_ref = f32[24,512]{1,0:T(8,128)S(1)} collective-permute-done((f32[24,512]{1,0:T(8,128)S(1)}, f32[24,512]{1,0:T(8,128)S(1)}, u32[]{:S(2)}, u32[]{:S(2)}) %collective-permute-start.9) | collective-permute-done | bytes 49184 | tf_op jit(solution)/shard_map/ppermute | solution.py:425
  54.2 0.8 %stiff.1 = (f32[128,512]{1,0:T(8,128)S(1)}, f32[144,512]{1,0:T(8,128)S(1)}, f32[48,512]{1,0:T(8,128)S(1)}, f32[48,512]{1,0:T(8,128)S(1)}) custom-call(f32[128,512]{1,0:T(8,128)S(1)} %get-tuple-element.41.gz_ref, f32[24,512]{1,0:T(8,128)S(1)} %collective-permute-done.8.ml_ref, f32[24,512]{1,0:T(8,128)S(1)} %collective-permute-done.9.mr_ref, ...), custom_call_target="tpu_custom_call" | custom-call | tf_op jit(solution)/shard_map/stiff/pallas_call | solution.py:410
  55.0 0.1 collective-permute-start.10
  55.1 5.3 %collective-permute-start.11 = (f32[48,512]{1,0:T(8,128)S(1)}, f32[48,512]{1,0:T(8,128)S(1)}, u32[]{:S(2)}, u32[]{:S(2)}) collective-permute-start(f32[48,512]{1,0:T(8,128)S(1)} %get-tuple-element.46), channel_id=1, source_target_pairs={{8,0},{16,8},{24,16},{32,24},{40,32},{48,40},{56,48},{64,56},{72,6... | collective-permute-start | bytes 294920 | tf_op jit(solution)/shard_map/ppermute | solution.py:425
  60.4 2.3 %collective-permute-done.10.sb_ref = f32[48,512]{1,0:T(8,128)S(1)} collective-permute-done((f32[48,512]{1,0:T(8,128)S(1)}, f32[48,512]{1,0:T(8,128)S(1)}, u32[]{:S(2)}, u32[]{:S(2)}) %collective-permute-start.10) | collective-permute-done | bytes 98336 | tf_op jit(solution)/shard_map/ppermute | solution.py:425
  62.7 0.0 collective-permute-done.11.sa_ref
  62.7 1.5 %box_second.1 = (f32[128,512]{1,0:T(8,128)S(1)}, f32[16,512]{1,0:T(8,128)S(1)}, f32[16,512]{1,0:T(8,128)S(1)}) custom-call(f32[144,512]{1,0:T(8,128)S(1)} %get-tuple-element.44.s_ref, f32[48,512]{1,0:T(8,128)S(1)} %collective-permute-done.10.sb_ref, f32[48,512]{1,0:T(8,128)S(1)} %collective-permute-done.11.sa_ref, bf16[208,720]{1,0:T(8,128)(2,1)S(1)} %copy-done.5, ...), custom_call_target="tpu_custom_call" | custom-call | tf_op jit(solution)/shard_map/box_second/pallas_call | solution.py:410
  64.2 0.1 collective-permute-start.12
  64.3 5.4 %collective-permute-start.13 = (f32[16,512]{1,0:T(8,128)S(1)}, f32[16,512]{1,0:T(8,128)S(1)}, u32[]{:S(2)}, u32[]{:S(2)}) collective-permute-start(f32[16,512]{1,0:T(8,128)S(1)} %get-tuple-element.49), channel_id=1, source_target_pairs={{8,0},{16,8},{24,16},{32,24},{40,32},{48,40},{56,48},{64,56},{72,6... | collective-permute-start | bytes 98312 | tf_op jit(solution)/shard_map/ppermute | solution.py:425
  69.7 1.5 %collective-permute-done.12.gb_ref = f32[16,512]{1,0:T(8,128)S(1)} collective-permute-done((f32[16,512]{1,0:T(8,128)S(1)}, f32[16,512]{1,0:T(8,128)S(1)}, u32[]{:S(2)}, u32[]{:S(2)}) %collective-permute-start.12) | collective-permute-done | bytes 32800 | tf_op jit(solution)/shard_map/ppermute | solution.py:425
  71.3 0.1 collective-permute-done.13.ga_ref
  71.3 0.1 last_z.1
  71.4 1.2 %collective-permute-start.14 = (f32[8,512]{1,0:T(8,128)S(1)}, f32[8,512]{1,0:T(8,128)S(1)}, u32[]{:S(2)}, u32[]{:S(2)}) collective-permute-start(f32[8,512]{1,0:T(8,128)S(1)} %get-tuple-element.52), channel_id=1, source_target_pairs={{0,1},{1,2},{2,3},{3,4},{4,5},{5,6},{6,7},{7,0},{8,9},{9,10},{10,1... | collective-permute-start | bytes 49160 | tf_op jit(solution)/shard_map/ppermute | solution.py:425
  72.6 0.9 %collective-permute-start.15 = (f32[8,512]{1,0:T(8,128)S(1)}, f32[8,512]{1,0:T(8,128)S(1)}, u32[]{:S(2)}, u32[]{:S(2)}) collective-permute-start(f32[8,512]{1,0:T(8,128)S(1)} %get-tuple-element.53), channel_id=1, source_target_pairs={{1,0},{2,1},{3,2},{4,3},{5,4},{6,5},{7,6},{0,7},{9,8},{10,9},{11,1... | collective-permute-start | bytes 49160 | tf_op jit(solution)/shard_map/ppermute | solution.py:425
  73.5 1.7 %collective-permute-done.14.ml_ref = f32[8,512]{1,0:T(8,128)S(1)} collective-permute-done((f32[8,512]{1,0:T(8,128)S(1)}, f32[8,512]{1,0:T(8,128)S(1)}, u32[]{:S(2)}, u32[]{:S(2)}) %collective-permute-start.14) | collective-permute-done | bytes 16416 | tf_op jit(solution)/shard_map/ppermute | solution.py:425
  75.2 2.0 %collective-permute-done.15.mr_ref = f32[8,512]{1,0:T(8,128)S(1)} collective-permute-done((f32[8,512]{1,0:T(8,128)S(1)}, f32[8,512]{1,0:T(8,128)S(1)}, u32[]{:S(2)}, u32[]{:S(2)}) %collective-permute-start.15) | collective-permute-done | bytes 16416 | tf_op jit(solution)/shard_map/ppermute | solution.py:425
  77.3 0.7 last_x.1
  (17 shorter events, 0.0 us)
Async XLA Ops:
  0.6 21.6 %copy-start.4 = (bf16[768,256]{1,0:T(8,128)(2,1)S(1)}, bf16[768,256]{1,0:T(8,128)(2,1)}, u32[]{:S(2)}) copy-start(bf16[768,256]{1,0:T(8,128)(2,1)} %constant.46.clone.wd_y) | copy-start | bytes 1179652
  0.6 1.3 %copy-start.6 = (bf16[768,768]{1,0:T(8,128)(2,1)S(1)}, bf16[768,768]{1,0:T(8,128)(2,1)}, u32[]{:S(2)}) copy-start(bf16[768,768]{1,0:T(8,128)(2,1)} %constant.36.clone.y_in) | copy-start | bytes 3538948
  2.0 1.1 %copy-start.7 = (f32[3,8,16,512]{3,2,1,0:T(8,128)S(1)}, f32[3,8,16,512]{3,2,1,0:T(8,128)}, u32[]{:S(2)}) copy-start(f32[3,8,16,512]{3,2,1,0:T(8,128)} %v_ref.1) | copy-start | bytes 2359300
  3.1 1.1 %copy-start.8 = (bf16[864,384]{1,0:T(8,128)(2,1)S(1)}, bf16[864,384]{1,0:T(8,128)(2,1)}, u32[]{:S(2)}) copy-start(bf16[864,384]{1,0:T(8,128)(2,1)} %constant.37.clone.zx_in) | copy-start | bytes 1990660
  4.2 1.1 %copy-start.10 = (bf16[1152,256]{1,0:T(8,128)(2,1)S(1)}, bf16[1152,256]{1,0:T(8,128)(2,1)}, u32[]{:S(2)}) copy-start(bf16[1152,256]{1,0:T(8,128)(2,1)} %constant.39.clone.y_out) | copy-start | bytes 1769476
  5.3 0.9 %copy-start.12 = (f32[8,16,512]{2,1,0:T(8,128)S(1)}, f32[8,16,512]{2,1,0:T(8,128)}, u32[]{:S(2)}) copy-start(f32[8,16,512]{2,1,0:T(8,128)} %b_ref.1) | copy-start | bytes 786436
  6.2 0.9 %copy-start.14 = (bf16[128,864]{1,0:T(8,128)(2,1)S(1)}, bf16[128,864]{1,0:T(8,128)(2,1)}, u32[]{:S(2)}) copy-start(bf16[128,864]{1,0:T(8,128)(2,1)} %constant.38.clone.zx_out) | copy-start | bytes 663556
  7.1 15.1 %copy-start.16 = (bf16[32,768]{1,0:T(8,128)(2,1)S(1)}, bf16[32,768]{1,0:T(8,128)(2,1)}, u32[]{:S(2)}) copy-start(bf16[32,768]{1,0:T(8,128)(2,1)} %constant.40.clone.m01) | copy-start | bytes 147460
  7.1 15.1 %copy-start.18 = (f32[1,512]{1,0:T(1,128)S(1)}, f32[1,512]{1,0:T(1,128)}, u32[]{:S(2)}) copy-start(f32[1,512]{1,0:T(1,128)} %constant.48.clone.w_y) | copy-start | bytes 6148
  7.1 15.1 %copy-start.19 = (bf16[32,384]{1,0:T(8,128)(2,1)S(1)}, bf16[32,384]{1,0:T(8,128)(2,1)}, u32[]{:S(2)}) copy-start(bf16[32,384]{1,0:T(8,128)(2,1)} %constant.41.clone.m2) | copy-start | bytes 73732
  7.2 22.9 %copy-start.13 = (bf16[144,864]{1,0:T(8,128)(2,1)S(1)}, bf16[144,864]{1,0:T(8,128)(2,1)}, u32[]{:S(2)}) copy-start(bf16[144,864]{1,0:T(8,128)(2,1)} %constant.42.clone.m01) | copy-start | bytes 746500
  7.2 22.9 %copy-start.15 = (bf16[144,432]{1,0:T(8,128)(2,1)S(1)}, bf16[144,432]{1,0:T(8,128)(2,1)}, u32[]{:S(2)}) copy-start(bf16[144,432]{1,0:T(8,128)(2,1)} %constant.43.clone.m2) | copy-start | bytes 373252
  7.2 31.7 %copy-start.1 = (bf16[1536,640]{1,0:T(8,128)(2,1)S(1)}, bf16[1536,640]{1,0:T(8,128)(2,1)}, u32[]{:S(2)}) copy-start(bf16[1536,640]{1,0:T(8,128)(2,1)} %constant.51.clone.ybox_in) | copy-start | bytes 5898244
  14.4 24.5 %copy-start = (bf16[1920,512]{1,0:T(8,128)(2,1)S(1)}, bf16[1920,512]{1,0:T(8,128)(2,1)}, u32[]{:S(2)}) copy-start(bf16[1920,512]{1,0:T(8,128)(2,1)} %constant.52.clone.ybox_out) | copy-start | bytes 5898244
  14.4 24.5 %copy-start.2 = (f32[208,640]{1,0:T(8,128)S(1)}, f32[208,640]{1,0:T(8,128)}, u32[]{:S(2)}) copy-start(f32[208,640]{1,0:T(8,128)} %constant.53.clone.inv) | copy-start | bytes 1597444
  14.5 24.5 %copy-start.5 = (bf16[208,720]{1,0:T(8,128)(2,1)S(1)}, bf16[208,720]{1,0:T(8,128)(2,1)}, u32[]{:S(2)}) copy-start(bf16[208,720]{1,0:T(8,128)(2,1)} %constant.49.clone.box_in) | copy-start | bytes 898564
  14.5 24.5 %copy-start.9 = (bf16[128,624]{1,0:T(8,128)(2,1)S(1)}, bf16[128,624]{1,0:T(8,128)(2,1)}, u32[]{:S(2)}) copy-start(bf16[128,624]{1,0:T(8,128)(2,1)} %constant.50.clone.box_out) | copy-start | bytes 479236
  14.5 7.7 %collective-permute-start = (f32[48,512]{1,0:T(8,128)S(1)}, f32[48,512]{1,0:T(8,128)S(1)}, u32[]{:S(2)}, u32[]{:S(2)}) collective-permute-start(f32[48,512]{1,0:T(8,128)S(1)} %get-tuple-element.29), channel_id=1, source_target_pairs={{0,8},{8,16},{16,24},{24,32},{32,40},{40,48},{48,56},{56,64},{64,7... | collective-permute-start | bytes 294920 | tf_op jit(solution)/shard_map/ppermute | solution.py:425
  14.6 7.6 %collective-permute-start.1 = (f32[48,512]{1,0:T(8,128)S(1)}, f32[48,512]{1,0:T(8,128)S(1)}, u32[]{:S(2)}, u32[]{:S(2)}) collective-permute-start(f32[48,512]{1,0:T(8,128)S(1)} %get-tuple-element.30), channel_id=1, source_target_pairs={{8,0},{16,8},{24,16},{32,24},{40,32},{48,40},{56,48},{64,56},{72,6... | collective-permute-start | bytes 294920 | tf_op jit(solution)/shard_map/ppermute | solution.py:425
  22.9 5.0 %collective-permute-start.2 = (f32[40,512]{1,0:T(8,128)S(1)}, f32[40,512]{1,0:T(8,128)S(1)}, u32[]{:S(2)}, u32[]{:S(2)}) collective-permute-start(f32[40,512]{1,0:T(8,128)S(1)} %get-tuple-element.32), channel_id=1, source_target_pairs={{0,1},{1,2},{2,3},{3,4},{4,5},{5,6},{6,7},{7,0},{8,9},{9,10},{10,1... | collective-permute-start | bytes 245768 | tf_op jit(solution)/shard_map/ppermute | solution.py:425
  24.7 5.3 %collective-permute-start.3 = (f32[40,512]{1,0:T(8,128)S(1)}, f32[40,512]{1,0:T(8,128)S(1)}, u32[]{:S(2)}, u32[]{:S(2)}) collective-permute-start(f32[40,512]{1,0:T(8,128)S(1)} %get-tuple-element.33), channel_id=1, source_target_pairs={{1,0},{2,1},{3,2},{4,3},{5,4},{6,5},{7,6},{0,7},{9,8},{10,9},{11,1... | collective-permute-start | bytes 245768 | tf_op jit(solution)/shard_map/ppermute | solution.py:425
  31.2 7.7 %collective-permute-start.4 = (f32[48,512]{1,0:T(8,128)S(1)}, f32[48,512]{1,0:T(8,128)S(1)}, u32[]{:S(2)}, u32[]{:S(2)}) collective-permute-start(f32[48,512]{1,0:T(8,128)S(1)} %get-tuple-element.36), channel_id=1, source_target_pairs={{0,8},{8,16},{16,24},{24,32},{32,40},{40,48},{48,56},{56,64},{64,7... | collective-permute-start | bytes 294920 | tf_op jit(solution)/shard_map/ppermute | solution.py:425
  31.3 7.7 %collective-permute-start.5 = (f32[48,512]{1,0:T(8,128)S(1)}, f32[48,512]{1,0:T(8,128)S(1)}, u32[]{:S(2)}, u32[]{:S(2)}) collective-permute-start(f32[48,512]{1,0:T(8,128)S(1)} %get-tuple-element.37), channel_id=1, source_target_pairs={{8,0},{16,8},{24,16},{32,24},{40,32},{48,40},{56,48},{64,56},{72,6... | collective-permute-start | bytes 294920 | tf_op jit(solution)/shard_map/ppermute | solution.py:425
  38.9 8.8 %copy-start.3 = (bf16[768,256]{1,0:T(8,128)(2,1)S(1)}, bf16[768,256]{1,0:T(8,128)(2,1)}, u32[]{:S(2)}) copy-start(bf16[768,256]{1,0:T(8,128)(2,1)} %constant.47.clone.k_y) | copy-start | bytes 1179652
  39.0 8.8 %copy-start.17 = (bf16[64,384]{1,0:T(8,128)(2,1)S(1)}, bf16[64,384]{1,0:T(8,128)(2,1)}, u32[]{:S(2)}) copy-start(bf16[64,384]{1,0:T(8,128)(2,1)} %constant.44.clone.st_msg) | copy-start | bytes 147460
  39.0 15.2 %copy-start.11 = (bf16[288,432]{1,0:T(8,128)(2,1)S(1)}, bf16[288,432]{1,0:T(8,128)(2,1)}, u32[]{:S(2)}) copy-start(bf16[288,432]{1,0:T(8,128)(2,1)} %constant.45.clone.st) | copy-start | bytes 746500
  40.5 7.0 %collective-permute-start.6 = (f32[16,512]{1,0:T(8,128)S(1)}, f32[16,512]{1,0:T(8,128)S(1)}, u32[]{:S(2)}, u32[]{:S(2)}) collective-permute-start(f32[16,512]{1,0:T(8,128)S(1)} %get-tuple-element.39), channel_id=1, source_target_pairs={{0,8},{8,16},{16,24},{24,32},{32,40},{40,48},{48,56},{56,64},{64,7... | collective-permute-start | bytes 98312 | tf_op jit(solution)/shard_map/ppermute | solution.py:425
  40.6 7.2 %collective-permute-start.7 = (f32[16,512]{1,0:T(8,128)S(1)}, f32[16,512]{1,0:T(8,128)S(1)}, u32[]{:S(2)}, u32[]{:S(2)}) collective-permute-start(f32[16,512]{1,0:T(8,128)S(1)} %get-tuple-element.40), channel_id=1, source_target_pairs={{8,0},{16,8},{24,16},{32,24},{40,32},{48,40},{56,48},{64,56},{72,6... | collective-permute-start | bytes 98312 | tf_op jit(solution)/shard_map/ppermute | solution.py:425
  48.2 4.1 %collective-permute-start.8 = (f32[24,512]{1,0:T(8,128)S(1)}, f32[24,512]{1,0:T(8,128)S(1)}, u32[]{:S(2)}, u32[]{:S(2)}) collective-permute-start(f32[24,512]{1,0:T(8,128)S(1)} %get-tuple-element.42), channel_id=1, source_target_pairs={{0,1},{1,2},{2,3},{3,4},{4,5},{5,6},{6,7},{7,0},{8,9},{9,10},{10,1... | collective-permute-start | bytes 147464 | tf_op jit(solution)/shard_map/ppermute | solution.py:425
  49.2 5.0 %collective-permute-start.9 = (f32[24,512]{1,0:T(8,128)S(1)}, f32[24,512]{1,0:T(8,128)S(1)}, u32[]{:S(2)}, u32[]{:S(2)}) collective-permute-start(f32[24,512]{1,0:T(8,128)S(1)} %get-tuple-element.43), channel_id=1, source_target_pairs={{1,0},{2,1},{3,2},{4,3},{5,4},{6,5},{7,6},{0,7},{9,8},{10,9},{11,1... | collective-permute-start | bytes 147464 | tf_op jit(solution)/shard_map/ppermute | solution.py:425
  55.0 7.7 %collective-permute-start.10 = (f32[48,512]{1,0:T(8,128)S(1)}, f32[48,512]{1,0:T(8,128)S(1)}, u32[]{:S(2)}, u32[]{:S(2)}) collective-permute-start(f32[48,512]{1,0:T(8,128)S(1)} %get-tuple-element.45), channel_id=1, source_target_pairs={{0,8},{8,16},{16,24},{24,32},{32,40},{40,48},{48,56},{56,64},{64,7... | collective-permute-start | bytes 294920 | tf_op jit(solution)/shard_map/ppermute | solution.py:425
  55.1 7.6 %collective-permute-start.11 = (f32[48,512]{1,0:T(8,128)S(1)}, f32[48,512]{1,0:T(8,128)S(1)}, u32[]{:S(2)}, u32[]{:S(2)}) collective-permute-start(f32[48,512]{1,0:T(8,128)S(1)} %get-tuple-element.46), channel_id=1, source_target_pairs={{8,0},{16,8},{24,16},{32,24},{40,32},{48,40},{56,48},{64,56},{72,6... | collective-permute-start | bytes 294920 | tf_op jit(solution)/shard_map/ppermute | solution.py:425
  64.2 7.0 %collective-permute-start.12 = (f32[16,512]{1,0:T(8,128)S(1)}, f32[16,512]{1,0:T(8,128)S(1)}, u32[]{:S(2)}, u32[]{:S(2)}) collective-permute-start(f32[16,512]{1,0:T(8,128)S(1)} %get-tuple-element.48), channel_id=1, source_target_pairs={{0,8},{8,16},{16,24},{24,32},{32,40},{40,48},{48,56},{56,64},{64,7... | collective-permute-start | bytes 98312 | tf_op jit(solution)/shard_map/ppermute | solution.py:425
  64.3 7.0 %collective-permute-start.13 = (f32[16,512]{1,0:T(8,128)S(1)}, f32[16,512]{1,0:T(8,128)S(1)}, u32[]{:S(2)}, u32[]{:S(2)}) collective-permute-start(f32[16,512]{1,0:T(8,128)S(1)} %get-tuple-element.49), channel_id=1, source_target_pairs={{8,0},{16,8},{24,16},{32,24},{40,32},{48,40},{56,48},{64,56},{72,6... | collective-permute-start | bytes 98312 | tf_op jit(solution)/shard_map/ppermute | solution.py:425
  71.4 3.8 %collective-permute-start.14 = (f32[8,512]{1,0:T(8,128)S(1)}, f32[8,512]{1,0:T(8,128)S(1)}, u32[]{:S(2)}, u32[]{:S(2)}) collective-permute-start(f32[8,512]{1,0:T(8,128)S(1)} %get-tuple-element.52), channel_id=1, source_target_pairs={{0,1},{1,2},{2,3},{3,4},{4,5},{5,6},{6,7},{7,0},{8,9},{9,10},{10,1... | collective-permute-start | bytes 49160 | tf_op jit(solution)/shard_map/ppermute | solution.py:425
  72.6 4.6 %collective-permute-start.15 = (f32[8,512]{1,0:T(8,128)S(1)}, f32[8,512]{1,0:T(8,128)S(1)}, u32[]{:S(2)}, u32[]{:S(2)}) collective-permute-start(f32[8,512]{1,0:T(8,128)S(1)} %get-tuple-element.53), channel_id=1, source_target_pairs={{1,0},{2,1},{3,2},{4,3},{5,4},{6,5},{7,6},{0,7},{9,8},{10,9},{11,1... | collective-permute-start | bytes 49160 | tf_op jit(solution)/shard_map/ppermute | solution.py:425
where the time goes:
time: 78.9 us; the launch traced here: 78 us
  starting transfers between devices  33.6 us (43%)
  waiting for transfers between devices  23 us (29%)
  Pallas kernels  14 us (18%)
  local copies, waits for them, and re-layouts  6.57 us (8%)
  between operations  0.86 us (1%)
    ppermute x8, starting transfers between devices, exchange(): lax.ppermute(backward, axis, behind)  29.2 us
    ppermute x8, waiting for transfers between devices, exchange(): lax.ppermute(forward, axis, ahead)  16.5 us
    pallas_call x9, Pallas kernels, call(): pl.pallas_call(kernel, out_shape=[shape(o) for o in outs], in_specs=[spec...  14 us
    unnamed x40, local copies, waits for them, and re-layouts  6.57 us
    ppermute x8, waiting for transfers between devices, exchange(): lax.ppermute(backward, axis, behind)  6.45 us
    ppermute x8, starting transfers between devices, exchange(): lax.ppermute(forward, axis, ahead)  4.41 us
  transfers between devices with their start and end apart: 16, of which 13 were waited for; matrix products, arithmetic and copies ran while one was open for 0% of the time, Pallas kernels for 0%

commit v1 on v0

v1 whole, which is shorter than its diff:
```python
import functools

import jax
import jax.numpy as jnp
import ml_dtypes
import numpy as np
from jax import lax
from jax.experimental import pallas as pl
from jax.experimental.pallas import tpu as pltpu
from jax.sharding import PartitionSpec as P

F32 = jnp.float32
BF16 = jnp.bfloat16
MIB = 2**20
FORCE_VMEM = 56


def legendre_pair(degree, points):
    below, current = np.ones(points.shape), points * 1.0
    for step in range(2, degree + 1):
        below, current = current, ((2 * step - 1) * points * current - (step - 1) * below) / step
    return current, below


def tables_1d():
    points = np.cos(np.pi * np.arange(8) / 7)
    for _ in range(60):
        top, below = legendre_pair(7, points)
        points = points - (points * top - below) / (8 * top)
    points = np.sort(points)
    top, below = legendre_pair(7, points)
    w = 2.0 / (56 * top**2)
    spacing = points[:, None] - points[None, :] + np.eye(8)
    deriv = top[:, None] / (top[None, :] * spacing) * (1.0 - np.eye(8))
    deriv[0, 0], deriv[-1, -1] = -14.0, 14.0
    gauss = np.cos(np.pi * (np.arange(12) + 0.75) / 12.5)
    for _ in range(60):
        top, below = legendre_pair(12, gauss)
        gauss = gauss - top / (12 * (gauss * top - below) / (gauss**2 - 1.0))
    top, below = legendre_pair(12, gauss)
    slope = 12 * (gauss * top - below) / (gauss**2 - 1.0)
    v = 2.0 / ((1.0 - gauss**2) * slope**2)
    interp = np.ones((12, 8))
    for col in range(8):
        for other in range(8):
            if other != col:
                interp[:, col] *= (gauss - points[other]) / (points[col] - points[other])
    stiff = deriv.T @ (w[:, None] * deriv)
    wide_stiff, wide_mass = np.zeros((22, 22)), np.zeros(22)
    for el in range(3):
        r = 7 * el
        wide_stiff[r : r + 8, r : r + 8] += stiff
        wide_mass[r : r + 8] += w
    scale = 1.0 / np.sqrt(wide_mass[6:16])
    lam, vec = np.linalg.eigh(scale[:, None] * wide_stiff[6:16, 6:16] * scale[None, :])
    return interp, interp @ deriv, deriv, stiff, w, scale[:, None] * vec, lam, v


def hi_lo(m):
    hi = m.astype(ml_dtypes.bfloat16)
    return hi, (m - hi.astype(np.float64)).astype(ml_dtypes.bfloat16)


def left_const(m):
    hi, lo = hi_lo(m)
    return np.concatenate([hi, hi, lo], axis=1)


def right_const(m):
    hi, lo = hi_lo(m)
    return np.concatenate([hi, hi, lo], axis=0)


def block_diag(m, count):
    return np.kron(np.eye(count), m)


def own(z, x):
    return 16 * z + x


def local_rows(terms, xs):
    out = np.zeros((8 * len(xs), 128))
    for k, x in enumerate(xs):
        el, j = divmod(x, 8)
        for z in range(8):
            for zm, xm in terms:
                for z2 in range(8):
                    for j2 in range(8):
                        out[8 * k + z, own(z2, 8 * el + j2)] += zm[z, z2] * xm[j, j2]
    return out


def extended_rows(terms):
    local = local_rows(terms, range(16)).reshape(16, 8, 128)
    out = np.zeros((144, 144))
    for x in range(16):
        for z in range(8):
            out[own(z, x), :128] = local[x, z]
            if x in (7, 8):
                out[own(z, x), :128] += local[15 - x, z]
    for z in range(8):
        for zm, xm in terms:
            for z2 in range(8):
                out[own(z, 0), 128 + z2] += zm[z, z2] * xm[7, 7]
                out[128 + z, 128 + z2] += zm[z, z2] * xm[6, 7]
                out[own(z, 15), 136 + z2] += zm[z, z2] * xm[0, 0]
                out[136 + z, 136 + z2] += zm[z, z2] * xm[1, 0]
    return out


def z_rows(mats):
    blocks = [np.zeros((144, 144)) for _ in mats]
    for out, m in zip(blocks, mats):
        out[:128, :128] = np.kron(m, np.eye(16))
        out[128:136, 128:136] = m
        out[136:, 136:] = m
    return np.concatenate(blocks, axis=1)


def join_rows(zm, w):
    out = np.zeros((192, 384))
    below, above, down, up, far_b, far_a = 144, 200, 256, 296, 336, 360
    for t in range(18):
        side = t - 16
        own_row = lambda z: own(z, t) if t < 16 else 128 + 8 * side + z
        layer = lambda base, k: base + 16 * k + t if t < 16 else base + 48 + 2 * side + k
        msg_face = lambda base: base + 32 + t if t < 16 else base + 52 + side
        face = lambda base, k: base + 16 * k + t if t < 16 else base + 36 + 2 * k + side
        far = lambda base: base + t if t < 16 else base + 20 + side
        b7, b6, a0, a1 = np.zeros((4, 384))
        b7[layer(below, 1)] = b6[layer(below, 0)] = 1.0
        b7[face(down, 0)], b7[face(down, 1)], b7[far(far_b)] = zm[7, 7], w[7], zm[7, 0]
        b6[face(down, 0)], b6[far(far_b)] = zm[6, 7], zm[6, 0]
        a0[layer(above, 0)] = a1[layer(above, 1)] = 1.0
        a0[face(up, 0)], a0[face(up, 1)], a0[far(far_a)] = zm[0, 0], w[0], zm[0, 7]
        a1[face(up, 0)], a1[far(far_a)] = zm[1, 0], zm[1, 7]
        for z in range(8):
            row = out[own_row(z)]
            row[own_row(z)] += 1.0
            row[msg_face(below)] += zm[z, 0]
            row[msg_face(above)] += zm[z, 7]
        out[own_row(0)] += b7
        out[own_row(7)] += a0
        out[144 + t], out[168 + t] = b6, a1
    return out


def box_rows(vec):
    nodes = np.zeros((10, 2, 10, 192))
    for zk in range(10):
        for el in range(2):
            for xk in range(10):
                x = 8 * el + (-2 if xk == 0 else 9 if xk == 9 else xk - 1)
                side = -1 if x < 0 else 1 if x > 15 else 0
                if 0 < zk < 9:
                    row = {0: own(zk - 1, x), -1: 128 + zk - 1, 1: 136 + zk - 1}[side]
                else:
                    row = (144 if zk == 0 else 168) + {0: x, -1: 16, 1: 17}[side]
                nodes[zk, el, xk, row] = 1.0
    into = np.einsum("zi,xj,zexr->iejr", vec, vec, nodes).reshape(200, 192)
    back = np.zeros((8, 16, 10, 2, 10))
    inner = vec[1:9]
    for z in range(8):
        for x in range(16):
            el, j = divmod(x, 8)
            block = inner[z][:, None] * inner[j][None, :]
            if x in (7, 8):
                back[z, x, :, el] += 0.5 * block
                back[z, x, :, 1 - el] += 0.5 * inner[z][:, None] * inner[7 - j][None, :]
            else:
                back[z, x, :, el] += block
    back = back.reshape(128, 200)
    return np.pad(into, ((0, 8), (0, 0))), np.pad(back, ((0, 0), (0, 8)))


def box_lanes(vec, count):
    into = np.zeros((8 * count, 10 * count))
    back = np.zeros((10 * count, 8 * count))
    for e in range(count):
        spots = [8 * e - 2] + list(range(8 * e, 8 * e + 8)) + [8 * e + 9]
        for k, y in enumerate(spots):
            if 0 <= y < 8 * count:
                into[y, 10 * e : 10 * e + 10] += vec[k]
        for j in range(8):
            col = vec[j + 1]
            y = 8 * e + j
            if j == 0 and e > 0:
                back[10 * e : 10 * e + 10, [y - 1, y]] += 0.5 * col[:, None]
            elif j == 7 and e < count - 1:
                back[10 * e : 10 * e + 10, [y, y + 1]] += 0.5 * col[:, None]
            else:
                back[10 * e : 10 * e + 10, y] += col
    return into, back


def face_coefs(zm):
    return np.array([[zm[0, 7], zm[1, 7]], [zm[6, 0], zm[7, 0]]])


def constants():
    interp, slopes, deriv, stiff, w, vec, lam, v = tables_1d()
    eye2 = np.eye(2)
    zx = lambda a, b: np.kron(a, np.kron(eye2, b))
    c = {}
    c["y_in"] = right_const(
        np.concatenate([block_diag(interp.T, 32), block_diag(slopes.T, 32)], axis=1)
    )
    c["zx_in"] = left_const(
        np.concatenate([zx(interp, interp), zx(slopes, interp), zx(interp, slopes)], axis=0)
    )
    test = v[:, None] * interp
    back = zx(test.T, test.T).reshape(8, 16, 288)
    pair = back[:, 7] + back[:, 8]
    back[:, 7], back[:, 8] = pair, pair
    c["zx_out"] = left_const(back.reshape(128, 288))
    c["y_out"] = right_const(block_diag(test, 32))
    one, wm, wd = np.eye(8), np.diag(w), w[:, None] * deriv
    sides = (14, 15, 1, 0)
    for name, xm in (("w", wm), ("wd", wd), ("k", stiff)):
        c["xm_" + name] = left_const(local_rows([(one, xm)], sides))
        c["xe_" + name] = left_const(extended_rows([(one, xm)]))
    c["z_div"], c["z_st"] = left_const(z_rows((wd, wm))), left_const(z_rows((stiff, wm)))
    c["join_div"], c["join_st"] = left_const(join_rows(wd, w)), left_const(join_rows(stiff, w))
    c["pick_div"], c["pick_st"] = face_coefs(wd), face_coefs(stiff)
    c["wd_y"] = right_const(block_diag(wd.T, 32))
    c["k_y"] = right_const(block_diag(stiff.T, 32))
    c["w_y"] = np.tile(w, 64)[None].astype(np.float32)
    into, back = box_rows(vec)
    c["box_in"], c["box_out"] = left_const(into), left_const(back)
    into, back = box_lanes(vec, 64)
    c["ybox_in"], c["ybox_out"] = right_const(into), right_const(back)
    inv = 1.0 / (lam[:, None, None, None] + lam[None, None, :, None] + lam)
    inv = np.broadcast_to(inv[:, :, :, None, :], (10, 1, 10, 64, 10))
    inv = np.broadcast_to(inv, (10, 2, 10, 64, 10)).reshape(200, 640)
    c["inv"] = np.pad(inv, ((0, 8), (0, 0))).astype(np.float32)
    return c


def split(x):
    hi = x.astype(BF16)
    return hi, (x - hi.astype(F32)).astype(BF16)


def rmul(x, const):
    hi, lo = split(x)
    return jnp.dot(jnp.concatenate([hi, lo, hi], axis=1), const, preferred_element_type=F32)


def lmul(const, x):
    hi, lo = split(x)
    return jnp.dot(const, jnp.concatenate([hi, lo, hi], axis=0), preferred_element_type=F32)


def rmul_halves(x, const):
    return jnp.concatenate([rmul(x[:, :256], const), rmul(x[:, 256:], const)], axis=1)


def dss_lanes(x):
    lane = lax.broadcasted_iota(jnp.int32, x.shape, 1)
    n = x.shape[1]
    up = jnp.where((lane % 8 == 7) & (lane < n - 1), pltpu.roll(x, n - 1, 1), 0.0)
    down = jnp.where((lane % 8 == 0) & (lane > 0), pltpu.roll(x, 1, 1), 0.0)
    return x + up + down


def flags():
    z, x = lax.axis_index("wide"), lax.axis_index("narrow")
    nz, nx = lax.axis_size("wide"), lax.axis_size("narrow")
    as_flag = lambda t: t.astype(F32)
    return as_flag(z > 0), as_flag(z < nz - 1), as_flag(x > 0), as_flag(x < nx - 1)


def force_kernel(*refs):
    sources, (f_ref, r_ref, l_ref), held, sem = refs[:10], refs[10:13], refs[13:23], refs[23]
    copies = [pltpu.make_async_copy(a, b, sem.at[k]) for k, (a, b) in enumerate(zip(sources, held))]
    for k in (0, 2, 1, 3, 4, 5, 6, 7, 8, 9):
        copies[k].start()
    v_ref, b_ref, y_in, zx_in, zx_out, y_out, xm_w, xm_wd, wd_y, w_y = held
    copies[0].wait()
    copies[2].wait()
    copies[1].wait()
    copies[3].wait()
    v = v_ref[...].reshape(384, 512)
    b = b_ref[...].reshape(128, 512)
    halves = []
    for h in range(2):
        cut = slice(256 * h, 256 * h + 256)
        first = rmul(v[:, cut], y_in[...])
        bq = lmul(zx_in[:288, :], rmul(b[:, cut], y_in[:, :384]))
        u, gz, gx, gy = [], [], [], []
        for c in range(3):
            rows = slice(128 * c, 128 * c + 128)
            most = lmul(zx_in[...], first[rows, :384])
            u.append(most[:288])
            gz.append(most[288:576])
            gx.append(most[576:])
            gy.append(lmul(zx_in[:288, :], first[rows, 384:]))
        b2 = bq * bq
        back = []
        if h == 0:
            for copy in copies[4:]:
                copy.wait()
        for c in range(3):
            conv = u[0] * gz[c] + u[1] * gx[c] + u[2] * gy[c]
            if c != 1:
                conv = conv + b2 * u[c]
            back.append(lmul(zx_out[...], -conv))
        halves.append(rmul(jnp.concatenate(back, axis=0), y_out[...]))
    f = dss_lanes(jnp.concatenate(halves, axis=1))
    f_ref[...] = f
    s = lmul(xm_wd[...], f[128:256]) * w_y[...]
    s = s + rmul_halves(lmul(xm_w[...], f[256:]), wd_y[...])
    r_ref[:16] = s[:16]
    l_ref[:16] = s[16:]
    for k, (c, step) in enumerate(((0, 0), (1, 0), (2, 0), (0, 1))):
        r_ref[16 + 8 * k : 24 + 8 * k] = edge(f_ref, 128 * c, 15 - step)
        l_ref[16 + 8 * k : 24 + 8 * k] = edge(f_ref, 128 * c, step)


def edge(ref, base, x):
    return jnp.concatenate([ref[base + x + 16 * z : base + x + 16 * z + 1] for z in range(8)], axis=0)


def add_edge(ref, base, x, rows):
    for z in range(8):
        ref[base + x + 16 * z : base + x + 16 * z + 1] += rows[z : z + 1]


def extend(s, from_l, from_r, acc_ref):
    acc_ref[...] = s
    add_edge(acc_ref, 0, 0, from_l[8:16])
    add_edge(acc_ref, 0, 15, from_r[8:16])
    acc_ref[128:136] += from_l[:8]
    acc_ref[136:144] += from_r[:8]
    acc_ref[...] = dss_lanes(acc_ref[...])


def with_edges(full, raw_ref, base, has_l, has_r):
    edges = [edge(raw_ref, base, 0) * has_l, edge(raw_ref, base, 15) * has_r]
    return jnp.concatenate([full, *edges], axis=0)


def scaled_edges(ghost, last, w_y, ends):
    return jnp.concatenate([ghost * ends[0], last * ends[1]], axis=0) * w_y[...]


def send_faces(w_end, u, h0_ref, h12_ref, up_ref, down_ref, up_face_ref, down_face_ref, in_ref):
    for ref, own_ref, a, b, z in (
        (up_ref, up_face_ref, 6, 7, 7),
        (down_ref, down_face_ref, 0, 1, 0),
    ):
        ref[:16] = u[16 * a : 16 * a + 16]
        ref[16:32] = u[16 * b : 16 * b + 16]
        ref[32:48] = own_ref[:16] = h0_ref[16 * z : 16 * z + 16]
        own_ref[16:32] = h12_ref[16 * z : 16 * z + 16]
        half = 16 if z == 7 else 0
        ref[half : half + 16] += w_end * own_ref[16:32]
        h12 = [w_end * h12_ref[128 + 8 * s + z : 129 + 8 * s + z] for s in (0, 1)]
        rows = [u[128 + 8 * s + k : 129 + 8 * s + k] for s in (0, 1) for k in (a, b)]
        rows[z // 7] = rows[z // 7] + h12[0]
        rows[2 + z // 7] = rows[2 + z // 7] + h12[1]
        faces = [h[128 + 8 * s + z : 129 + 8 * s + z] for h in (h0_ref, h12_ref) for s in (0, 1)]
        ref[48:56] = jnp.concatenate(rows + faces, axis=0)
        own_ref[32:] = ref[48:56]
    in_ref[...] = jnp.where(is_odd(), down_ref[...], up_ref[...])


def is_odd():
    return lax.axis_index("wide") % 2 == 1


def div_kernel(ends, f_ref, ml_ref, mr_ref, xe_w, xe_wd, z_div, wd_y, w_y, *refs):
    force_ref, f_up_ref, f_down_ref, u_ref, *faces = refs[:9]
    h0_ref, h12_ref, fx_ref, sem = refs[9:]
    _, _, has_l, has_r = flags()
    ml, mr = ml_ref[...] * has_l, mr_ref[...] * has_r
    fx_ref[...] = f_ref[...]
    full = []
    for c in range(3):
        base, piece = 128 * c, slice(16 + 8 * c, 24 + 8 * c)
        add_edge(fx_ref, base, 0, ml[piece])
        add_edge(fx_ref, base, 15, mr[piece])
        full.append(with_edges(fx_ref[base : base + 128], f_ref, base, has_l, has_r))
        f_up_ref[16 * c : 16 * c + 16] = fx_ref[base + 112 : base + 128]
        f_down_ref[16 * c : 16 * c + 16] = fx_ref[base : base + 16]
    copy = pltpu.make_async_copy(fx_ref, force_ref, sem.at[0])
    copy.start()
    from_l = scaled_edges(ml[40:48], ml[16:24], w_y, ends)
    from_r = scaled_edges(mr[40:48], mr[16:24], w_y, ends)
    extend(lmul(xe_w[...], full[0]) * w_y[...], from_l, from_r, h0_ref)
    h = lmul(xe_wd[...], full[1]) * w_y[...] + rmul_halves(lmul(xe_w[...], full[2]), wd_y[...])
    extend(h, ml[:16], mr[:16], h12_ref)
    u = lmul(z_div[...], jnp.concatenate([h0_ref[...], h12_ref[...]], axis=0))
    u_ref[...] = u
    send_faces(ends[1], u, h0_ref, h12_ref, *faces)
    copy.wait()


def outer_kernel(coefs, up_ref, down_ref, in_ref, out_ref):
    odd = is_odd()
    ca = jnp.where(odd, coefs[1][0], coefs[0][0])
    cb = jnp.where(odd, coefs[1][1], coefs[0][1])
    out_ref[...] = jnp.where(odd, up_ref[...], down_ref[...])
    face, far_l, far_r = in_ref[32:48], in_ref[52:53], in_ref[53:54]
    out_ref[:16] += ca * face
    out_ref[16:32] += cb * face
    out_ref[48:52] += jnp.concatenate([ca * far_l, cb * far_l, ca * far_r, cb * far_r], axis=0)


def far_kernel(out_msg_ref, far_ref):
    has_b, has_a, _, _ = flags()
    flag = jnp.where(is_odd(), has_a, has_b)
    far_ref[:16] = out_msg_ref[32:48] * flag
    far_ref[16:] = out_msg_ref[48:56] * flag


def join(u_ref, up_ref, down_ref, in_ref, out_ref, far_ref, const):
    has_b, has_a, _, _ = flags()
    odd = is_odd()
    inner = in_ref[...]
    outer = out_ref[...] * jnp.where(odd, has_a, has_b)
    far = far_ref[...]
    rows = [
        u_ref[...],
        jnp.where(odd, inner, outer),
        jnp.where(odd, outer, inner),
        down_ref[...] * has_b,
        up_ref[...] * has_a,
        jnp.where(odd, far, 0.0),
        jnp.where(odd, 0.0, far),
    ]
    return lmul(const[...], jnp.concatenate(rows, axis=0))


def box(s, box_in, ybox_in, inv, box_out, ybox_out):
    has_b, has_a, has_l, has_r = flags()
    t = rmul(lmul(box_in[...], s), ybox_in[...]) * inv[...]
    g = rmul(lmul(box_out[...], t), ybox_out[...])
    row = lax.broadcasted_iota(jnp.int32, (128, 1), 0)
    z, x = row // 16, row % 16
    weight = 1.0 - 0.5 * jnp.where(z == 0, has_b, jnp.where(z == 7, has_a, 0.0))
    weight = weight * (1.0 - 0.5 * jnp.where(x == 0, has_l, jnp.where(x == 15, has_r, 0.0)))
    return g * weight


def first_kernel(*refs):
    join_refs, box_refs, (xm_w, xm_k, k_y, w_y) = refs[:7], refs[7:12], refs[12:16]
    s_ref, g_ref, r_ref, l_ref = refs[16:]
    s = join(*join_refs)
    s_ref[...] = s
    g = box(s, *box_refs)
    g_ref[...] = g
    q = lmul(xm_k[...], g) * w_y[...] + rmul_halves(lmul(xm_w[...], g), k_y[...])
    r_ref[:16] = q[:16]
    l_ref[:16] = q[16:]
    r_ref[16:24] = edge(g_ref, 0, 15)
    l_ref[16:24] = edge(g_ref, 0, 0)
    r_ref[24:] = edge(g_ref, 0, 14)
    l_ref[24:] = edge(g_ref, 0, 1)


def stiff_kernel(ends, g_ref, ml_ref, mr_ref, xe_w, xe_k, z_st, k_y, w_y, *refs):
    gx_ref, u_ref, *faces = refs[:7]
    p_ref, q_ref = refs[7:]
    _, _, has_l, has_r = flags()
    ml, mr = ml_ref[...] * has_l, mr_ref[...] * has_r
    gx_ref[...] = g_ref[...]
    add_edge(gx_ref, 0, 0, ml[16:24])
    add_edge(gx_ref, 0, 15, mr[16:24])
    full = with_edges(gx_ref[...], g_ref, 0, has_l, has_r)
    from_l = scaled_edges(ml[24:], ml[16:24], w_y, ends)
    from_r = scaled_edges(mr[24:], mr[16:24], w_y, ends)
    plain = lmul(xe_w[...], full)
    extend(plain * w_y[...], from_l, from_r, p_ref)
    q = lmul(xe_k[...], full) * w_y[...] + rmul_halves(plain, k_y[...])
    extend(q, ml[:16], mr[:16], q_ref)
    u = lmul(z_st[...], jnp.concatenate([p_ref[...], q_ref[...]], axis=0))
    u_ref[...] = u
    send_faces(ends[1], u, p_ref, q_ref, *faces)


def second_kernel(s_ref, *refs):
    join_refs, box_refs, (g_ref, r_ref, l_ref) = refs[:7], refs[7:12], refs[12:]
    g_ref[...] = box(s_ref[...] - join(*join_refs), *box_refs)
    r_ref[...] = edge(g_ref, 0, 15)
    l_ref[...] = edge(g_ref, 0, 0)


def last_x_kernel(g_ref, gx_ref, ml_ref, mr_ref, f_up, f_down, out_ref, in_msg_ref, out_msg_ref):
    _, _, has_l, has_r = flags()
    out_ref[...] = g_ref[...] + gx_ref[...]
    add_edge(out_ref, 0, 0, ml_ref[...] * has_l)
    add_edge(out_ref, 0, 15, mr_ref[...] * has_r)
    odd = is_odd()
    for rows, up, down in (
        (slice(0, 16), out_ref[112:], out_ref[:16]),
        (slice(16, 64), f_up[...], f_down[...]),
    ):
        in_msg_ref[rows] = jnp.where(odd, down, up)
        out_msg_ref[rows] = jnp.where(odd, up, down)


def last_z_kernel(g_ref, f_up, f_down, in_ref, out_msg_ref, _, out_ref, force_ref, face_ref, sem):
    has_b, has_a, _, _ = flags()
    odd = is_odd()
    inner, outer = in_ref[...], out_msg_ref[...] * jnp.where(odd, has_a, has_b)
    below, above = jnp.where(odd, inner, outer), jnp.where(odd, outer, inner)
    face_ref[:48] = f_down[...] + below[16:]
    face_ref[48:] = f_up[...] + above[16:]
    copies = []
    for c in range(3):
        for k, row in enumerate((128 * c, 128 * c + 112)):
            src = face_ref.at[pl.ds(48 * k + 16 * c, 16)]
            dst = force_ref.at[pl.ds(row, 16)]
            copies.append(pltpu.make_async_copy(src, dst, sem.at[2 * c + k]))
            copies[-1].start()
    out_ref[...] = g_ref[...]
    out_ref[:16] += below[:16]
    out_ref[112:] += above[:16]
    for copy in copies:
        copy.wait()


def call(kernel, name, outs, *args, scratch=(), sems=0, vmem=16, hbm_in=(), hbm_out=(), alias=None):
    shape = lambda rows: jax.ShapeDtypeStruct((rows, 512), F32)
    spec = lambda k, far: pl.BlockSpec(memory_space=pltpu.HBM if k in far else pltpu.VMEM)
    scratch = [pltpu.VMEM((k, 512), F32) if isinstance(k, int) else k for k in scratch]
    return pl.pallas_call(
        kernel,
        out_shape=[shape(o) for o in outs],
        in_specs=[spec(k, hbm_in) for k in range(len(args))],
        out_specs=[spec(k, hbm_out) for k in range(len(outs))],
        scratch_shapes=scratch + ([pltpu.SemaphoreType.DMA((sems,))] if sems else []),
        input_output_aliases=alias or {},
        compiler_params=pltpu.CompilerParams(vmem_limit_bytes=vmem * MIB),
        name=name,
    )(*args)


def exchange_x(rightward, leftward):
    n = lax.axis_size("narrow")
    right = [(i, (i + 1) % n) for i in range(n)]
    left = [(j, i) for i, j in right]
    return lax.ppermute(rightward, "narrow", right), lax.ppermute(leftward, "narrow", left)


def other_core(x):
    n = lax.axis_size("wide")
    return lax.ppermute(x, "wide", [(i, i + 1 - 2 * (i % 2)) for i in range(n)])


def next_chip(x):
    nz, nx = lax.axis_size("wide"), lax.axis_size("narrow")
    pairs = []
    for z in range(nz):
        to = z - 1 + 2 * (z % 2)
        for k in range(nx):
            other = (to, k) if 0 <= to < nz else (z, k + 1 - 2 * (k % 2))
            pairs.append((z * nx + k, other[0] * nx + other[1]))
    return lax.ppermute(x, ("wide", "narrow"), pairs)


def meet(up, down, inner_msg, coefs, name):
    inner = other_core(inner_msg)
    coefs = [[float(t) for t in row] for row in coefs]
    (msg,) = call(functools.partial(outer_kernel, coefs), name, (56,), up, down, inner)
    outer = next_chip(msg)
    (far,) = call(far_kernel, name + "_far", (24,), outer)
    return inner, outer, other_core(far)


def shards(velocity, bfield):
    tables = constants()
    picks = tables.pop("pick_div"), tables.pop("pick_st")
    c = {name: jnp.asarray(value) for name, value in tables.items()}
    consts = lambda *names: [c[name] for name in names]
    weights = tables_1d()[4]
    ends = float(weights[1]), float(weights[0])
    force_args = (
        velocity,
        bfield,
        *consts("y_in", "zx_in", "zx_out", "y_out", "xm_w", "xm_wd", "wd_y", "w_y"),
    )
    f, right, left = call(
        force_kernel,
        "force",
        (384, 48, 48),
        *force_args,
        scratch=[pltpu.VMEM(a.shape, a.dtype) for a in force_args],
        sems=10,
        vmem=FORCE_VMEM,
        hbm_in=range(10),
    )
    from_l, from_r = exchange_x(right, left)
    force, f_up, f_down, u, up, down, up_face, down_face, inner = call(
        functools.partial(div_kernel, ends),
        "div",
        (384, 48, 48, 144, 56, 56, 40, 40, 56),
        f,
        from_l,
        from_r,
        *consts("xe_w", "xe_wd", "z_div", "wd_y", "w_y"),
        scratch=(144, 144, 384),
        sems=1,
        hbm_out=(0,),
    )
    inner, outer, far = meet(up, down, inner, picks[0], "div_out")
    box_consts = consts("box_in", "ybox_in", "inv", "box_out", "ybox_out")
    s, g, right, left = call(
        first_kernel,
        "first_pass",
        (192, 128, 32, 32),
        u,
        up_face,
        down_face,
        inner,
        outer,
        far,
        c["join_div"],
        *box_consts,
        *consts("xm_w", "xm_k", "k_y", "w_y"),
    )
    from_l, from_r = exchange_x(right, left)
    gx, u, up, down, up_face, down_face, inner = call(
        functools.partial(stiff_kernel, ends),
        "stiff",
        (128, 144, 56, 56, 40, 40, 56),
        g,
        from_l,
        from_r,
        *consts("xe_w", "xe_k", "z_st", "k_y", "w_y"),
        scratch=(144, 144),
    )
    inner, outer, far = meet(up, down, inner, picks[1], "stiff_out")
    g, right, left = call(
        second_kernel,
        "second_pass",
        (128, 8, 8),
        s,
        u,
        up_face,
        down_face,
        inner,
        outer,
        far,
        c["join_st"],
        *box_consts,
    )
    from_l, from_r = exchange_x(right, left)
    total, inner, outer = call(
        last_x_kernel, "last_x", (128, 64, 64), g, gx, from_l, from_r, f_up, f_down
    )
    outer, inner = next_chip(outer), other_core(inner)
    pressure, force = call(
        last_z_kernel,
        "last_z",
        (128, 384),
        total,
        f_up,
        f_down,
        inner,
        outer,
        force,
        scratch=(96,),
        sems=6,
        hbm_in=(5,),
        hbm_out=(1,),
        alias={5: 1},
    )
    return force.reshape(3, 8, 16, 512), pressure.reshape(8, 16, 512)


def solution(mesh):
    placed = (P(None, "wide", "narrow", None), P("wide", "narrow", None))
    return jax.shard_map(
        shards, mesh=mesh, in_specs=placed, out_specs=placed, check_vma=False
    )
```

time: 78.9 us -> 73.6 us (0.933)
  starting transfers between devices: 33.6 us -> 20.4 us
  waiting for transfers between devices: 23 us -> 29.9 us
  Pallas kernels: 14 us -> 19.1 us
  local copies, waits for them, and re-layouts: 6.57 us -> 2.15 us
    ppermute x16 -> x14, starting transfers between devices: 33.6 us -> 20.4 us  [the longest x3 13.6 us: next_chip(): return lax.ppermute(x, ('wide', 'narrow'), pairs)]
    ppermute x16 -> x14, waiting for transfers between devices: 23 us -> 29.9 us  [the longest x3 10.3 us: next_chip(): return lax.ppermute(x, ('wide', 'narrow'), pairs)]
    pallas_call x9 -> x11, Pallas kernels: 14 us -> 19.1 us  [call(): pl.pallas_call(kernel, out_shape=[shape(o) for o in outs], in_specs=[spec...]
    unnamed x40 -> x36, local copies, waits for them, and re-layouts: 6.57 us -> 2.15 us
  transfers between devices with their start and end apart: 16 -> 14, of which waited for: 13 -> 13; matrix products, arithmetic and copies ran while one was open for 0% -> 0% of each run, Pallas kernels for 0% -> 0%
where the time goes in v1:
time: 73.6 us; the launch traced here: 72.7 us
  waiting for transfers between devices  29.9 us (41%)
  starting transfers between devices  20.4 us (28%)
  Pallas kernels  19.1 us (26%)
  local copies, waits for them, and re-layouts  2.15 us (3%)
  between operations  1.1 us (1%)
    pallas_call x11, Pallas kernels, call(): pl.pallas_call(kernel, out_shape=[shape(o) for o in outs], in_specs=[spec...  19.1 us
    ppermute x3, starting transfers between devices, next_chip(): return lax.ppermute(x, ('wide', 'narrow'), pairs)  13.6 us
    ppermute x3, waiting for transfers between devices, next_chip(): return lax.ppermute(x, ('wide', 'narrow'), pairs)  10.3 us
    ppermute x3, waiting for transfers between devices, exchange_x(): lax.ppermute(leftward, 'narrow', left)  7.34 us
    ppermute x3, waiting for transfers between devices, exchange_x(): lax.ppermute(rightward, 'narrow', right)  7.19 us
    ppermute x3, starting transfers between devices, exchange_x(): lax.ppermute(rightward, 'narrow', right)  5.1 us
    ppermute x5, waiting for transfers between devices, other_core(): return lax.ppermute(x, 'wide', [(i, i + 1 - 2 * (i % 2)) for i in range(n)])  5.06 us
    unnamed x36, local copies, waits for them, and re-layouts  2.15 us
  transfers between devices with their start and end apart: 14, of which 13 were waited for; matrix products, arithmetic and copies ran while one was open for 0% of the time, Pallas kernels for 0%

profile of v1, /device:TPU:6, one launch (start us, length us, event | category | flops | bytes accessed | tf_op | source)
XLA Modules:
  0.0 72.7 jit_solution(17898710954637365683)
XLA Ops:
  0.6 0.0 copy-start.3
  0.6 0.0 copy-start.8
  0.7 0.0 copy-start.12
  0.7 0.0 copy-start.16
  0.7 0.0 copy-start.1
  0.7 0.0 copy-start.4
  0.7 0.0 copy-start.5
  0.7 0.0 copy-start.7
  0.7 0.0 copy-start.10
  0.7 0.0 copy-start.15
  0.8 0.0 copy-start.17
  0.8 10.6 %force.1 = (f32[384,512]{1,0:T(8,128)}, f32[48,512]{1,0:T(8,128)}, f32[48,512]{1,0:T(8,128)}) custom-call(f32[3,8,16,512]{3,2,1,0:T(8,128)} %refs_0_.1, f32[8,16,512]{2,1,0:T(8,128)} %refs_1_.1, bf16[768,768]{1,0:T(8,128)(2,1)} %constant.44.clone.refs_2_, bf16[864,384]{1,0:T(8,128)(2,1)} %constant.45.clone.refs_3_, bf16[128,864]{1,0:T(8,128)(2,1)} %constant.46.clone.refs_4_, ...), custom_call_target="tpu_custom_call" | custom-call | tf_op jit(solution)/shard_map/force/pallas_call | solution.py:529
  11.4 0.0 copy-start
  11.4 0.0 copy-start.2
  11.4 1.9 %collective-permute-start = (f32[48,512]{1,0:T(8,128)}, f32[48,512]{1,0:T(8,128)S(1)}, u32[]{:S(2)}, u32[]{:S(2)}) collective-permute-start(f32[48,512]{1,0:T(8,128)} %get-tuple-element.34), channel_id=1, source_target_pairs={{0,1},{1,2},{2,3},{3,4},{4,5},{5,6},{6,7},{7,0},{8,9},{9,10},{10,1... | collective-permute-start | bytes 294920 | tf_op jit(solution)/shard_map/ppermute | solution.py:545
  13.4 0.2 collective-permute-start.1
  13.5 3.2 %collective-permute-done.ml_ref = f32[48,512]{1,0:T(8,128)S(1)} collective-permute-done((f32[48,512]{1,0:T(8,128)}, f32[48,512]{1,0:T(8,128)S(1)}, u32[]{:S(2)}, u32[]{:S(2)}) %collective-permute-start) | collective-permute-done | bytes 98336 | tf_op jit(solution)/shard_map/ppermute | solution.py:545
  16.8 2.7 %collective-permute-done.1.mr_ref = f32[48,512]{1,0:T(8,128)S(1)} collective-permute-done((f32[48,512]{1,0:T(8,128)}, f32[48,512]{1,0:T(8,128)S(1)}, u32[]{:S(2)}, u32[]{:S(2)}) %collective-permute-start.1) | collective-permute-done | bytes 98336 | tf_op jit(solution)/shard_map/ppermute | solution.py:545
  19.5 0.0 copy-done.3
  19.5 0.0 copy-done.8
  19.5 0.0 copy-done.12
  19.5 0.0 copy-done.16
  19.5 0.0 copy-start.6
  19.5 1.1 %copy-done.6 = f32[384,512]{1,0:T(8,128)S(1)} copy-done((f32[384,512]{1,0:T(8,128)S(1)}, f32[384,512]{1,0:T(8,128)}, u32[]{:S(2)}) %copy-start.6) | copy-done | bytes 786456
  20.6 0.9 %copy-done.13 = bf16[144,432]{1,0:T(8,128)(2,1)S(1)} copy-done((bf16[144,432]{1,0:T(8,128)(2,1)S(1)}, bf16[144,432]{1,0:T(8,128)(2,1)}, u32[]{:S(2)}) %copy-start.13) | copy-done | bytes 124440
  21.5 1.5 %div.1 = (f32[384,512]{1,0:T(8,128)}, f32[48,512]{1,0:T(8,128)S(1)}, f32[48,512]{1,0:T(8,128)S(1)}, f32[144,512]{1,0:T(8,128)S(1)}, f32[56,512]{1,0:T(8,128)S(1)...) custom-call(f32[384,512]{1,0:T(8,128)S(1)} %copy-done.6, ...), custom_call_target="tpu_custom_call" | custom-call | tf_op jit(solution)/shard_map/div/pallas_call | solution.py:529
  23.0 0.1 collective-permute-start.2
  23.1 1.3 %collective-permute-done.2.in_ref.refs_3_ = f32[56,512]{1,0:T(8,128)S(1)} collective-permute-done((f32[56,512]{1,0:T(8,128)S(1)}, f32[56,512]{1,0:T(8,128)S(1)}, u32[]{:S(2)}, u32[]{:S(2)}) %collective-permute-start.2) | collective-permute-done | bytes 114720 | tf_op jit(solution)/shard_map/ppermute | solution.py:550
  24.5 4.7 %collective-permute-start.3 = (f32[56,512]{1,0:T(8,128)S(1)}, f32[56,512]{1,0:T(8,128)S(1)}, u32[]{:S(2)}, u32[]{:S(2)}) collective-permute-start(f32[56,512]{1,0:T(8,128)S(1)} %div_out.1), channel_id=1, source_target_pairs={{0,1},{1,0},{2,3},{3,2},{4,5},{5,4},{6,7},{7,6},{8,16},{9,17},{10,... | collective-permute-start | bytes 344072 | tf_op jit(solution)/shard_map/ppermute | solution.py:561
  29.2 3.2 %collective-permute-done.3.out_msg_ref.refs_4_ = f32[56,512]{1,0:T(8,128)S(1)} collective-permute-done((f32[56,512]{1,0:T(8,128)S(1)}, f32[56,512]{1,0:T(8,128)S(1)}, u32[]{:S(2)}, u32[]{:S(2)}) %collective-permute-start.3) | collective-permute-done | bytes 114720 | tf_op jit(solution)/shard_map/ppermute | solution.py:561
  32.4 0.1 collective-permute-start.4
  32.5 1.2 %collective-permute-done.4.refs_5_ = f32[24,512]{1,0:T(8,128)S(1)} collective-permute-done((f32[24,512]{1,0:T(8,128)S(1)}, f32[24,512]{1,0:T(8,128)S(1)}, u32[]{:S(2)}, u32[]{:S(2)}) %collective-permute-start.4) | collective-permute-done | bytes 49184 | tf_op jit(solution)/shard_map/ppermute | solution.py:550
  33.7 0.0 copy-done.7
  33.7 0.0 copy-done.10
  33.7 0.0 copy-done.15
  33.7 0.0 copy-done.17
  33.7 0.0 copy-done
  33.8 0.0 copy-done.2
  33.8 0.0 copy-start.11
  33.8 0.0 copy-start.14
  33.8 2.4 %first_pass.1 = (f32[192,512]{1,0:T(8,128)S(1)}, f32[128,512]{1,0:T(8,128)S(1)}, f32[32,512]{1,0:T(8,128)S(1)}, f32[32,512]{1,0:T(8,128)S(1)}) custom-call(f32[144,512]{1,0:T(8,128)S(1)} %get-tuple-element.36.refs_0_, f32[40,512]{1,0:T(8,128)S(1)} %get-tuple-element.37.refs_1_, f32[40,512]{1,0:T(8,128)S(1)} %get-tuple-element.38.refs_2_, ...), custom_call_target="tpu_custom_call" | custom-call | tf_op jit(solution)/shard_map/first_pass/pallas_call | solution.py:529
  36.2 0.0 copy-start.9
  36.2 2.0 %collective-permute-start.5 = (f32[32,512]{1,0:T(8,128)S(1)}, f32[32,512]{1,0:T(8,128)S(1)}, u32[]{:S(2)}, u32[]{:S(2)}) collective-permute-start(f32[32,512]{1,0:T(8,128)S(1)} %get-tuple-element.44), channel_id=1, source_target_pairs={{0,1},{1,2},{2,3},{3,4},{4,5},{5,6},{6,7},{7,0},{8,9},{9,10},{10,1... | collective-permute-start | bytes 196616 | tf_op jit(solution)/shard_map/ppermute | solution.py:545
  38.2 0.3 collective-permute-start.6
  38.5 2.2 %collective-permute-done.5.ml_ref = f32[32,512]{1,0:T(8,128)S(1)} collective-permute-done((f32[32,512]{1,0:T(8,128)S(1)}, f32[32,512]{1,0:T(8,128)S(1)}, u32[]{:S(2)}, u32[]{:S(2)}) %collective-permute-start.5) | collective-permute-done | bytes 65568 | tf_op jit(solution)/shard_map/ppermute | solution.py:545
  40.7 2.7 %collective-permute-done.6.mr_ref = f32[32,512]{1,0:T(8,128)S(1)} collective-permute-done((f32[32,512]{1,0:T(8,128)S(1)}, f32[32,512]{1,0:T(8,128)S(1)}, u32[]{:S(2)}, u32[]{:S(2)}) %collective-permute-start.6) | collective-permute-done | bytes 65568 | tf_op jit(solution)/shard_map/ppermute | solution.py:545
  43.4 1.1 %stiff.1 = (f32[128,512]{1,0:T(8,128)S(1)}, f32[144,512]{1,0:T(8,128)S(1)}, f32[56,512]{1,0:T(8,128)S(1)}, f32[56,512]{1,0:T(8,128)S(1)}, f32[40,512]{1,0:T(8,12...) custom-call(f32[128,512]{1,0:T(8,128)S(1)} %get-tuple-element.43.g_ref, ...), custom_call_target="tpu_custom_call" | custom-call | tf_op jit(solution)/shard_map/stiff/pallas_call | solution.py:529
  44.4 0.1 collective-permute-start.7
  44.5 1.3 %collective-permute-done.7.in_ref.refs_3_ = f32[56,512]{1,0:T(8,128)S(1)} collective-permute-done((f32[56,512]{1,0:T(8,128)S(1)}, f32[56,512]{1,0:T(8,128)S(1)}, u32[]{:S(2)}, u32[]{:S(2)}) %collective-permute-start.7) | collective-permute-done | bytes 114720 | tf_op jit(solution)/shard_map/ppermute | solution.py:550
  45.9 4.4 %collective-permute-start.8 = (f32[56,512]{1,0:T(8,128)S(1)}, f32[56,512]{1,0:T(8,128)S(1)}, u32[]{:S(2)}, u32[]{:S(2)}) collective-permute-start(f32[56,512]{1,0:T(8,128)S(1)} %stiff_out.1), channel_id=1, source_target_pairs={{0,1},{1,0},{2,3},{3,2},{4,5},{5,4},{6,7},{7,6},{8,16},{9,17},{10,... | collective-permute-start | bytes 344072 | tf_op jit(solution)/shard_map/ppermute | solution.py:561
  50.2 3.6 %collective-permute-done.8.out_msg_ref.refs_4_ = f32[56,512]{1,0:T(8,128)S(1)} collective-permute-done((f32[56,512]{1,0:T(8,128)S(1)}, f32[56,512]{1,0:T(8,128)S(1)}, u32[]{:S(2)}, u32[]{:S(2)}) %collective-permute-start.8) | collective-permute-done | bytes 114720 | tf_op jit(solution)/shard_map/ppermute | solution.py:561
  53.8 0.1 collective-permute-start.9
  53.9 1.2 %collective-permute-done.9.refs_5_ = f32[24,512]{1,0:T(8,128)S(1)} collective-permute-done((f32[24,512]{1,0:T(8,128)S(1)}, f32[24,512]{1,0:T(8,128)S(1)}, u32[]{:S(2)}, u32[]{:S(2)}) %collective-permute-start.9) | collective-permute-done | bytes 49184 | tf_op jit(solution)/shard_map/ppermute | solution.py:550
  55.1 1.9 %second_pass.1 = (f32[128,512]{1,0:T(8,128)S(1)}, f32[8,512]{1,0:T(8,128)S(1)}, f32[8,512]{1,0:T(8,128)S(1)}) custom-call(f32[192,512]{1,0:T(8,128)S(1)} %get-tuple-element.42.s_ref, f32[144,512]{1,0:T(8,128)S(1)} %get-tuple-element.46.refs_0_, f32[40,512]{1,0:T(8,128)S(1)} %get-tuple-element.47.refs_1_, f32[40,512]{1,0:T(8,128)S(1)} %get-tuple-element.48.refs_2_, ...), custom_call_target="tpu_custom_call" | custom-call | tf_op jit(solution)/shard_map/second_pass/pallas_call | solution.py:529
  57.0 1.2 %collective-permute-start.10 = (f32[8,512]{1,0:T(8,128)S(1)}, f32[8,512]{1,0:T(8,128)S(1)}, u32[]{:S(2)}, u32[]{:S(2)}) collective-permute-start(f32[8,512]{1,0:T(8,128)S(1)} %get-tuple-element.54), channel_id=1, source_target_pairs={{0,1},{1,2},{2,3},{3,4},{4,5},{5,6},{6,7},{7,0},{8,9},{9,10},{10,1... | collective-permute-start | bytes 49160 | tf_op jit(solution)/shard_map/ppermute | solution.py:545
  58.2 0.9 %collective-permute-start.11 = (f32[8,512]{1,0:T(8,128)S(1)}, f32[8,512]{1,0:T(8,128)S(1)}, u32[]{:S(2)}, u32[]{:S(2)}) collective-permute-start(f32[8,512]{1,0:T(8,128)S(1)} %get-tuple-element.55), channel_id=1, source_target_pairs={{1,0},{2,1},{3,2},{4,3},{5,4},{6,5},{7,6},{0,7},{9,8},{10,9},{11,1... | collective-permute-start | bytes 49160 | tf_op jit(solution)/shard_map/ppermute | solution.py:545
  59.1 1.7 %collective-permute-done.10.ml_ref = f32[8,512]{1,0:T(8,128)S(1)} collective-permute-done((f32[8,512]{1,0:T(8,128)S(1)}, f32[8,512]{1,0:T(8,128)S(1)}, u32[]{:S(2)}, u32[]{:S(2)}) %collective-permute-start.10) | collective-permute-done | bytes 16416 | tf_op jit(solution)/shard_map/ppermute | solution.py:545
  60.8 2.0 %collective-permute-done.11.mr_ref = f32[8,512]{1,0:T(8,128)S(1)} collective-permute-done((f32[8,512]{1,0:T(8,128)S(1)}, f32[8,512]{1,0:T(8,128)S(1)}, u32[]{:S(2)}, u32[]{:S(2)}) %collective-permute-start.11) | collective-permute-done | bytes 16416 | tf_op jit(solution)/shard_map/ppermute | solution.py:545
  62.8 0.1 last_x.1
  62.9 0.1 collective-permute-start.12
  63.0 4.5 %collective-permute-start.13 = (f32[64,512]{1,0:T(8,128)S(1)}, f32[64,512]{1,0:T(8,128)S(1)}, u32[]{:S(2)}, u32[]{:S(2)}) collective-permute-start(f32[64,512]{1,0:T(8,128)S(1)} %get-tuple-element.60), channel_id=1, source_target_pairs={{0,1},{1,0},{2,3},{3,2},{4,5},{5,4},{6,7},{7,6},{8,16},{9,17},{10,... | collective-permute-start | bytes 393224 | tf_op jit(solution)/shard_map/ppermute | solution.py:561
  67.5 0.0 collective-permute-done.12.in_ref
  67.5 3.6 %collective-permute-done.13.out_msg_ref = f32[64,512]{1,0:T(8,128)S(1)} collective-permute-done((f32[64,512]{1,0:T(8,128)S(1)}, f32[64,512]{1,0:T(8,128)S(1)}, u32[]{:S(2)}, u32[]{:S(2)}) %collective-permute-start.13) | collective-permute-done | bytes 131104 | tf_op jit(solution)/shard_map/ppermute | solution.py:561
  71.1 1.5 %last_z.1 = (f32[128,512]{1,0:T(8,128)}, f32[384,512]{1,0:T(8,128)}) custom-call(f32[128,512]{1,0:T(8,128)S(1)} %get-tuple-element.58.g_ref, f32[48,512]{1,0:T(8,128)S(1)} %get-tuple-element.56.f_up, f32[48,512]{1,0:T(8,128)S(1)} %get-tuple-element.57.f_down, f32[64,512]{1,0:T(8,128)S(1)} %collective-permute-done.12.in_ref, ...), custom_call_target="tpu_custom_call", output_to_operand_aliasing={{1}: (5, {})} | custom-call | tf_op jit(solution)/shard_map/last_z/pallas_call | solution.py:529
  (11 shorter events, 0.1 us)
Async XLA Ops:
  0.6 18.8 %copy-start.3 = (bf16[768,256]{1,0:T(8,128)(2,1)S(1)}, bf16[768,256]{1,0:T(8,128)(2,1)}, u32[]{:S(2)}) copy-start(bf16[768,256]{1,0:T(8,128)(2,1)} %constant.58.clone.refs_8_.wd_y) | copy-start | bytes 1179652
  0.6 18.8 %copy-start.8 = (bf16[144,432]{1,0:T(8,128)(2,1)S(1)}, bf16[144,432]{1,0:T(8,128)(2,1)}, u32[]{:S(2)}) copy-start(bf16[144,432]{1,0:T(8,128)(2,1)} %constant.49.clone.xe_w) | copy-start | bytes 373252
  0.7 18.8 %copy-start.12 = (bf16[144,864]{1,0:T(8,128)(2,1)S(1)}, bf16[144,864]{1,0:T(8,128)(2,1)}, u32[]{:S(2)}) copy-start(bf16[144,864]{1,0:T(8,128)(2,1)} %constant.54.clone.z_div) | copy-start | bytes 746500
  0.7 18.8 %copy-start.16 = (f32[1,512]{1,0:T(1,128)S(1)}, f32[1,512]{1,0:T(1,128)}, u32[]{:S(2)}) copy-start(f32[1,512]{1,0:T(1,128)} %constant.60.clone.refs_9_.w_y.refs_15_) | copy-start | bytes 6148
  0.7 33.0 %copy-start.1 = (bf16[1536,640]{1,0:T(8,128)(2,1)S(1)}, bf16[1536,640]{1,0:T(8,128)(2,1)}, u32[]{:S(2)}) copy-start(bf16[1536,640]{1,0:T(8,128)(2,1)} %constant.63.clone.refs_8_) | copy-start | bytes 5898244
  0.7 33.0 %copy-start.4 = (bf16[768,256]{1,0:T(8,128)(2,1)S(1)}, bf16[768,256]{1,0:T(8,128)(2,1)}, u32[]{:S(2)}) copy-start(bf16[768,256]{1,0:T(8,128)(2,1)} %constant.59.clone.refs_14_.k_y) | copy-start | bytes 1179652
  0.7 33.0 %copy-start.5 = (bf16[208,576]{1,0:T(8,128)(2,1)S(1)}, bf16[208,576]{1,0:T(8,128)(2,1)}, u32[]{:S(2)}) copy-start(bf16[208,576]{1,0:T(8,128)(2,1)} %constant.61.clone.refs_7_) | copy-start | bytes 718852
  0.7 33.0 %copy-start.7 = (bf16[128,624]{1,0:T(8,128)(2,1)S(1)}, bf16[128,624]{1,0:T(8,128)(2,1)}, u32[]{:S(2)}) copy-start(bf16[128,624]{1,0:T(8,128)(2,1)} %constant.62.clone.refs_10_) | copy-start | bytes 479236
  0.7 33.0 %copy-start.10 = (bf16[192,1152]{1,0:T(8,128)(2,1)S(1)}, bf16[192,1152]{1,0:T(8,128)(2,1)}, u32[]{:S(2)}) copy-start(bf16[192,1152]{1,0:T(8,128)(2,1)} %constant.56.clone.refs_6_) | copy-start | bytes 1327108
  0.7 33.0 %copy-start.15 = (bf16[32,384]{1,0:T(8,128)(2,1)S(1)}, bf16[32,384]{1,0:T(8,128)(2,1)}, u32[]{:S(2)}) copy-start(bf16[32,384]{1,0:T(8,128)(2,1)} %constant.48.clone.refs_6_.refs_12_) | copy-start | bytes 73732
  0.8 33.0 %copy-start.17 = (bf16[32,384]{1,0:T(8,128)(2,1)S(1)}, bf16[32,384]{1,0:T(8,128)(2,1)}, u32[]{:S(2)}) copy-start(bf16[32,384]{1,0:T(8,128)(2,1)} %constant.52.clone.refs_13_) | copy-start | bytes 73732
  11.4 22.3 %copy-start = (bf16[1920,512]{1,0:T(8,128)(2,1)S(1)}, bf16[1920,512]{1,0:T(8,128)(2,1)}, u32[]{:S(2)}) copy-start(bf16[1920,512]{1,0:T(8,128)(2,1)} %constant.64.clone.refs_11_) | copy-start | bytes 5898244
  11.4 22.3 %copy-start.2 = (f32[208,640]{1,0:T(8,128)S(1)}, f32[208,640]{1,0:T(8,128)}, u32[]{:S(2)}) copy-start(f32[208,640]{1,0:T(8,128)} %constant.65.clone.refs_9_) | copy-start | bytes 1597444
  11.4 5.3 %collective-permute-start = (f32[48,512]{1,0:T(8,128)}, f32[48,512]{1,0:T(8,128)S(1)}, u32[]{:S(2)}, u32[]{:S(2)}) collective-permute-start(f32[48,512]{1,0:T(8,128)} %get-tuple-element.34), channel_id=1, source_target_pairs={{0,1},{1,2},{2,3},{3,4},{4,5},{5,6},{6,7},{7,0},{8,9},{9,10},{10,1... | collective-permute-start | bytes 294920 | tf_op jit(solution)/shard_map/ppermute | solution.py:545
  13.4 6.1 %collective-permute-start.1 = (f32[48,512]{1,0:T(8,128)}, f32[48,512]{1,0:T(8,128)S(1)}, u32[]{:S(2)}, u32[]{:S(2)}) collective-permute-start(f32[48,512]{1,0:T(8,128)} %get-tuple-element.35), channel_id=1, source_target_pairs={{1,0},{2,1},{3,2},{4,3},{5,4},{6,5},{7,6},{0,7},{9,8},{10,9},{11,1... | collective-permute-start | bytes 294920 | tf_op jit(solution)/shard_map/ppermute | solution.py:545
  19.5 1.1 %copy-start.6 = (f32[384,512]{1,0:T(8,128)S(1)}, f32[384,512]{1,0:T(8,128)}, u32[]{:S(2)}) copy-start(f32[384,512]{1,0:T(8,128)} %get-tuple-element.33.f_ref) | copy-start | bytes 2359300
  20.6 0.9 %copy-start.13 = (bf16[144,432]{1,0:T(8,128)(2,1)S(1)}, bf16[144,432]{1,0:T(8,128)(2,1)}, u32[]{:S(2)}) copy-start(bf16[144,432]{1,0:T(8,128)(2,1)} %constant.51.clone.xe_wd) | copy-start | bytes 373252
  23.0 1.4 %collective-permute-start.2 = (f32[56,512]{1,0:T(8,128)S(1)}, f32[56,512]{1,0:T(8,128)S(1)}, u32[]{:S(2)}, u32[]{:S(2)}) collective-permute-start(f32[56,512]{1,0:T(8,128)S(1)} %get-tuple-element.39), channel_id=1, source_target_pairs={{0,8},{8,0},{16,24},{24,16},{32,40},{40,32},{48,56},{56,48},{64,72... | collective-permute-start | bytes 344072 | tf_op jit(solution)/shard_map/ppermute | solution.py:550
  24.5 7.9 %collective-permute-start.3 = (f32[56,512]{1,0:T(8,128)S(1)}, f32[56,512]{1,0:T(8,128)S(1)}, u32[]{:S(2)}, u32[]{:S(2)}) collective-permute-start(f32[56,512]{1,0:T(8,128)S(1)} %div_out.1), channel_id=1, source_target_pairs={{0,1},{1,0},{2,3},{3,2},{4,5},{5,4},{6,7},{7,6},{8,16},{9,17},{10,... | collective-permute-start | bytes 344072 | tf_op jit(solution)/shard_map/ppermute | solution.py:561
  32.4 1.3 %collective-permute-start.4 = (f32[24,512]{1,0:T(8,128)S(1)}, f32[24,512]{1,0:T(8,128)S(1)}, u32[]{:S(2)}, u32[]{:S(2)}) collective-permute-start(f32[24,512]{1,0:T(8,128)S(1)} %div_out_far.1), channel_id=1, source_target_pairs={{0,8},{8,0},{16,24},{24,16},{32,40},{40,32},{48,56},{56,48},{64,72... | collective-permute-start | bytes 147464 | tf_op jit(solution)/shard_map/ppermute | solution.py:550
  33.8 9.6 %copy-start.11 = (bf16[144,864]{1,0:T(8,128)(2,1)S(1)}, bf16[144,864]{1,0:T(8,128)(2,1)}, u32[]{:S(2)}) copy-start(bf16[144,864]{1,0:T(8,128)(2,1)} %constant.55.clone.z_st) | copy-start | bytes 746500
  33.8 9.6 %copy-start.14 = (bf16[144,432]{1,0:T(8,128)(2,1)S(1)}, bf16[144,432]{1,0:T(8,128)(2,1)}, u32[]{:S(2)}) copy-start(bf16[144,432]{1,0:T(8,128)(2,1)} %constant.53.clone.xe_k) | copy-start | bytes 373252
  36.2 18.9 %copy-start.9 = (bf16[192,1152]{1,0:T(8,128)(2,1)S(1)}, bf16[192,1152]{1,0:T(8,128)(2,1)}, u32[]{:S(2)}) copy-start(bf16[192,1152]{1,0:T(8,128)(2,1)} %constant.57.clone.refs_6_) | copy-start | bytes 1327108
  36.2 4.5 %collective-permute-start.5 = (f32[32,512]{1,0:T(8,128)S(1)}, f32[32,512]{1,0:T(8,128)S(1)}, u32[]{:S(2)}, u32[]{:S(2)}) collective-permute-start(f32[32,512]{1,0:T(8,128)S(1)} %get-tuple-element.44), channel_id=1, source_target_pairs={{0,1},{1,2},{2,3},{3,4},{4,5},{5,6},{6,7},{7,0},{8,9},{9,10},{10,1... | collective-permute-start | bytes 196616 | tf_op jit(solution)/shard_map/ppermute | solution.py:545
  38.2 5.2 %collective-permute-start.6 = (f32[32,512]{1,0:T(8,128)S(1)}, f32[32,512]{1,0:T(8,128)S(1)}, u32[]{:S(2)}, u32[]{:S(2)}) collective-permute-start(f32[32,512]{1,0:T(8,128)S(1)} %get-tuple-element.45), channel_id=1, source_target_pairs={{1,0},{2,1},{3,2},{4,3},{5,4},{6,5},{7,6},{0,7},{9,8},{10,9},{11,1... | collective-permute-start | bytes 196616 | tf_op jit(solution)/shard_map/ppermute | solution.py:545
  44.4 1.4 %collective-permute-start.7 = (f32[56,512]{1,0:T(8,128)S(1)}, f32[56,512]{1,0:T(8,128)S(1)}, u32[]{:S(2)}, u32[]{:S(2)}) collective-permute-start(f32[56,512]{1,0:T(8,128)S(1)} %get-tuple-element.49), channel_id=1, source_target_pairs={{0,8},{8,0},{16,24},{24,16},{32,40},{40,32},{48,56},{56,48},{64,72... | collective-permute-start | bytes 344072 | tf_op jit(solution)/shard_map/ppermute | solution.py:550
  45.9 7.9 %collective-permute-start.8 = (f32[56,512]{1,0:T(8,128)S(1)}, f32[56,512]{1,0:T(8,128)S(1)}, u32[]{:S(2)}, u32[]{:S(2)}) collective-permute-start(f32[56,512]{1,0:T(8,128)S(1)} %stiff_out.1), channel_id=1, source_target_pairs={{0,1},{1,0},{2,3},{3,2},{4,5},{5,4},{6,7},{7,6},{8,16},{9,17},{10,... | collective-permute-start | bytes 344072 | tf_op jit(solution)/shard_map/ppermute | solution.py:561
  53.8 1.3 %collective-permute-start.9 = (f32[24,512]{1,0:T(8,128)S(1)}, f32[24,512]{1,0:T(8,128)S(1)}, u32[]{:S(2)}, u32[]{:S(2)}) collective-permute-start(f32[24,512]{1,0:T(8,128)S(1)} %stiff_out_far.1), channel_id=1, source_target_pairs={{0,8},{8,0},{16,24},{24,16},{32,40},{40,32},{48,56},{56,48},{64,72... | collective-permute-start | bytes 147464 | tf_op jit(solution)/shard_map/ppermute | solution.py:550
  57.0 3.8 %collective-permute-start.10 = (f32[8,512]{1,0:T(8,128)S(1)}, f32[8,512]{1,0:T(8,128)S(1)}, u32[]{:S(2)}, u32[]{:S(2)}) collective-permute-start(f32[8,512]{1,0:T(8,128)S(1)} %get-tuple-element.54), channel_id=1, source_target_pairs={{0,1},{1,2},{2,3},{3,4},{4,5},{5,6},{6,7},{7,0},{8,9},{9,10},{10,1... | collective-permute-start | bytes 49160 | tf_op jit(solution)/shard_map/ppermute | solution.py:545
  58.2 4.6 %collective-permute-start.11 = (f32[8,512]{1,0:T(8,128)S(1)}, f32[8,512]{1,0:T(8,128)S(1)}, u32[]{:S(2)}, u32[]{:S(2)}) collective-permute-start(f32[8,512]{1,0:T(8,128)S(1)} %get-tuple-element.55), channel_id=1, source_target_pairs={{1,0},{2,1},{3,2},{4,3},{5,4},{6,5},{7,6},{0,7},{9,8},{10,9},{11,1... | collective-permute-start | bytes 49160 | tf_op jit(solution)/shard_map/ppermute | solution.py:545
  62.9 4.6 %collective-permute-start.12 = (f32[64,512]{1,0:T(8,128)S(1)}, f32[64,512]{1,0:T(8,128)S(1)}, u32[]{:S(2)}, u32[]{:S(2)}) collective-permute-start(f32[64,512]{1,0:T(8,128)S(1)} %get-tuple-element.59), channel_id=1, source_target_pairs={{0,8},{8,0},{16,24},{24,16},{32,40},{40,32},{48,56},{56,48},{64,72... | collective-permute-start | bytes 393224 | tf_op jit(solution)/shard_map/ppermute | solution.py:550
  63.0 8.1 %collective-permute-start.13 = (f32[64,512]{1,0:T(8,128)S(1)}, f32[64,512]{1,0:T(8,128)S(1)}, u32[]{:S(2)}, u32[]{:S(2)}) collective-permute-start(f32[64,512]{1,0:T(8,128)S(1)} %get-tuple-element.60), channel_id=1, source_target_pairs={{0,1},{1,0},{2,3},{3,2},{4,5},{5,4},{6,7},{7,6},{8,16},{9,17},{10,... | collective-permute-start | bytes 393224 | tf_op jit(solution)/shard_map/ppermute | solution.py:561

commit v2 on v1

--- a/solution.py
+++ b/solution.py
@@ -12,7 +12,6 @@
 F32 = jnp.float32
 BF16 = jnp.bfloat16
 MIB = 2**20
-FORCE_VMEM = 56
 
 
 def legendre_pair(degree, points):
@@ -67,8 +66,7 @@
 
 
 def right_const(m):
-    hi, lo = hi_lo(m)
-    return np.concatenate([hi, hi, lo], axis=0)
+    return np.concatenate(hi_lo(m), axis=0)
 
 
 def block_diag(m, count):
@@ -206,8 +204,9 @@
     c["y_in"] = right_const(
         np.concatenate([block_diag(interp.T, 32), block_diag(slopes.T, 32)], axis=1)
     )
-    c["zx_in"] = left_const(
-        np.concatenate([zx(interp, interp), zx(slopes, interp), zx(interp, slopes)], axis=0)
+    c["zx_in"] = np.concatenate(
+        hi_lo(np.concatenate([zx(interp, interp), zx(slopes, interp), zx(interp, slopes)], axis=0)),
+        axis=1,
     )
     test = v[:, None] * interp
     back = zx(test.T, test.T).reshape(8, 16, 288)
@@ -244,6 +243,8 @@
 
 def rmul(x, const):
     hi, lo = split(x)
+    depth = const.shape[0] // 2
+    const = jnp.concatenate([const[:depth], const], axis=0)
     return jnp.dot(jnp.concatenate([hi, lo, hi], axis=1), const, preferred_element_type=F32)
 
 
@@ -273,40 +274,40 @@
 
 def force_kernel(*refs):
     sources, (f_ref, r_ref, l_ref), held, sem = refs[:10], refs[10:13], refs[13:23], refs[23]
+    v_ref, b_ref, y_in, zx_in, zx_out, y_out, xm_w, xm_wd, wd_y, w_y = held
     copies = [pltpu.make_async_copy(a, b, sem.at[k]) for k, (a, b) in enumerate(zip(sources, held))]
-    for k in (0, 2, 1, 3, 4, 5, 6, 7, 8, 9):
+    for k in (2, 0, 1, 3, 4, 5, 6, 7, 8, 9):
         copies[k].start()
-    v_ref, b_ref, y_in, zx_in, zx_out, y_out, xm_w, xm_wd, wd_y, w_y = held
+    copies[2].wait()
     copies[0].wait()
-    copies[2].wait()
-    copies[1].wait()
-    copies[3].wait()
     v = v_ref[...].reshape(384, 512)
+    parts = [rmul(v[:, cut], y_in[...]) for cut in (slice(0, 256), slice(256, 512))]
+    value = jnp.concatenate([p[:, :384] for p in parts], axis=1)
+    slope = jnp.concatenate([p[:, 384:] for p in parts], axis=1)
+    for copy in (copies[1], *copies[3:]):
+        copy.wait()
+    low = zx_in[...]
+    zx3 = jnp.concatenate([low[:, :128], low], axis=1)
+    u, gz, gx, gy = [], [], [], []
+    for c in range(3):
+        rows = slice(128 * c, 128 * c + 128)
+        most = lmul(zx3, value[rows])
+        u.append(most[:288])
+        gz.append(most[288:576])
+        gx.append(most[576:])
+        gy.append(lmul(zx3[:288], slope[rows]))
     b = b_ref[...].reshape(128, 512)
-    halves = []
-    for h in range(2):
-        cut = slice(256 * h, 256 * h + 256)
-        first = rmul(v[:, cut], y_in[...])
-        bq = lmul(zx_in[:288, :], rmul(b[:, cut], y_in[:, :384]))
-        u, gz, gx, gy = [], [], [], []
-        for c in range(3):
-            rows = slice(128 * c, 128 * c + 128)
-            most = lmul(zx_in[...], first[rows, :384])
-            u.append(most[:288])
-            gz.append(most[288:576])
-            gx.append(most[576:])
-            gy.append(lmul(zx_in[:288, :], first[rows, 384:]))
-        b2 = bq * bq
-        back = []
-        if h == 0:
-            for copy in copies[4:]:
-                copy.wait()
-        for c in range(3):
-            conv = u[0] * gz[c] + u[1] * gx[c] + u[2] * gy[c]
-            if c != 1:
-                conv = conv + b2 * u[c]
-            back.append(lmul(zx_out[...], -conv))
-        halves.append(rmul(jnp.concatenate(back, axis=0), y_out[...]))
+    parts = [rmul(b[:, cut], y_in[:, :384]) for cut in (slice(0, 256), slice(256, 512))]
+    bq = lmul(zx3[:288], jnp.concatenate(parts, axis=1))
+    b2 = bq * bq
+    back = []
+    for c in range(3):
+        conv = u[0] * gz[c] + u[1] * gx[c] + u[2] * gy[c]
+        if c != 1:
+            conv = conv + b2 * u[c]
+        back.append(lmul(zx_out[...], -conv))
+    back = jnp.concatenate(back, axis=0)
+    halves = [rmul(back[:, cut], y_out[...]) for cut in (slice(0, 384), slice(384, 768))]
     f = dss_lanes(jnp.concatenate(halves, axis=1))
     f_ref[...] = f
     s = lmul(xm_wd[...], f[128:256]) * w_y[...]
@@ -501,23 +502,24 @@
         out_msg_ref[rows] = jnp.where(odd, up, down)
 
 
-def last_z_kernel(g_ref, f_up, f_down, in_ref, out_msg_ref, _, out_ref, force_ref, face_ref, sem):
+def last_z_kernel(g_ref, f_up, f_down, in_ref, out_msg_ref, _, out_ref, force_ref, face_ref, p_ref, sem):
     has_b, has_a, _, _ = flags()
     odd = is_odd()
     inner, outer = in_ref[...], out_msg_ref[...] * jnp.where(odd, has_a, has_b)
     below, above = jnp.where(odd, inner, outer), jnp.where(odd, outer, inner)
+    p_ref[...] = g_ref[...]
+    p_ref[:16] += below[:16]
+    p_ref[112:] += above[:16]
     face_ref[:48] = f_down[...] + below[16:]
     face_ref[48:] = f_up[...] + above[16:]
-    copies = []
+    copies = [pltpu.make_async_copy(p_ref, out_ref, sem.at[6])]
     for c in range(3):
         for k, row in enumerate((128 * c, 128 * c + 112)):
             src = face_ref.at[pl.ds(48 * k + 16 * c, 16)]
             dst = force_ref.at[pl.ds(row, 16)]
             copies.append(pltpu.make_async_copy(src, dst, sem.at[2 * c + k]))
-            copies[-1].start()
-    out_ref[...] = g_ref[...]
-    out_ref[:16] += below[:16]
-    out_ref[112:] += above[:16]
+    for copy in copies:
+        copy.start()
     for copy in copies:
         copy.wait()
 
@@ -582,6 +584,7 @@
         bfield,
         *consts("y_in", "zx_in", "zx_out", "y_out", "xm_w", "xm_wd", "wd_y", "w_y"),
     )
+    force_args = [pltpu.with_memory_space_constraint(x, pltpu.HBM) for x in force_args]
     f, right, left = call(
         force_kernel,
         "force",
@@ -589,7 +592,7 @@
         *force_args,
         scratch=[pltpu.VMEM(a.shape, a.dtype) for a in force_args],
         sems=10,
-        vmem=FORCE_VMEM,
+        vmem=32,
         hbm_in=range(10),
     )
     from_l, from_r = exchange_x(right, left)
@@ -662,10 +665,10 @@
         inner,
         outer,
         force,
-        scratch=(96,),
-        sems=6,
+        scratch=(96, 128),
+        sems=7,
         hbm_in=(5,),
-        hbm_out=(1,),
+        hbm_out=(0, 1),
         alias={5: 1},
     )
     return force.reshape(3, 8, 16, 512), pressure.reshape(8, 16, 512)

time: 73.6 us -> 68.3 us (0.928)
  Pallas kernels: 19.1 us -> 16.1 us
  local copies, waits for them, and re-layouts: 2.15 us -> 0.12 us
    pallas_call x11, Pallas kernels: 19.1 us -> 16.1 us  [call(): pl.pallas_call(kernel, out_shape=[shape(o) for o in outs], in_specs=[spec...]
    unnamed x36 -> x34, local copies, waits for them, and re-layouts: 2.15 us -> 0.12 us
where the time goes in v2:
time: 68.3 us; the launch traced here: 67.5 us
  waiting for transfers between devices  29.8 us (44%)
  starting transfers between devices  20.4 us (30%)
  Pallas kernels  16.1 us (24%)
  between operations  1.11 us (2%)
    pallas_call x11, Pallas kernels, call(): pl.pallas_call(kernel, out_shape=[shape(o) for o in outs], in_specs=[spec...  16.1 us
    ppermute x3, starting transfers between devices, next_chip(): return lax.ppermute(x, ('wide', 'narrow'), pairs)  13.7 us
    ppermute x3, waiting for transfers between devices, next_chip(): return lax.ppermute(x, ('wide', 'narrow'), pairs)  10.4 us
    ppermute x3, waiting for transfers between devices, exchange_x(): lax.ppermute(leftward, 'narrow', left)  7.45 us
    ppermute x3, waiting for transfers between devices, exchange_x(): lax.ppermute(rightward, 'narrow', right)  6.88 us
    ppermute x5, waiting for transfers between devices, other_core(): return lax.ppermute(x, 'wide', [(i, i + 1 - 2 * (i % 2)) for i in range(n)])  5.06 us
    ppermute x3, starting transfers between devices, exchange_x(): lax.ppermute(rightward, 'narrow', right)  4.92 us
  transfers between devices with their start and end apart: 14, of which 13 were waited for; matrix products, arithmetic and copies ran while one was open for 0% of the time, Pallas kernels for 0%

profile of v2, /device:TPU:6, one launch (start us, length us, event | category | flops | bytes accessed | tf_op | source)
XLA Modules:
  0.0 67.5 jit_solution(3386890756335567155)
XLA Ops:
  0.6 0.0 copy-start.4
  0.6 0.0 copy-start.7
  0.7 0.0 copy-start.11
  0.7 0.0 copy-start.13
  0.7 0.0 copy-start.15
  0.7 0.0 copy-start.1
  0.7 0.0 copy-start.6
  0.7 0.0 copy-start.9
  0.7 8.3 %force.1 = (f32[384,512]{1,0:T(8,128)S(1)}, f32[48,512]{1,0:T(8,128)S(1)}, f32[48,512]{1,0:T(8,128)S(1)}) custom-call(f32[3,8,16,512]{3,2,1,0:T(8,128)} %refs_0_.1, f32[8,16,512]{2,1,0:T(8,128)} %refs_1_.1, bf16[512,768]{1,0:T(8,128)(2,1)} %constant.44.clone.refs_2_, bf16[864,256]{1,0:T(8,128)(2,1)} %constant.45.clone.refs_3_, ...), custom_call_target="tpu_custom_call" | custom-call | tf_op jit(solution)/shard_map/force/pallas_call | solution.py:531
  9.0 0.0 copy-start
  9.0 0.0 copy-start.2
  9.0 0.0 copy-start.3
  9.1 0.0 copy-start.5
  9.1 0.0 copy-start.14
  9.1 0.0 copy-start.16
  9.1 1.9 %collective-permute-start = (f32[48,512]{1,0:T(8,128)S(1)}, f32[48,512]{1,0:T(8,128)S(1)}, u32[]{:S(2)}, u32[]{:S(2)}) collective-permute-start(f32[48,512]{1,0:T(8,128)S(1)} %get-tuple-element.34), channel_id=1, source_target_pairs={{0,1},{1,2},{2,3},{3,4},{4,5},{5,6},{6,7},{7,0},{8,9},{9,10},{10,1... | collective-permute-start | bytes 294920 | tf_op jit(solution)/shard_map/ppermute | solution.py:547
  11.0 0.2 collective-permute-start.1
  11.2 2.9 %collective-permute-done.ml_ref = f32[48,512]{1,0:T(8,128)S(1)} collective-permute-done((f32[48,512]{1,0:T(8,128)S(1)}, f32[48,512]{1,0:T(8,128)S(1)}, u32[]{:S(2)}, u32[]{:S(2)}) %collective-permute-start) | collective-permute-done | bytes 98336 | tf_op jit(solution)/shard_map/ppermute | solution.py:547
  14.1 2.8 %collective-permute-done.1.mr_ref = f32[48,512]{1,0:T(8,128)S(1)} collective-permute-done((f32[48,512]{1,0:T(8,128)S(1)}, f32[48,512]{1,0:T(8,128)S(1)}, u32[]{:S(2)}, u32[]{:S(2)}) %collective-permute-start.1) | collective-permute-done | bytes 98336 | tf_op jit(solution)/shard_map/ppermute | solution.py:547
  16.9 0.0 copy-done.4
  16.9 0.0 copy-done.7
  16.9 0.0 copy-done.11
  16.9 0.0 copy-done.13
  16.9 0.0 copy-done.15
  16.9 1.5 %div.1 = (f32[384,512]{1,0:T(8,128)}, f32[48,512]{1,0:T(8,128)S(1)}, f32[48,512]{1,0:T(8,128)S(1)}, f32[144,512]{1,0:T(8,128)S(1)}, f32[56,512]{1,0:T(8,128)S(1)...) custom-call(f32[384,512]{1,0:T(8,128)S(1)} %get-tuple-element.33.f_ref, ...), custom_call_target="tpu_custom_call" | custom-call | tf_op jit(solution)/shard_map/div/pallas_call | solution.py:531
  18.4 0.1 collective-permute-start.2
  18.5 1.3 %collective-permute-done.2.in_ref.refs_3_ = f32[56,512]{1,0:T(8,128)S(1)} collective-permute-done((f32[56,512]{1,0:T(8,128)S(1)}, f32[56,512]{1,0:T(8,128)S(1)}, u32[]{:S(2)}, u32[]{:S(2)}) %collective-permute-start.2) | collective-permute-done | bytes 114720 | tf_op jit(solution)/shard_map/ppermute | solution.py:552
  19.9 4.7 %collective-permute-start.3 = (f32[56,512]{1,0:T(8,128)S(1)}, f32[56,512]{1,0:T(8,128)S(1)}, u32[]{:S(2)}, u32[]{:S(2)}) collective-permute-start(f32[56,512]{1,0:T(8,128)S(1)} %div_out.1), channel_id=1, source_target_pairs={{0,1},{1,0},{2,3},{3,2},{4,5},{5,4},{6,7},{7,6},{8,16},{9,17},{10,... | collective-permute-start | bytes 344072 | tf_op jit(solution)/shard_map/ppermute | solution.py:563
  24.6 3.2 %collective-permute-done.3.out_msg_ref.refs_4_ = f32[56,512]{1,0:T(8,128)S(1)} collective-permute-done((f32[56,512]{1,0:T(8,128)S(1)}, f32[56,512]{1,0:T(8,128)S(1)}, u32[]{:S(2)}, u32[]{:S(2)}) %collective-permute-start.3) | collective-permute-done | bytes 114720 | tf_op jit(solution)/shard_map/ppermute | solution.py:563
  27.8 0.1 collective-permute-start.4
  27.9 1.2 %collective-permute-done.4.refs_5_ = f32[24,512]{1,0:T(8,128)S(1)} collective-permute-done((f32[24,512]{1,0:T(8,128)S(1)}, f32[24,512]{1,0:T(8,128)S(1)}, u32[]{:S(2)}, u32[]{:S(2)}) %collective-permute-start.4) | collective-permute-done | bytes 49184 | tf_op jit(solution)/shard_map/ppermute | solution.py:552
  29.1 0.0 copy-done.1
  29.1 0.0 copy-done.6
  29.1 0.0 copy-done.9
  29.1 0.0 copy-done
  29.1 0.0 copy-done.2
  29.2 0.0 copy-start.10
  29.2 0.0 copy-start.12
  29.2 2.3 %first_pass.1 = (f32[192,512]{1,0:T(8,128)S(1)}, f32[128,512]{1,0:T(8,128)S(1)}, f32[32,512]{1,0:T(8,128)S(1)}, f32[32,512]{1,0:T(8,128)S(1)}) custom-call(f32[144,512]{1,0:T(8,128)S(1)} %get-tuple-element.36.refs_0_, f32[40,512]{1,0:T(8,128)S(1)} %get-tuple-element.37.refs_1_, f32[40,512]{1,0:T(8,128)S(1)} %get-tuple-element.38.refs_2_, ...), custom_call_target="tpu_custom_call" | custom-call | tf_op jit(solution)/shard_map/first_pass/pallas_call | solution.py:531
  31.5 0.0 copy-start.8
  31.5 1.8 %collective-permute-start.5 = (f32[32,512]{1,0:T(8,128)S(1)}, f32[32,512]{1,0:T(8,128)S(1)}, u32[]{:S(2)}, u32[]{:S(2)}) collective-permute-start(f32[32,512]{1,0:T(8,128)S(1)} %get-tuple-element.44), channel_id=1, source_target_pairs={{0,1},{1,2},{2,3},{3,4},{4,5},{5,6},{6,7},{7,0},{8,9},{9,10},{10,1... | collective-permute-start | bytes 196616 | tf_op jit(solution)/shard_map/ppermute | solution.py:547
  33.4 0.3 collective-permute-start.6
  33.6 2.2 %collective-permute-done.5.ml_ref = f32[32,512]{1,0:T(8,128)S(1)} collective-permute-done((f32[32,512]{1,0:T(8,128)S(1)}, f32[32,512]{1,0:T(8,128)S(1)}, u32[]{:S(2)}, u32[]{:S(2)}) %collective-permute-start.5) | collective-permute-done | bytes 65568 | tf_op jit(solution)/shard_map/ppermute | solution.py:547
  35.9 2.7 %collective-permute-done.6.mr_ref = f32[32,512]{1,0:T(8,128)S(1)} collective-permute-done((f32[32,512]{1,0:T(8,128)S(1)}, f32[32,512]{1,0:T(8,128)S(1)}, u32[]{:S(2)}, u32[]{:S(2)}) %collective-permute-start.6) | collective-permute-done | bytes 65568 | tf_op jit(solution)/shard_map/ppermute | solution.py:547
  38.5 0.0 copy-done.10
  38.5 1.1 %stiff.1 = (f32[128,512]{1,0:T(8,128)S(1)}, f32[144,512]{1,0:T(8,128)S(1)}, f32[56,512]{1,0:T(8,128)S(1)}, f32[56,512]{1,0:T(8,128)S(1)}, f32[40,512]{1,0:T(8,12...) custom-call(f32[128,512]{1,0:T(8,128)S(1)} %get-tuple-element.43.g_ref, ...), custom_call_target="tpu_custom_call" | custom-call | tf_op jit(solution)/shard_map/stiff/pallas_call | solution.py:531
  39.6 0.1 collective-permute-start.7
  39.7 1.3 %collective-permute-done.7.in_ref.refs_3_ = f32[56,512]{1,0:T(8,128)S(1)} collective-permute-done((f32[56,512]{1,0:T(8,128)S(1)}, f32[56,512]{1,0:T(8,128)S(1)}, u32[]{:S(2)}, u32[]{:S(2)}) %collective-permute-start.7) | collective-permute-done | bytes 114720 | tf_op jit(solution)/shard_map/ppermute | solution.py:552
  41.1 4.5 %collective-permute-start.8 = (f32[56,512]{1,0:T(8,128)S(1)}, f32[56,512]{1,0:T(8,128)S(1)}, u32[]{:S(2)}, u32[]{:S(2)}) collective-permute-start(f32[56,512]{1,0:T(8,128)S(1)} %stiff_out.1), channel_id=1, source_target_pairs={{0,1},{1,0},{2,3},{3,2},{4,5},{5,4},{6,7},{7,6},{8,16},{9,17},{10,... | collective-permute-start | bytes 344072 | tf_op jit(solution)/shard_map/ppermute | solution.py:563
  45.6 3.6 %collective-permute-done.8.out_msg_ref.refs_4_ = f32[56,512]{1,0:T(8,128)S(1)} collective-permute-done((f32[56,512]{1,0:T(8,128)S(1)}, f32[56,512]{1,0:T(8,128)S(1)}, u32[]{:S(2)}, u32[]{:S(2)}) %collective-permute-start.8) | collective-permute-done | bytes 114720 | tf_op jit(solution)/shard_map/ppermute | solution.py:563
  49.2 0.1 collective-permute-start.9
  49.2 1.2 %collective-permute-done.9.refs_5_ = f32[24,512]{1,0:T(8,128)S(1)} collective-permute-done((f32[24,512]{1,0:T(8,128)S(1)}, f32[24,512]{1,0:T(8,128)S(1)}, u32[]{:S(2)}, u32[]{:S(2)}) %collective-permute-start.9) | collective-permute-done | bytes 49184 | tf_op jit(solution)/shard_map/ppermute | solution.py:552
  50.5 0.0 copy-done.8
  50.5 1.9 %second_pass.1 = (f32[128,512]{1,0:T(8,128)S(1)}, f32[8,512]{1,0:T(8,128)S(1)}, f32[8,512]{1,0:T(8,128)S(1)}) custom-call(f32[192,512]{1,0:T(8,128)S(1)} %get-tuple-element.42.s_ref, f32[144,512]{1,0:T(8,128)S(1)} %get-tuple-element.46.refs_0_, f32[40,512]{1,0:T(8,128)S(1)} %get-tuple-element.47.refs_1_, f32[40,512]{1,0:T(8,128)S(1)} %get-tuple-element.48.refs_2_, ...), custom_call_target="tpu_custom_call" | custom-call | tf_op jit(solution)/shard_map/second_pass/pallas_call | solution.py:531
  52.4 1.2 %collective-permute-start.10 = (f32[8,512]{1,0:T(8,128)S(1)}, f32[8,512]{1,0:T(8,128)S(1)}, u32[]{:S(2)}, u32[]{:S(2)}) collective-permute-start(f32[8,512]{1,0:T(8,128)S(1)} %get-tuple-element.54), channel_id=1, source_target_pairs={{0,1},{1,2},{2,3},{3,4},{4,5},{5,6},{6,7},{7,0},{8,9},{9,10},{10,1... | collective-permute-start | bytes 49160 | tf_op jit(solution)/shard_map/ppermute | solution.py:547
  53.6 0.9 %collective-permute-start.11 = (f32[8,512]{1,0:T(8,128)S(1)}, f32[8,512]{1,0:T(8,128)S(1)}, u32[]{:S(2)}, u32[]{:S(2)}) collective-permute-start(f32[8,512]{1,0:T(8,128)S(1)} %get-tuple-element.55), channel_id=1, source_target_pairs={{1,0},{2,1},{3,2},{4,3},{5,4},{6,5},{7,6},{0,7},{9,8},{10,9},{11,1... | collective-permute-start | bytes 49160 | tf_op jit(solution)/shard_map/ppermute | solution.py:547
  54.5 1.7 %collective-permute-done.10.ml_ref = f32[8,512]{1,0:T(8,128)S(1)} collective-permute-done((f32[8,512]{1,0:T(8,128)S(1)}, f32[8,512]{1,0:T(8,128)S(1)}, u32[]{:S(2)}, u32[]{:S(2)}) %collective-permute-start.10) | collective-permute-done | bytes 16416 | tf_op jit(solution)/shard_map/ppermute | solution.py:547
  56.2 2.0 %collective-permute-done.11.mr_ref = f32[8,512]{1,0:T(8,128)S(1)} collective-permute-done((f32[8,512]{1,0:T(8,128)S(1)}, f32[8,512]{1,0:T(8,128)S(1)}, u32[]{:S(2)}, u32[]{:S(2)}) %collective-permute-start.11) | collective-permute-done | bytes 16416 | tf_op jit(solution)/shard_map/ppermute | solution.py:547
  58.2 0.1 last_x.1
  58.3 0.1 collective-permute-start.12
  58.4 4.5 %collective-permute-start.13 = (f32[64,512]{1,0:T(8,128)S(1)}, f32[64,512]{1,0:T(8,128)S(1)}, u32[]{:S(2)}, u32[]{:S(2)}) collective-permute-start(f32[64,512]{1,0:T(8,128)S(1)} %get-tuple-element.60), channel_id=1, source_target_pairs={{0,1},{1,0},{2,3},{3,2},{4,5},{5,4},{6,7},{7,6},{8,16},{9,17},{10,... | collective-permute-start | bytes 393224 | tf_op jit(solution)/shard_map/ppermute | solution.py:563
  62.9 0.0 collective-permute-done.12.in_ref
  62.9 3.6 %collective-permute-done.13.out_msg_ref = f32[64,512]{1,0:T(8,128)S(1)} collective-permute-done((f32[64,512]{1,0:T(8,128)S(1)}, f32[64,512]{1,0:T(8,128)S(1)}, u32[]{:S(2)}, u32[]{:S(2)}) %collective-permute-start.13) | collective-permute-done | bytes 131104 | tf_op jit(solution)/shard_map/ppermute | solution.py:563
  66.5 0.8 %last_z.1 = (f32[128,512]{1,0:T(8,128)}, f32[384,512]{1,0:T(8,128)}) custom-call(f32[128,512]{1,0:T(8,128)S(1)} %get-tuple-element.58.g_ref, f32[48,512]{1,0:T(8,128)S(1)} %get-tuple-element.56.f_up, f32[48,512]{1,0:T(8,128)S(1)} %get-tuple-element.57.f_down, f32[64,512]{1,0:T(8,128)S(1)} %collective-permute-done.12.in_ref, ...), custom_call_target="tpu_custom_call", output_to_operand_aliasing={{1}: (5, {})} | custom-call | tf_op jit(solution)/shard_map/last_z/pallas_call | solution.py:531
  (9 shorter events, 0.1 us)
Async XLA Ops:
  0.6 16.3 %copy-start.4 = (bf16[512,256]{1,0:T(8,128)(2,1)S(1)}, bf16[512,256]{1,0:T(8,128)(2,1)}, u32[]{:S(2)}) copy-start(bf16[512,256]{1,0:T(8,128)(2,1)} %constant.58.clone.refs_8_.wd_y) | copy-start | bytes 786436
  0.6 16.3 %copy-start.7 = (bf16[144,432]{1,0:T(8,128)(2,1)S(1)}, bf16[144,432]{1,0:T(8,128)(2,1)}, u32[]{:S(2)}) copy-start(bf16[144,432]{1,0:T(8,128)(2,1)} %constant.49.clone.xe_w) | copy-start | bytes 373252
  0.7 16.3 %copy-start.11 = (bf16[144,864]{1,0:T(8,128)(2,1)S(1)}, bf16[144,864]{1,0:T(8,128)(2,1)}, u32[]{:S(2)}) copy-start(bf16[144,864]{1,0:T(8,128)(2,1)} %constant.54.clone.z_div) | copy-start | bytes 746500
  0.7 16.3 %copy-start.13 = (bf16[144,432]{1,0:T(8,128)(2,1)S(1)}, bf16[144,432]{1,0:T(8,128)(2,1)}, u32[]{:S(2)}) copy-start(bf16[144,432]{1,0:T(8,128)(2,1)} %constant.51.clone.xe_wd) | copy-start | bytes 373252
  0.7 16.3 %copy-start.15 = (f32[1,512]{1,0:T(1,128)S(1)}, f32[1,512]{1,0:T(1,128)}, u32[]{:S(2)}) copy-start(f32[1,512]{1,0:T(1,128)} %constant.60.clone.refs_9_.w_y.refs_15_) | copy-start | bytes 6148
  0.7 28.4 %copy-start.1 = (bf16[1024,640]{1,0:T(8,128)(2,1)S(1)}, bf16[1024,640]{1,0:T(8,128)(2,1)}, u32[]{:S(2)}) copy-start(bf16[1024,640]{1,0:T(8,128)(2,1)} %constant.63.clone.refs_8_) | copy-start | bytes 3932164
  0.7 28.4 %copy-start.6 = (bf16[128,624]{1,0:T(8,128)(2,1)S(1)}, bf16[128,624]{1,0:T(8,128)(2,1)}, u32[]{:S(2)}) copy-start(bf16[128,624]{1,0:T(8,128)(2,1)} %constant.62.clone.refs_10_) | copy-start | bytes 479236
  0.7 28.4 %copy-start.9 = (bf16[192,1152]{1,0:T(8,128)(2,1)S(1)}, bf16[192,1152]{1,0:T(8,128)(2,1)}, u32[]{:S(2)}) copy-start(bf16[192,1152]{1,0:T(8,128)(2,1)} %constant.56.clone.refs_6_) | copy-start | bytes 1327108
  9.0 20.1 %copy-start = (bf16[1280,512]{1,0:T(8,128)(2,1)S(1)}, bf16[1280,512]{1,0:T(8,128)(2,1)}, u32[]{:S(2)}) copy-start(bf16[1280,512]{1,0:T(8,128)(2,1)} %constant.64.clone.refs_11_) | copy-start | bytes 3932164
  9.0 20.1 %copy-start.2 = (f32[208,640]{1,0:T(8,128)S(1)}, f32[208,640]{1,0:T(8,128)}, u32[]{:S(2)}) copy-start(f32[208,640]{1,0:T(8,128)} %constant.65.clone.refs_9_) | copy-start | bytes 1597444
  9.0 20.1 %copy-start.3 = (bf16[208,576]{1,0:T(8,128)(2,1)S(1)}, bf16[208,576]{1,0:T(8,128)(2,1)}, u32[]{:S(2)}) copy-start(bf16[208,576]{1,0:T(8,128)(2,1)} %constant.61.clone.refs_7_) | copy-start | bytes 718852
  9.1 20.1 %copy-start.5 = (bf16[512,256]{1,0:T(8,128)(2,1)S(1)}, bf16[512,256]{1,0:T(8,128)(2,1)}, u32[]{:S(2)}) copy-start(bf16[512,256]{1,0:T(8,128)(2,1)} %constant.59.clone.refs_14_.k_y) | copy-start | bytes 786436
  9.1 20.1 %copy-start.14 = (bf16[32,384]{1,0:T(8,128)(2,1)S(1)}, bf16[32,384]{1,0:T(8,128)(2,1)}, u32[]{:S(2)}) copy-start(bf16[32,384]{1,0:T(8,128)(2,1)} %constant.48.clone.refs_6_.refs_12_) | copy-start | bytes 73732
  9.1 20.1 %copy-start.16 = (bf16[32,384]{1,0:T(8,128)(2,1)S(1)}, bf16[32,384]{1,0:T(8,128)(2,1)}, u32[]{:S(2)}) copy-start(bf16[32,384]{1,0:T(8,128)(2,1)} %constant.52.clone.refs_13_) | copy-start | bytes 73732
  9.1 5.0 %collective-permute-start = (f32[48,512]{1,0:T(8,128)S(1)}, f32[48,512]{1,0:T(8,128)S(1)}, u32[]{:S(2)}, u32[]{:S(2)}) collective-permute-start(f32[48,512]{1,0:T(8,128)S(1)} %get-tuple-element.34), channel_id=1, source_target_pairs={{0,1},{1,2},{2,3},{3,4},{4,5},{5,6},{6,7},{7,0},{8,9},{9,10},{10,1... | collective-permute-start | bytes 294920 | tf_op jit(solution)/shard_map/ppermute | solution.py:547
  11.0 5.9 %collective-permute-start.1 = (f32[48,512]{1,0:T(8,128)S(1)}, f32[48,512]{1,0:T(8,128)S(1)}, u32[]{:S(2)}, u32[]{:S(2)}) collective-permute-start(f32[48,512]{1,0:T(8,128)S(1)} %get-tuple-element.35), channel_id=1, source_target_pairs={{1,0},{2,1},{3,2},{4,3},{5,4},{6,5},{7,6},{0,7},{9,8},{10,9},{11,1... | collective-permute-start | bytes 294920 | tf_op jit(solution)/shard_map/ppermute | solution.py:547
  18.4 1.4 %collective-permute-start.2 = (f32[56,512]{1,0:T(8,128)S(1)}, f32[56,512]{1,0:T(8,128)S(1)}, u32[]{:S(2)}, u32[]{:S(2)}) collective-permute-start(f32[56,512]{1,0:T(8,128)S(1)} %get-tuple-element.39), channel_id=1, source_target_pairs={{0,8},{8,0},{16,24},{24,16},{32,40},{40,32},{48,56},{56,48},{64,72... | collective-permute-start | bytes 344072 | tf_op jit(solution)/shard_map/ppermute | solution.py:552
  19.9 7.9 %collective-permute-start.3 = (f32[56,512]{1,0:T(8,128)S(1)}, f32[56,512]{1,0:T(8,128)S(1)}, u32[]{:S(2)}, u32[]{:S(2)}) collective-permute-start(f32[56,512]{1,0:T(8,128)S(1)} %div_out.1), channel_id=1, source_target_pairs={{0,1},{1,0},{2,3},{3,2},{4,5},{5,4},{6,7},{7,6},{8,16},{9,17},{10,... | collective-permute-start | bytes 344072 | tf_op jit(solution)/shard_map/ppermute | solution.py:563
  27.8 1.3 %collective-permute-start.4 = (f32[24,512]{1,0:T(8,128)S(1)}, f32[24,512]{1,0:T(8,128)S(1)}, u32[]{:S(2)}, u32[]{:S(2)}) collective-permute-start(f32[24,512]{1,0:T(8,128)S(1)} %div_out_far.1), channel_id=1, source_target_pairs={{0,8},{8,0},{16,24},{24,16},{32,40},{40,32},{48,56},{56,48},{64,72... | collective-permute-start | bytes 147464 | tf_op jit(solution)/shard_map/ppermute | solution.py:552
  29.2 9.4 %copy-start.10 = (bf16[144,864]{1,0:T(8,128)(2,1)S(1)}, bf16[144,864]{1,0:T(8,128)(2,1)}, u32[]{:S(2)}) copy-start(bf16[144,864]{1,0:T(8,128)(2,1)} %constant.55.clone.z_st) | copy-start | bytes 746500
  29.2 9.4 %copy-start.12 = (bf16[144,432]{1,0:T(8,128)(2,1)S(1)}, bf16[144,432]{1,0:T(8,128)(2,1)}, u32[]{:S(2)}) copy-start(bf16[144,432]{1,0:T(8,128)(2,1)} %constant.53.clone.xe_k) | copy-start | bytes 373252
  31.5 18.9 %copy-start.8 = (bf16[192,1152]{1,0:T(8,128)(2,1)S(1)}, bf16[192,1152]{1,0:T(8,128)(2,1)}, u32[]{:S(2)}) copy-start(bf16[192,1152]{1,0:T(8,128)(2,1)} %constant.57.clone.refs_6_) | copy-start | bytes 1327108
  31.5 4.3 %collective-permute-start.5 = (f32[32,512]{1,0:T(8,128)S(1)}, f32[32,512]{1,0:T(8,128)S(1)}, u32[]{:S(2)}, u32[]{:S(2)}) collective-permute-start(f32[32,512]{1,0:T(8,128)S(1)} %get-tuple-element.44), channel_id=1, source_target_pairs={{0,1},{1,2},{2,3},{3,4},{4,5},{5,6},{6,7},{7,0},{8,9},{9,10},{10,1... | collective-permute-start | bytes 196616 | tf_op jit(solution)/shard_map/ppermute | solution.py:547
  33.4 5.2 %collective-permute-start.6 = (f32[32,512]{1,0:T(8,128)S(1)}, f32[32,512]{1,0:T(8,128)S(1)}, u32[]{:S(2)}, u32[]{:S(2)}) collective-permute-start(f32[32,512]{1,0:T(8,128)S(1)} %get-tuple-element.45), channel_id=1, source_target_pairs={{1,0},{2,1},{3,2},{4,3},{5,4},{6,5},{7,6},{0,7},{9,8},{10,9},{11,1... | collective-permute-start | bytes 196616 | tf_op jit(solution)/shard_map/ppermute | solution.py:547
  39.6 1.4 %collective-permute-start.7 = (f32[56,512]{1,0:T(8,128)S(1)}, f32[56,512]{1,0:T(8,128)S(1)}, u32[]{:S(2)}, u32[]{:S(2)}) collective-permute-start(f32[56,512]{1,0:T(8,128)S(1)} %get-tuple-element.49), channel_id=1, source_target_pairs={{0,8},{8,0},{16,24},{24,16},{32,40},{40,32},{48,56},{56,48},{64,72... | collective-permute-start | bytes 344072 | tf_op jit(solution)/shard_map/ppermute | solution.py:552
  41.1 8.1 %collective-permute-start.8 = (f32[56,512]{1,0:T(8,128)S(1)}, f32[56,512]{1,0:T(8,128)S(1)}, u32[]{:S(2)}, u32[]{:S(2)}) collective-permute-start(f32[56,512]{1,0:T(8,128)S(1)} %stiff_out.1), channel_id=1, source_target_pairs={{0,1},{1,0},{2,3},{3,2},{4,5},{5,4},{6,7},{7,6},{8,16},{9,17},{10,... | collective-permute-start | bytes 344072 | tf_op jit(solution)/shard_map/ppermute | solution.py:563
  49.2 1.3 %collective-permute-start.9 = (f32[24,512]{1,0:T(8,128)S(1)}, f32[24,512]{1,0:T(8,128)S(1)}, u32[]{:S(2)}, u32[]{:S(2)}) collective-permute-start(f32[24,512]{1,0:T(8,128)S(1)} %stiff_out_far.1), channel_id=1, source_target_pairs={{0,8},{8,0},{16,24},{24,16},{32,40},{40,32},{48,56},{56,48},{64,72... | collective-permute-start | bytes 147464 | tf_op jit(solution)/shard_map/ppermute | solution.py:552
  52.4 3.8 %collective-permute-start.10 = (f32[8,512]{1,0:T(8,128)S(1)}, f32[8,512]{1,0:T(8,128)S(1)}, u32[]{:S(2)}, u32[]{:S(2)}) collective-permute-start(f32[8,512]{1,0:T(8,128)S(1)} %get-tuple-element.54), channel_id=1, source_target_pairs={{0,1},{1,2},{2,3},{3,4},{4,5},{5,6},{6,7},{7,0},{8,9},{9,10},{10,1... | collective-permute-start | bytes 49160 | tf_op jit(solution)/shard_map/ppermute | solution.py:547
  53.6 4.6 %collective-permute-start.11 = (f32[8,512]{1,0:T(8,128)S(1)}, f32[8,512]{1,0:T(8,128)S(1)}, u32[]{:S(2)}, u32[]{:S(2)}) collective-permute-start(f32[8,512]{1,0:T(8,128)S(1)} %get-tuple-element.55), channel_id=1, source_target_pairs={{1,0},{2,1},{3,2},{4,3},{5,4},{6,5},{7,6},{0,7},{9,8},{10,9},{11,1... | collective-permute-start | bytes 49160 | tf_op jit(solution)/shard_map/ppermute | solution.py:547
  58.3 4.6 %collective-permute-start.12 = (f32[64,512]{1,0:T(8,128)S(1)}, f32[64,512]{1,0:T(8,128)S(1)}, u32[]{:S(2)}, u32[]{:S(2)}) collective-permute-start(f32[64,512]{1,0:T(8,128)S(1)} %get-tuple-element.59), channel_id=1, source_target_pairs={{0,8},{8,0},{16,24},{24,16},{32,40},{40,32},{48,56},{56,48},{64,72... | collective-permute-start | bytes 393224 | tf_op jit(solution)/shard_map/ppermute | solution.py:552
  58.4 8.1 %collective-permute-start.13 = (f32[64,512]{1,0:T(8,128)S(1)}, f32[64,512]{1,0:T(8,128)S(1)}, u32[]{:S(2)}, u32[]{:S(2)}) collective-permute-start(f32[64,512]{1,0:T(8,128)S(1)} %get-tuple-element.60), channel_id=1, source_target_pairs={{0,1},{1,0},{2,3},{3,2},{4,5},{5,4},{6,7},{7,6},{8,16},{9,17},{10,... | collective-permute-start | bytes 393224 | tf_op jit(solution)/shard_map/ppermute | solution.py:563

commit v3 on v2

--- a/solution.py
+++ b/solution.py
@@ -198,21 +198,17 @@
 
 def constants():
     interp, slopes, deriv, stiff, w, vec, lam, v = tables_1d()
-    eye2 = np.eye(2)
-    zx = lambda a, b: np.kron(a, np.kron(eye2, b))
     c = {}
     c["y_in"] = right_const(
         np.concatenate([block_diag(interp.T, 32), block_diag(slopes.T, 32)], axis=1)
     )
-    c["zx_in"] = np.concatenate(
-        hi_lo(np.concatenate([zx(interp, interp), zx(slopes, interp), zx(interp, slopes)], axis=0)),
-        axis=1,
+    c["zx_in"] = left_const(
+        np.concatenate(
+            [np.kron(interp, interp), np.kron(slopes, interp), np.kron(interp, slopes)], axis=0
+        )
     )
     test = v[:, None] * interp
-    back = zx(test.T, test.T).reshape(8, 16, 288)
-    pair = back[:, 7] + back[:, 8]
-    back[:, 7], back[:, 8] = pair, pair
-    c["zx_out"] = left_const(back.reshape(128, 288))
+    c["zx_out"] = left_const(np.kron(test.T, test.T))
     c["y_out"] = right_const(block_diag(test, 32))
     one, wm, wd = np.eye(8), np.diag(w), w[:, None] * deriv
     sides = (14, 15, 1, 0)
@@ -220,13 +216,14 @@
         c["xm_" + name] = left_const(local_rows([(one, xm)], sides))
         c["xe_" + name] = left_const(extended_rows([(one, xm)]))
     c["z_div"], c["z_st"] = left_const(z_rows((wd, wm))), left_const(z_rows((stiff, wm)))
-    c["join_div"], c["join_st"] = left_const(join_rows(wd, w)), left_const(join_rows(stiff, w))
     c["pick_div"], c["pick_st"] = face_coefs(wd), face_coefs(stiff)
     c["wd_y"] = right_const(block_diag(wd.T, 32))
     c["k_y"] = right_const(block_diag(stiff.T, 32))
     c["w_y"] = np.tile(w, 64)[None].astype(np.float32)
     into, back = box_rows(vec)
-    c["box_in"], c["box_out"] = left_const(into), left_const(back)
+    c["box_div"] = left_const(into @ join_rows(wd, w))
+    c["box_st"] = left_const(into @ join_rows(stiff, w))
+    c["box_out"] = left_const(back)
     into, back = box_lanes(vec, 64)
     c["ybox_in"], c["ybox_out"] = right_const(into), right_const(back)
     inv = 1.0 / (lam[:, None, None, None] + lam[None, None, :, None] + lam)
@@ -280,36 +277,45 @@
         copies[k].start()
     copies[2].wait()
     copies[0].wait()
-    v = v_ref[...].reshape(384, 512)
+    v = jnp.concatenate([v_ref[:, :, k : k + 8].reshape(192, 512) for k in (0, 8)], axis=0)
     parts = [rmul(v[:, cut], y_in[...]) for cut in (slice(0, 256), slice(256, 512))]
     value = jnp.concatenate([p[:, :384] for p in parts], axis=1)
     slope = jnp.concatenate([p[:, 384:] for p in parts], axis=1)
     for copy in (copies[1], *copies[3:]):
         copy.wait()
-    low = zx_in[...]
-    zx3 = jnp.concatenate([low[:, :128], low], axis=1)
-    u, gz, gx, gy = [], [], [], []
-    for c in range(3):
-        rows = slice(128 * c, 128 * c + 128)
-        most = lmul(zx3, value[rows])
-        u.append(most[:288])
-        gz.append(most[288:576])
-        gx.append(most[576:])
-        gy.append(lmul(zx3[:288], slope[rows]))
-    b = b_ref[...].reshape(128, 512)
+    b = jnp.concatenate([b_ref[:, k : k + 8].reshape(64, 512) for k in (0, 8)], axis=0)
     parts = [rmul(b[:, cut], y_in[:, :384]) for cut in (slice(0, 256), slice(256, 512))]
-    bq = lmul(zx3[:288], jnp.concatenate(parts, axis=1))
-    b2 = bq * bq
+    field = jnp.concatenate(parts, axis=1)
     back = []
-    for c in range(3):
-        conv = u[0] * gz[c] + u[1] * gx[c] + u[2] * gy[c]
-        if c != 1:
-            conv = conv + b2 * u[c]
-        back.append(lmul(zx_out[...], -conv))
+    for el in range(2):
+        u, gz, gx, gy = [], [], [], []
+        for c in range(3):
+            rows = slice(192 * el + 64 * c, 192 * el + 64 * c + 64)
+            most = lmul(zx_in[...], value[rows])
+            u.append(most[:144])
+            gz.append(most[144:288])
+            gx.append(most[288:])
+            gy.append(lmul(zx_in[:144], slope[rows]))
+        bq = lmul(zx_in[:144], field[64 * el : 64 * el + 64])
+        b2 = bq * bq
+        for c in range(3):
+            conv = u[0] * gz[c] + u[1] * gx[c] + u[2] * gy[c]
+            if c != 1:
+                conv = conv + b2 * u[c]
+            back.append(lmul(zx_out[...], -conv))
     back = jnp.concatenate(back, axis=0)
     halves = [rmul(back[:, cut], y_out[...]) for cut in (slice(0, 384), slice(384, 768))]
     f = dss_lanes(jnp.concatenate(halves, axis=1))
-    f_ref[...] = f
+    first, second = f[:192], f[192:]
+    node = lax.broadcasted_iota(jnp.int32, (192, 512), 0) % 8
+    both = (
+        first + jnp.where(node == 7, pltpu.roll(second, 7, 0), 0.0),
+        second + jnp.where(node == 0, pltpu.roll(first, 185, 0), 0.0),
+    )
+    for k in range(24):
+        for el in range(2):
+            f_ref[16 * k + 8 * el : 16 * k + 8 * el + 8] = both[el][8 * k : 8 * k + 8]
+    f = f_ref[...]
     s = lmul(xm_wd[...], f[128:256]) * w_y[...]
     s = s + rmul_halves(lmul(xm_w[...], f[256:]), wd_y[...])
     r_ref[:16] = s[:16]
@@ -434,9 +440,9 @@
     return lmul(const[...], jnp.concatenate(rows, axis=0))
 
 
-def box(s, box_in, ybox_in, inv, box_out, ybox_out):
+def box(t, ybox_in, inv, box_out, ybox_out):
     has_b, has_a, has_l, has_r = flags()
-    t = rmul(lmul(box_in[...], s), ybox_in[...]) * inv[...]
+    t = rmul(t, ybox_in[...]) * inv[...]
     g = rmul(lmul(box_out[...], t), ybox_out[...])
     row = lax.broadcasted_iota(jnp.int32, (128, 1), 0)
     z, x = row // 16, row % 16
@@ -446,11 +452,11 @@
 
 
 def first_kernel(*refs):
-    join_refs, box_refs, (xm_w, xm_k, k_y, w_y) = refs[:7], refs[7:12], refs[12:16]
-    s_ref, g_ref, r_ref, l_ref = refs[16:]
-    s = join(*join_refs)
-    s_ref[...] = s
-    g = box(s, *box_refs)
+    join_refs, box_refs, (xm_w, xm_k, k_y, w_y) = refs[:7], refs[7:11], refs[11:15]
+    t_ref, g_ref, r_ref, l_ref = refs[15:]
+    t = join(*join_refs)
+    t_ref[...] = t
+    g = box(t, *box_refs)
     g_ref[...] = g
     q = lmul(xm_k[...], g) * w_y[...] + rmul_halves(lmul(xm_w[...], g), k_y[...])
     r_ref[:16] = q[:16]
@@ -481,9 +487,9 @@
     send_faces(ends[1], u, p_ref, q_ref, *faces)
 
 
-def second_kernel(s_ref, *refs):
-    join_refs, box_refs, (g_ref, r_ref, l_ref) = refs[:7], refs[7:12], refs[12:]
-    g_ref[...] = box(s_ref[...] - join(*join_refs), *box_refs)
+def second_kernel(t_ref, *refs):
+    join_refs, box_refs, (g_ref, r_ref, l_ref) = refs[:7], refs[7:11], refs[11:]
+    g_ref[...] = box(t_ref[...] - join(*join_refs), *box_refs)
     r_ref[...] = edge(g_ref, 0, 15)
     l_ref[...] = edge(g_ref, 0, 0)
 
@@ -609,18 +615,18 @@
         hbm_out=(0,),
     )
     inner, outer, far = meet(up, down, inner, picks[0], "div_out")
-    box_consts = consts("box_in", "ybox_in", "inv", "box_out", "ybox_out")
-    s, g, right, left = call(
+    box_consts = consts("ybox_in", "inv", "box_out", "ybox_out")
+    spectral, g, right, left = call(
         first_kernel,
         "first_pass",
-        (192, 128, 32, 32),
+        (208, 128, 32, 32),
         u,
         up_face,
         down_face,
         inner,
         outer,
         far,
-        c["join_div"],
+        c["box_div"],
         *box_consts,
         *consts("xm_w", "xm_k", "k_y", "w_y"),
     )
@@ -640,14 +646,14 @@
         second_kernel,
         "second_pass",
         (128, 8, 8),
-        s,
+        spectral,
         u,
         up_face,
         down_face,
         inner,
         outer,
         far,
-        c["join_st"],
+        c["box_st"],
         *box_consts,
     )
     from_l, from_r = exchange_x(right, left)

time: 68.3 us -> 66.4 us (0.972)
  Pallas kernels: 16.1 us -> 14.2 us
    pallas_call x11, Pallas kernels: 16.1 us -> 14.2 us  [call(): pl.pallas_call(kernel, out_shape=[shape(o) for o in outs], in_specs=[spec...]
where the time goes in v3:
time: 66.4 us; the launch traced here: 65.6 us
  waiting for transfers between devices  29.7 us (45%)
  starting transfers between devices  20.5 us (31%)
  Pallas kernels  14.2 us (21%)
  between operations  1.08 us (2%)
    pallas_call x11, Pallas kernels, call(): pl.pallas_call(kernel, out_shape=[shape(o) for o in outs], in_specs=[spec...  14.2 us
    ppermute x3, starting transfers between devices, next_chip(): return lax.ppermute(x, ('wide', 'narrow'), pairs)  13.6 us
    ppermute x3, waiting for transfers between devices, next_chip(): return lax.ppermute(x, ('wide', 'narrow'), pairs)  10.3 us
    ppermute x3, waiting for transfers between devices, exchange_x(): lax.ppermute(leftward, 'narrow', left)  7.45 us
    ppermute x3, waiting for transfers between devices, exchange_x(): lax.ppermute(rightward, 'narrow', right)  6.87 us
    ppermute x5, waiting for transfers between devices, other_core(): return lax.ppermute(x, 'wide', [(i, i + 1 - 2 * (i % 2)) for i in range(n)])  5.06 us
    ppermute x3, starting transfers between devices, exchange_x(): lax.ppermute(rightward, 'narrow', right)  4.92 us
    ppermute x3, starting transfers between devices, exchange_x(): lax.ppermute(leftward, 'narrow', left)  1.37 us
  transfers between devices with their start and end apart: 14, of which 13 were waited for; matrix products, arithmetic and copies ran while one was open for 0% of the time, Pallas kernels for 0%

profile of v3, /device:TPU:6, one launch (start us, length us, event | category | flops | bytes accessed | tf_op | source)
XLA Modules:
  0.0 65.6 jit_solution(8610140807101991020)
XLA Ops:
  0.6 0.0 copy-start.4
  0.6 0.0 copy-start.6
  0.7 0.0 copy-start.10
  0.7 0.0 copy-start.12
  0.7 0.0 copy-start.14
  0.7 0.0 copy-start.1
  0.7 0.0 copy-start.7
  0.7 7.0 %force.1 = (f32[384,512]{1,0:T(8,128)S(1)}, f32[48,512]{1,0:T(8,128)S(1)}, f32[48,512]{1,0:T(8,128)S(1)}) custom-call(f32[3,8,16,512]{3,2,1,0:T(8,128)} %refs_0_.1, f32[8,16,512]{2,1,0:T(8,128)} %refs_1_.1, bf16[512,768]{1,0:T(8,128)(2,1)} %constant.42.clone.refs_2_, bf16[432,192]{1,0:T(8,128)(2,1)} %constant.43.clone.refs_3_, ...), custom_call_target="tpu_custom_call" | custom-call | tf_op jit(solution)/shard_map/force/pallas_call | solution.py:537
  7.7 0.0 copy-start
  7.8 0.0 copy-start.2
  7.8 0.0 copy-start.3
  7.8 0.0 copy-start.5
  7.8 0.0 copy-start.13
  7.8 0.0 copy-start.15
  7.8 1.9 %collective-permute-start = (f32[48,512]{1,0:T(8,128)S(1)}, f32[48,512]{1,0:T(8,128)S(1)}, u32[]{:S(2)}, u32[]{:S(2)}) collective-permute-start(f32[48,512]{1,0:T(8,128)S(1)} %get-tuple-element.34), channel_id=1, source_target_pairs={{0,1},{1,2},{2,3},{3,4},{4,5},{5,6},{6,7},{7,0},{8,9},{9,10},{10,1... | collective-permute-start | bytes 294920 | tf_op jit(solution)/shard_map/ppermute | solution.py:553
  9.7 0.2 collective-permute-start.1
  9.9 2.9 %collective-permute-done.ml_ref = f32[48,512]{1,0:T(8,128)S(1)} collective-permute-done((f32[48,512]{1,0:T(8,128)S(1)}, f32[48,512]{1,0:T(8,128)S(1)}, u32[]{:S(2)}, u32[]{:S(2)}) %collective-permute-start) | collective-permute-done | bytes 98336 | tf_op jit(solution)/shard_map/ppermute | solution.py:553
  12.8 2.8 %collective-permute-done.1.mr_ref = f32[48,512]{1,0:T(8,128)S(1)} collective-permute-done((f32[48,512]{1,0:T(8,128)S(1)}, f32[48,512]{1,0:T(8,128)S(1)}, u32[]{:S(2)}, u32[]{:S(2)}) %collective-permute-start.1) | collective-permute-done | bytes 98336 | tf_op jit(solution)/shard_map/ppermute | solution.py:553
  15.6 0.0 copy-done.4
  15.6 0.0 copy-done.6
  15.6 0.0 copy-done.10
  15.6 0.0 copy-done.12
  15.6 0.0 copy-done.14
  15.7 1.5 %div.1 = (f32[384,512]{1,0:T(8,128)}, f32[48,512]{1,0:T(8,128)S(1)}, f32[48,512]{1,0:T(8,128)S(1)}, f32[144,512]{1,0:T(8,128)S(1)}, f32[56,512]{1,0:T(8,128)S(1)...) custom-call(f32[384,512]{1,0:T(8,128)S(1)} %get-tuple-element.33.f_ref, ...), custom_call_target="tpu_custom_call" | custom-call | tf_op jit(solution)/shard_map/div/pallas_call | solution.py:537
  17.1 0.1 collective-permute-start.2
  17.2 1.3 %collective-permute-done.2.in_ref.refs_3_ = f32[56,512]{1,0:T(8,128)S(1)} collective-permute-done((f32[56,512]{1,0:T(8,128)S(1)}, f32[56,512]{1,0:T(8,128)S(1)}, u32[]{:S(2)}, u32[]{:S(2)}) %collective-permute-start.2) | collective-permute-done | bytes 114720 | tf_op jit(solution)/shard_map/ppermute | solution.py:558
  18.6 4.7 %collective-permute-start.3 = (f32[56,512]{1,0:T(8,128)S(1)}, f32[56,512]{1,0:T(8,128)S(1)}, u32[]{:S(2)}, u32[]{:S(2)}) collective-permute-start(f32[56,512]{1,0:T(8,128)S(1)} %div_out.1), channel_id=1, source_target_pairs={{0,1},{1,0},{2,3},{3,2},{4,5},{5,4},{6,7},{7,6},{8,16},{9,17},{10,... | collective-permute-start | bytes 344072 | tf_op jit(solution)/shard_map/ppermute | solution.py:569
  23.3 3.2 %collective-permute-done.3.out_msg_ref.refs_4_ = f32[56,512]{1,0:T(8,128)S(1)} collective-permute-done((f32[56,512]{1,0:T(8,128)S(1)}, f32[56,512]{1,0:T(8,128)S(1)}, u32[]{:S(2)}, u32[]{:S(2)}) %collective-permute-start.3) | collective-permute-done | bytes 114720 | tf_op jit(solution)/shard_map/ppermute | solution.py:569
  26.5 0.1 collective-permute-start.4
  26.6 1.2 %collective-permute-done.4.refs_5_ = f32[24,512]{1,0:T(8,128)S(1)} collective-permute-done((f32[24,512]{1,0:T(8,128)S(1)}, f32[24,512]{1,0:T(8,128)S(1)}, u32[]{:S(2)}, u32[]{:S(2)}) %collective-permute-start.4) | collective-permute-done | bytes 49184 | tf_op jit(solution)/shard_map/ppermute | solution.py:558
  27.8 0.0 copy-done.1
  27.8 0.0 copy-done
  27.8 0.0 copy-done.2
  27.8 0.0 copy-done.3
  27.8 0.0 copy-done.5
  27.8 0.0 copy-done.13
  27.8 0.0 copy-done.15
  27.9 0.0 copy-start.9
  27.9 0.0 copy-start.11
  27.9 2.1 %first_pass.1 = (f32[208,512]{1,0:T(8,128)S(1)}, f32[128,512]{1,0:T(8,128)S(1)}, f32[32,512]{1,0:T(8,128)S(1)}, f32[32,512]{1,0:T(8,128)S(1)}) custom-call(f32[144,512]{1,0:T(8,128)S(1)} %get-tuple-element.36.refs_0_, f32[40,512]{1,0:T(8,128)S(1)} %get-tuple-element.37.refs_1_, f32[40,512]{1,0:T(8,128)S(1)} %get-tuple-element.38.refs_2_, ...), custom_call_target="tpu_custom_call" | custom-call | tf_op jit(solution)/shard_map/first_pass/pallas_call | solution.py:537
  30.0 0.0 copy-start.8
  30.0 1.8 %collective-permute-start.5 = (f32[32,512]{1,0:T(8,128)S(1)}, f32[32,512]{1,0:T(8,128)S(1)}, u32[]{:S(2)}, u32[]{:S(2)}) collective-permute-start(f32[32,512]{1,0:T(8,128)S(1)} %get-tuple-element.44), channel_id=1, source_target_pairs={{0,1},{1,2},{2,3},{3,4},{4,5},{5,6},{6,7},{7,0},{8,9},{9,10},{10,1... | collective-permute-start | bytes 196616 | tf_op jit(solution)/shard_map/ppermute | solution.py:553
  31.8 0.3 collective-permute-start.6
  32.1 2.2 %collective-permute-done.5.ml_ref = f32[32,512]{1,0:T(8,128)S(1)} collective-permute-done((f32[32,512]{1,0:T(8,128)S(1)}, f32[32,512]{1,0:T(8,128)S(1)}, u32[]{:S(2)}, u32[]{:S(2)}) %collective-permute-start.5) | collective-permute-done | bytes 65568 | tf_op jit(solution)/shard_map/ppermute | solution.py:553
  34.3 2.7 %collective-permute-done.6.mr_ref = f32[32,512]{1,0:T(8,128)S(1)} collective-permute-done((f32[32,512]{1,0:T(8,128)S(1)}, f32[32,512]{1,0:T(8,128)S(1)}, u32[]{:S(2)}, u32[]{:S(2)}) %collective-permute-start.6) | collective-permute-done | bytes 65568 | tf_op jit(solution)/shard_map/ppermute | solution.py:553
  37.0 0.0 copy-done.9
  37.0 1.1 %stiff.1 = (f32[128,512]{1,0:T(8,128)S(1)}, f32[144,512]{1,0:T(8,128)S(1)}, f32[56,512]{1,0:T(8,128)S(1)}, f32[56,512]{1,0:T(8,128)S(1)}, f32[40,512]{1,0:T(8,12...) custom-call(f32[128,512]{1,0:T(8,128)S(1)} %get-tuple-element.43.g_ref, ...), custom_call_target="tpu_custom_call" | custom-call | tf_op jit(solution)/shard_map/stiff/pallas_call | solution.py:537
  38.0 0.1 collective-permute-start.7
  38.1 1.3 %collective-permute-done.7.in_ref.refs_3_ = f32[56,512]{1,0:T(8,128)S(1)} collective-permute-done((f32[56,512]{1,0:T(8,128)S(1)}, f32[56,512]{1,0:T(8,128)S(1)}, u32[]{:S(2)}, u32[]{:S(2)}) %collective-permute-start.7) | collective-permute-done | bytes 114720 | tf_op jit(solution)/shard_map/ppermute | solution.py:558
  39.5 4.4 %collective-permute-start.8 = (f32[56,512]{1,0:T(8,128)S(1)}, f32[56,512]{1,0:T(8,128)S(1)}, u32[]{:S(2)}, u32[]{:S(2)}) collective-permute-start(f32[56,512]{1,0:T(8,128)S(1)} %stiff_out.1), channel_id=1, source_target_pairs={{0,1},{1,0},{2,3},{3,2},{4,5},{5,4},{6,7},{7,6},{8,16},{9,17},{10,... | collective-permute-start | bytes 344072 | tf_op jit(solution)/shard_map/ppermute | solution.py:569
  43.8 3.6 %collective-permute-done.8.out_msg_ref.refs_4_ = f32[56,512]{1,0:T(8,128)S(1)} collective-permute-done((f32[56,512]{1,0:T(8,128)S(1)}, f32[56,512]{1,0:T(8,128)S(1)}, u32[]{:S(2)}, u32[]{:S(2)}) %collective-permute-start.8) | collective-permute-done | bytes 114720 | tf_op jit(solution)/shard_map/ppermute | solution.py:569
  47.4 0.3 collective-permute-start.9
  47.7 1.2 %collective-permute-done.9.refs_5_ = f32[24,512]{1,0:T(8,128)S(1)} collective-permute-done((f32[24,512]{1,0:T(8,128)S(1)}, f32[24,512]{1,0:T(8,128)S(1)}, u32[]{:S(2)}, u32[]{:S(2)}) %collective-permute-start.9) | collective-permute-done | bytes 49184 | tf_op jit(solution)/shard_map/ppermute | solution.py:558
  48.9 1.6 %second_pass.1 = (f32[128,512]{1,0:T(8,128)S(1)}, f32[8,512]{1,0:T(8,128)S(1)}, f32[8,512]{1,0:T(8,128)S(1)}) custom-call(f32[208,512]{1,0:T(8,128)S(1)} %get-tuple-element.42.t_ref, f32[144,512]{1,0:T(8,128)S(1)} %get-tuple-element.46.refs_0_, f32[40,512]{1,0:T(8,128)S(1)} %get-tuple-element.47.refs_1_, f32[40,512]{1,0:T(8,128)S(1)} %get-tuple-element.48.refs_2_, ...), custom_call_target="tpu_custom_call" | custom-call | tf_op jit(solution)/shard_map/second_pass/pallas_call | solution.py:537
  50.5 1.2 %collective-permute-start.10 = (f32[8,512]{1,0:T(8,128)S(1)}, f32[8,512]{1,0:T(8,128)S(1)}, u32[]{:S(2)}, u32[]{:S(2)}) collective-permute-start(f32[8,512]{1,0:T(8,128)S(1)} %get-tuple-element.54), channel_id=1, source_target_pairs={{0,1},{1,2},{2,3},{3,4},{4,5},{5,6},{6,7},{7,0},{8,9},{9,10},{10,1... | collective-permute-start | bytes 49160 | tf_op jit(solution)/shard_map/ppermute | solution.py:553
  51.7 0.9 %collective-permute-start.11 = (f32[8,512]{1,0:T(8,128)S(1)}, f32[8,512]{1,0:T(8,128)S(1)}, u32[]{:S(2)}, u32[]{:S(2)}) collective-permute-start(f32[8,512]{1,0:T(8,128)S(1)} %get-tuple-element.55), channel_id=1, source_target_pairs={{1,0},{2,1},{3,2},{4,3},{5,4},{6,5},{7,6},{0,7},{9,8},{10,9},{11,1... | collective-permute-start | bytes 49160 | tf_op jit(solution)/shard_map/ppermute | solution.py:553
  52.6 1.7 %collective-permute-done.10.ml_ref = f32[8,512]{1,0:T(8,128)S(1)} collective-permute-done((f32[8,512]{1,0:T(8,128)S(1)}, f32[8,512]{1,0:T(8,128)S(1)}, u32[]{:S(2)}, u32[]{:S(2)}) %collective-permute-start.10) | collective-permute-done | bytes 16416 | tf_op jit(solution)/shard_map/ppermute | solution.py:553
  54.3 2.0 %collective-permute-done.11.mr_ref = f32[8,512]{1,0:T(8,128)S(1)} collective-permute-done((f32[8,512]{1,0:T(8,128)S(1)}, f32[8,512]{1,0:T(8,128)S(1)}, u32[]{:S(2)}, u32[]{:S(2)}) %collective-permute-start.11) | collective-permute-done | bytes 16416 | tf_op jit(solution)/shard_map/ppermute | solution.py:553
  56.3 0.1 last_x.1
  56.4 0.1 collective-permute-start.12
  56.5 4.5 %collective-permute-start.13 = (f32[64,512]{1,0:T(8,128)S(1)}, f32[64,512]{1,0:T(8,128)S(1)}, u32[]{:S(2)}, u32[]{:S(2)}) collective-permute-start(f32[64,512]{1,0:T(8,128)S(1)} %get-tuple-element.60), channel_id=1, source_target_pairs={{0,1},{1,0},{2,3},{3,2},{4,5},{5,4},{6,7},{7,6},{8,16},{9,17},{10,... | collective-permute-start | bytes 393224 | tf_op jit(solution)/shard_map/ppermute | solution.py:569
  61.0 0.0 collective-permute-done.12.in_ref
  61.0 3.6 %collective-permute-done.13.out_msg_ref = f32[64,512]{1,0:T(8,128)S(1)} collective-permute-done((f32[64,512]{1,0:T(8,128)S(1)}, f32[64,512]{1,0:T(8,128)S(1)}, u32[]{:S(2)}, u32[]{:S(2)}) %collective-permute-start.13) | collective-permute-done | bytes 131104 | tf_op jit(solution)/shard_map/ppermute | solution.py:569
  64.6 0.9 %last_z.1 = (f32[128,512]{1,0:T(8,128)}, f32[384,512]{1,0:T(8,128)}) custom-call(f32[128,512]{1,0:T(8,128)S(1)} %get-tuple-element.58.g_ref, f32[48,512]{1,0:T(8,128)S(1)} %get-tuple-element.56.f_up, f32[48,512]{1,0:T(8,128)S(1)} %get-tuple-element.57.f_down, f32[64,512]{1,0:T(8,128)S(1)} %collective-permute-done.12.in_ref, ...), custom_call_target="tpu_custom_call", output_to_operand_aliasing={{1}: (5, {})} | custom-call | tf_op jit(solution)/shard_map/last_z/pallas_call | solution.py:537
  (7 shorter events, 0.1 us)
Async XLA Ops:
  0.6 15.0 %copy-start.4 = (bf16[512,256]{1,0:T(8,128)(2,1)S(1)}, bf16[512,256]{1,0:T(8,128)(2,1)}, u32[]{:S(2)}) copy-start(bf16[512,256]{1,0:T(8,128)(2,1)} %constant.54.clone.refs_8_.wd_y) | copy-start | bytes 786436
  0.6 15.0 %copy-start.6 = (bf16[144,432]{1,0:T(8,128)(2,1)S(1)}, bf16[144,432]{1,0:T(8,128)(2,1)}, u32[]{:S(2)}) copy-start(bf16[144,432]{1,0:T(8,128)(2,1)} %constant.47.clone.xe_w) | copy-start | bytes 373252
  0.7 15.0 %copy-start.10 = (bf16[144,864]{1,0:T(8,128)(2,1)S(1)}, bf16[144,864]{1,0:T(8,128)(2,1)}, u32[]{:S(2)}) copy-start(bf16[144,864]{1,0:T(8,128)(2,1)} %constant.52.clone.z_div) | copy-start | bytes 746500
  0.7 15.0 %copy-start.12 = (bf16[144,432]{1,0:T(8,128)(2,1)S(1)}, bf16[144,432]{1,0:T(8,128)(2,1)}, u32[]{:S(2)}) copy-start(bf16[144,432]{1,0:T(8,128)(2,1)} %constant.49.clone.xe_wd) | copy-start | bytes 373252
  0.7 15.0 %copy-start.14 = (f32[1,512]{1,0:T(1,128)S(1)}, f32[1,512]{1,0:T(1,128)}, u32[]{:S(2)}) copy-start(f32[1,512]{1,0:T(1,128)} %constant.56.clone.refs_9_.w_y.refs_14_) | copy-start | bytes 6148
  0.7 27.1 %copy-start.1 = (bf16[1024,640]{1,0:T(8,128)(2,1)S(1)}, bf16[1024,640]{1,0:T(8,128)(2,1)}, u32[]{:S(2)}) copy-start(bf16[1024,640]{1,0:T(8,128)(2,1)} %constant.60.clone.refs_7_) | copy-start | bytes 3932164
  0.7 27.1 %copy-start.7 = (bf16[208,1152]{1,0:T(8,128)(2,1)S(1)}, bf16[208,1152]{1,0:T(8,128)(2,1)}, u32[]{:S(2)}) copy-start(bf16[208,1152]{1,0:T(8,128)(2,1)} %constant.57.clone.refs_6_) | copy-start | bytes 1437700
  7.7 20.1 %copy-start = (bf16[1280,512]{1,0:T(8,128)(2,1)S(1)}, bf16[1280,512]{1,0:T(8,128)(2,1)}, u32[]{:S(2)}) copy-start(bf16[1280,512]{1,0:T(8,128)(2,1)} %constant.61.clone.refs_10_) | copy-start | bytes 3932164
  7.8 20.1 %copy-start.2 = (f32[208,640]{1,0:T(8,128)S(1)}, f32[208,640]{1,0:T(8,128)}, u32[]{:S(2)}) copy-start(f32[208,640]{1,0:T(8,128)} %constant.62.clone.refs_8_) | copy-start | bytes 1597444
  7.8 20.0 %copy-start.3 = (bf16[512,256]{1,0:T(8,128)(2,1)S(1)}, bf16[512,256]{1,0:T(8,128)(2,1)}, u32[]{:S(2)}) copy-start(bf16[512,256]{1,0:T(8,128)(2,1)} %constant.55.clone.refs_13_.k_y) | copy-start | bytes 786436
  7.8 20.0 %copy-start.5 = (bf16[128,624]{1,0:T(8,128)(2,1)S(1)}, bf16[128,624]{1,0:T(8,128)(2,1)}, u32[]{:S(2)}) copy-start(bf16[128,624]{1,0:T(8,128)(2,1)} %constant.59.clone.refs_9_) | copy-start | bytes 479236
  7.8 20.0 %copy-start.13 = (bf16[32,384]{1,0:T(8,128)(2,1)S(1)}, bf16[32,384]{1,0:T(8,128)(2,1)}, u32[]{:S(2)}) copy-start(bf16[32,384]{1,0:T(8,128)(2,1)} %constant.46.clone.refs_6_.refs_11_) | copy-start | bytes 73732
  7.8 20.0 %copy-start.15 = (bf16[32,384]{1,0:T(8,128)(2,1)S(1)}, bf16[32,384]{1,0:T(8,128)(2,1)}, u32[]{:S(2)}) copy-start(bf16[32,384]{1,0:T(8,128)(2,1)} %constant.50.clone.refs_12_) | copy-start | bytes 73732
  7.8 5.0 %collective-permute-start = (f32[48,512]{1,0:T(8,128)S(1)}, f32[48,512]{1,0:T(8,128)S(1)}, u32[]{:S(2)}, u32[]{:S(2)}) collective-permute-start(f32[48,512]{1,0:T(8,128)S(1)} %get-tuple-element.34), channel_id=1, source_target_pairs={{0,1},{1,2},{2,3},{3,4},{4,5},{5,6},{6,7},{7,0},{8,9},{9,10},{10,1... | collective-permute-start | bytes 294920 | tf_op jit(solution)/shard_map/ppermute | solution.py:553
  9.7 5.9 %collective-permute-start.1 = (f32[48,512]{1,0:T(8,128)S(1)}, f32[48,512]{1,0:T(8,128)S(1)}, u32[]{:S(2)}, u32[]{:S(2)}) collective-permute-start(f32[48,512]{1,0:T(8,128)S(1)} %get-tuple-element.35), channel_id=1, source_target_pairs={{1,0},{2,1},{3,2},{4,3},{5,4},{6,5},{7,6},{0,7},{9,8},{10,9},{11,1... | collective-permute-start | bytes 294920 | tf_op jit(solution)/shard_map/ppermute | solution.py:553
  17.1 1.4 %collective-permute-start.2 = (f32[56,512]{1,0:T(8,128)S(1)}, f32[56,512]{1,0:T(8,128)S(1)}, u32[]{:S(2)}, u32[]{:S(2)}) collective-permute-start(f32[56,512]{1,0:T(8,128)S(1)} %get-tuple-element.39), channel_id=1, source_target_pairs={{0,8},{8,0},{16,24},{24,16},{32,40},{40,32},{48,56},{56,48},{64,72... | collective-permute-start | bytes 344072 | tf_op jit(solution)/shard_map/ppermute | solution.py:558
  18.6 7.9 %collective-permute-start.3 = (f32[56,512]{1,0:T(8,128)S(1)}, f32[56,512]{1,0:T(8,128)S(1)}, u32[]{:S(2)}, u32[]{:S(2)}) collective-permute-start(f32[56,512]{1,0:T(8,128)S(1)} %div_out.1), channel_id=1, source_target_pairs={{0,1},{1,0},{2,3},{3,2},{4,5},{5,4},{6,7},{7,6},{8,16},{9,17},{10,... | collective-permute-start | bytes 344072 | tf_op jit(solution)/shard_map/ppermute | solution.py:569
  26.5 1.3 %collective-permute-start.4 = (f32[24,512]{1,0:T(8,128)S(1)}, f32[24,512]{1,0:T(8,128)S(1)}, u32[]{:S(2)}, u32[]{:S(2)}) collective-permute-start(f32[24,512]{1,0:T(8,128)S(1)} %div_out_far.1), channel_id=1, source_target_pairs={{0,8},{8,0},{16,24},{24,16},{32,40},{40,32},{48,56},{56,48},{64,72... | collective-permute-start | bytes 147464 | tf_op jit(solution)/shard_map/ppermute | solution.py:558
  27.9 9.1 %copy-start.9 = (bf16[144,864]{1,0:T(8,128)(2,1)S(1)}, bf16[144,864]{1,0:T(8,128)(2,1)}, u32[]{:S(2)}) copy-start(bf16[144,864]{1,0:T(8,128)(2,1)} %constant.53.clone.z_st) | copy-start | bytes 746500
  27.9 9.1 %copy-start.11 = (bf16[144,432]{1,0:T(8,128)(2,1)S(1)}, bf16[144,432]{1,0:T(8,128)(2,1)}, u32[]{:S(2)}) copy-start(bf16[144,432]{1,0:T(8,128)(2,1)} %constant.51.clone.xe_k) | copy-start | bytes 373252
  30.0 18.9 %copy-start.8 = (bf16[208,1152]{1,0:T(8,128)(2,1)S(1)}, bf16[208,1152]{1,0:T(8,128)(2,1)}, u32[]{:S(2)}) copy-start(bf16[208,1152]{1,0:T(8,128)(2,1)} %constant.58.clone.refs_6_) | copy-start | bytes 1437700
  30.0 4.3 %collective-permute-start.5 = (f32[32,512]{1,0:T(8,128)S(1)}, f32[32,512]{1,0:T(8,128)S(1)}, u32[]{:S(2)}, u32[]{:S(2)}) collective-permute-start(f32[32,512]{1,0:T(8,128)S(1)} %get-tuple-element.44), channel_id=1, source_target_pairs={{0,1},{1,2},{2,3},{3,4},{4,5},{5,6},{6,7},{7,0},{8,9},{9,10},{10,1... | collective-permute-start | bytes 196616 | tf_op jit(solution)/shard_map/ppermute | solution.py:553
  31.8 5.2 %collective-permute-start.6 = (f32[32,512]{1,0:T(8,128)S(1)}, f32[32,512]{1,0:T(8,128)S(1)}, u32[]{:S(2)}, u32[]{:S(2)}) collective-permute-start(f32[32,512]{1,0:T(8,128)S(1)} %get-tuple-element.45), channel_id=1, source_target_pairs={{1,0},{2,1},{3,2},{4,3},{5,4},{6,5},{7,6},{0,7},{9,8},{10,9},{11,1... | collective-permute-start | bytes 196616 | tf_op jit(solution)/shard_map/ppermute | solution.py:553
  38.0 1.4 %collective-permute-start.7 = (f32[56,512]{1,0:T(8,128)S(1)}, f32[56,512]{1,0:T(8,128)S(1)}, u32[]{:S(2)}, u32[]{:S(2)}) collective-permute-start(f32[56,512]{1,0:T(8,128)S(1)} %get-tuple-element.49), channel_id=1, source_target_pairs={{0,8},{8,0},{16,24},{24,16},{32,40},{40,32},{48,56},{56,48},{64,72... | collective-permute-start | bytes 344072 | tf_op jit(solution)/shard_map/ppermute | solution.py:558
  39.5 7.9 %collective-permute-start.8 = (f32[56,512]{1,0:T(8,128)S(1)}, f32[56,512]{1,0:T(8,128)S(1)}, u32[]{:S(2)}, u32[]{:S(2)}) collective-permute-start(f32[56,512]{1,0:T(8,128)S(1)} %stiff_out.1), channel_id=1, source_target_pairs={{0,1},{1,0},{2,3},{3,2},{4,5},{5,4},{6,7},{7,6},{8,16},{9,17},{10,... | collective-permute-start | bytes 344072 | tf_op jit(solution)/shard_map/ppermute | solution.py:569
  47.4 1.5 %collective-permute-start.9 = (f32[24,512]{1,0:T(8,128)S(1)}, f32[24,512]{1,0:T(8,128)S(1)}, u32[]{:S(2)}, u32[]{:S(2)}) collective-permute-start(f32[24,512]{1,0:T(8,128)S(1)} %stiff_out_far.1), channel_id=1, source_target_pairs={{0,8},{8,0},{16,24},{24,16},{32,40},{40,32},{48,56},{56,48},{64,72... | collective-permute-start | bytes 147464 | tf_op jit(solution)/shard_map/ppermute | solution.py:558
  50.5 3.8 %collective-permute-start.10 = (f32[8,512]{1,0:T(8,128)S(1)}, f32[8,512]{1,0:T(8,128)S(1)}, u32[]{:S(2)}, u32[]{:S(2)}) collective-permute-start(f32[8,512]{1,0:T(8,128)S(1)} %get-tuple-element.54), channel_id=1, source_target_pairs={{0,1},{1,2},{2,3},{3,4},{4,5},{5,6},{6,7},{7,0},{8,9},{9,10},{10,1... | collective-permute-start | bytes 49160 | tf_op jit(solution)/shard_map/ppermute | solution.py:553
  51.7 4.6 %collective-permute-start.11 = (f32[8,512]{1,0:T(8,128)S(1)}, f32[8,512]{1,0:T(8,128)S(1)}, u32[]{:S(2)}, u32[]{:S(2)}) collective-permute-start(f32[8,512]{1,0:T(8,128)S(1)} %get-tuple-element.55), channel_id=1, source_target_pairs={{1,0},{2,1},{3,2},{4,3},{5,4},{6,5},{7,6},{0,7},{9,8},{10,9},{11,1... | collective-permute-start | bytes 49160 | tf_op jit(solution)/shard_map/ppermute | solution.py:553
  56.4 4.6 %collective-permute-start.12 = (f32[64,512]{1,0:T(8,128)S(1)}, f32[64,512]{1,0:T(8,128)S(1)}, u32[]{:S(2)}, u32[]{:S(2)}) collective-permute-start(f32[64,512]{1,0:T(8,128)S(1)} %get-tuple-element.59), channel_id=1, source_target_pairs={{0,8},{8,0},{16,24},{24,16},{32,40},{40,32},{48,56},{56,48},{64,72... | collective-permute-start | bytes 393224 | tf_op jit(solution)/shard_map/ppermute | solution.py:558
  56.5 8.1 %collective-permute-start.13 = (f32[64,512]{1,0:T(8,128)S(1)}, f32[64,512]{1,0:T(8,128)S(1)}, u32[]{:S(2)}, u32[]{:S(2)}) collective-permute-start(f32[64,512]{1,0:T(8,128)S(1)} %get-tuple-element.60), channel_id=1, source_target_pairs={{0,1},{1,0},{2,3},{3,2},{4,5},{5,4},{6,7},{7,6},{8,16},{9,17},{10,... | collective-permute-start | bytes 393224 | tf_op jit(solution)/shard_map/ppermute | solution.py:569

commit v4 on v3

--- a/solution.py
+++ b/solution.py
@@ -415,6 +415,11 @@
     out_ref[48:52] += jnp.concatenate([ca * far_l, cb * far_l, ca * far_r, cb * far_r], axis=0)
 
 
+def outer_force_kernel(coefs, f_up, f_down, up_ref, down_ref, in_ref, out_ref, f_out_ref):
+    outer_kernel(coefs, up_ref, down_ref, in_ref, out_ref)
+    f_out_ref[...] = jnp.where(is_odd(), f_up[...], f_down[...])
+
+
 def far_kernel(out_msg_ref, far_ref):
     has_b, has_a, _, _ = flags()
     flag = jnp.where(is_odd(), has_a, has_b)
@@ -452,12 +457,15 @@
 
 
 def first_kernel(*refs):
-    join_refs, box_refs, (xm_w, xm_k, k_y, w_y) = refs[:7], refs[7:11], refs[11:15]
-    t_ref, g_ref, r_ref, l_ref = refs[15:]
-    t = join(*join_refs)
+    t_ref, g_ref = refs[11:]
+    t = join(*refs[:7])
     t_ref[...] = t
-    g = box(t, *box_refs)
-    g_ref[...] = g
+    g_ref[...] = box(t, *refs[7:11])
+
+
+def stiff_msg_kernel(g_ref, xm_w, xm_k, k_y, w_y, *refs):
+    r_ref, l_ref = refs[-2:]
+    g = g_ref[...]
     q = lmul(xm_k[...], g) * w_y[...] + rmul_halves(lmul(xm_w[...], g), k_y[...])
     r_ref[:16] = q[:16]
     l_ref[:16] = q[16:]
@@ -500,18 +508,19 @@
     add_edge(out_ref, 0, 0, ml_ref[...] * has_l)
     add_edge(out_ref, 0, 15, mr_ref[...] * has_r)
     odd = is_odd()
-    for rows, up, down in (
-        (slice(0, 16), out_ref[112:], out_ref[:16]),
-        (slice(16, 64), f_up[...], f_down[...]),
-    ):
-        in_msg_ref[rows] = jnp.where(odd, down, up)
-        out_msg_ref[rows] = jnp.where(odd, up, down)
-
-
-def last_z_kernel(g_ref, f_up, f_down, in_ref, out_msg_ref, _, out_ref, force_ref, face_ref, p_ref, sem):
+    up, down = out_ref[112:], out_ref[:16]
+    out_msg_ref[...] = jnp.where(odd, up, down)
+    in_msg_ref[:16] = jnp.where(odd, down, up)
+    in_msg_ref[16:] = jnp.where(odd, f_down[...], f_up[...])
+
+
+def last_z_kernel(
+    out_msg_ref, in_ref, f_out_ref, g_ref, f_up, f_down, _, out_ref, force_ref, face_ref, p_ref, sem
+):
     has_b, has_a, _, _ = flags()
     odd = is_odd()
-    inner, outer = in_ref[...], out_msg_ref[...] * jnp.where(odd, has_a, has_b)
+    inner, flag = in_ref[...], jnp.where(odd, has_a, has_b)
+    outer = jnp.concatenate([out_msg_ref[...], f_out_ref[...]], axis=0) * flag
     below, above = jnp.where(odd, inner, outer), jnp.where(odd, outer, inner)
     p_ref[...] = g_ref[...]
     p_ref[:16] += below[:16]
@@ -569,13 +578,14 @@
     return lax.ppermute(x, ("wide", "narrow"), pairs)
 
 
-def meet(up, down, inner_msg, coefs, name):
+def meet(up, down, inner_msg, coefs, name, force_faces=()):
     inner = other_core(inner_msg)
     coefs = [[float(t) for t in row] for row in coefs]
-    (msg,) = call(functools.partial(outer_kernel, coefs), name, (56,), up, down, inner)
-    outer = next_chip(msg)
+    kernel, outs = (outer_force_kernel, (56, 48)) if force_faces else (outer_kernel, (56,))
+    msgs = call(functools.partial(kernel, coefs), name, outs, *force_faces, up, down, inner)
+    outer = next_chip(msgs[0])
     (far,) = call(far_kernel, name + "_far", (24,), outer)
-    return inner, outer, other_core(far)
+    return inner, outer, other_core(far), *map(next_chip, msgs[1:])
 
 
 def shards(velocity, bfield):
@@ -614,12 +624,12 @@
         sems=1,
         hbm_out=(0,),
     )
-    inner, outer, far = meet(up, down, inner, picks[0], "div_out")
+    inner, outer, far, f_out = meet(up, down, inner, picks[0], "div_out", (f_up, f_down))
     box_consts = consts("ybox_in", "inv", "box_out", "ybox_out")
-    spectral, g, right, left = call(
+    spectral, g = call(
         first_kernel,
         "first_pass",
-        (208, 128, 32, 32),
+        (208, 128),
         u,
         up_face,
         down_face,
@@ -628,8 +638,9 @@
         far,
         c["box_div"],
         *box_consts,
-        *consts("xm_w", "xm_k", "k_y", "w_y"),
-    )
+    )
+    msg_consts = consts("xm_w", "xm_k", "k_y", "w_y")
+    right, left = call(stiff_msg_kernel, "stiff_msg", (32, 32), g, *msg_consts, f_out)
     from_l, from_r = exchange_x(right, left)
     gx, u, up, down, up_face, down_face, inner = call(
         functools.partial(stiff_kernel, ends),
@@ -658,24 +669,25 @@
     )
     from_l, from_r = exchange_x(right, left)
     total, inner, outer = call(
-        last_x_kernel, "last_x", (128, 64, 64), g, gx, from_l, from_r, f_up, f_down
+        last_x_kernel, "last_x", (128, 64, 16), g, gx, from_l, from_r, f_up, f_down
     )
     outer, inner = next_chip(outer), other_core(inner)
     pressure, force = call(
         last_z_kernel,
         "last_z",
         (128, 384),
+        outer,
+        inner,
+        f_out,
         total,
         f_up,
         f_down,
-        inner,
-        outer,
         force,
         scratch=(96, 128),
         sems=7,
-        hbm_in=(5,),
+        hbm_in=(6,),
         hbm_out=(0, 1),
-        alias={5: 1},
+        alias={6: 1},
     )
     return force.reshape(3, 8, 16, 512), pressure.reshape(8, 16, 512)
 

time: 66.4 us -> 65.4 us (0.985)
    ppermute x3, waiting for transfers between devices: 7.45 us -> 6.35 us  [exchange_x(): lax.ppermute(leftward, 'narrow', left)]
    ppermute x3, starting transfers between devices: 4.92 us -> 4.19 us  [exchange_x(): lax.ppermute(rightward, 'narrow', right)]
    ppermute x3, starting transfers between devices: 1.37 us -> 2.09 us  [exchange_x(): lax.ppermute(leftward, 'narrow', left)]
    ppermute x3 -> x4, waiting for transfers between devices: 10.3 us -> 11 us  [next_chip(): return lax.ppermute(x, ('wide', 'narrow'), pairs)]
    ppermute x3 -> x4, starting transfers between devices: 13.6 us -> 13.2 us  [next_chip(): return lax.ppermute(x, ('wide', 'narrow'), pairs)]
    pallas_call x11 -> x12, Pallas kernels: 14.2 us -> 14.3 us  [call(): pl.pallas_call(kernel, out_shape=[shape(o) for o in outs], in_specs=[spec...]
  transfers between devices with their start and end apart: 14 -> 15, of which waited for: 13 -> 14; matrix products, arithmetic and copies ran while one was open for 0% -> 0% of each run, Pallas kernels for 0% -> 3%
where the time goes in v4:
time: 65.4 us; the launch traced here: 65.2 us
  waiting for transfers between devices  29.7 us (45%)
  starting transfers between devices  20.1 us (31%)
  Pallas kernels  14.3 us (22%)
  between operations  1.08 us (2%)
    pallas_call x12, Pallas kernels, call(): pl.pallas_call(kernel, out_shape=[shape(o) for o in outs], in_specs=[spec...  14.3 us
    ppermute x4, starting transfers between devices, next_chip(): return lax.ppermute(x, ('wide', 'narrow'), pairs)  13.2 us
    ppermute x4, waiting for transfers between devices, next_chip(): return lax.ppermute(x, ('wide', 'narrow'), pairs)  11 us
    ppermute x3, waiting for transfers between devices, exchange_x(): lax.ppermute(rightward, 'narrow', right)  7.26 us
    ppermute x3, waiting for transfers between devices, exchange_x(): lax.ppermute(leftward, 'narrow', left)  6.35 us
    ppermute x5, waiting for transfers between devices, other_core(): return lax.ppermute(x, 'wide', [(i, i + 1 - 2 * (i % 2)) for i in range(n)])  5.06 us
    ppermute x3, starting transfers between devices, exchange_x(): lax.ppermute(rightward, 'narrow', right)  4.19 us
    ppermute x3, starting transfers between devices, exchange_x(): lax.ppermute(leftward, 'narrow', left)  2.09 us
  transfers between devices with their start and end apart: 15, of which 14 were waited for; matrix products, arithmetic and copies ran while one was open for 0% of the time, Pallas kernels for 3%

profile of v4, /device:TPU:6, one launch (start us, length us, event | category | flops | bytes accessed | tf_op | source)
XLA Modules:
  0.0 65.2 jit_solution(15820686422564159952)
XLA Ops:
  0.6 0.0 copy-start.4
  0.6 0.0 copy-start.6
  0.7 0.0 copy-start.10
  0.7 0.0 copy-start.12
  0.7 0.0 copy-start.14
  0.7 0.0 copy-start.1
  0.7 7.0 %force.1 = (f32[384,512]{1,0:T(8,128)S(1)}, f32[48,512]{1,0:T(8,128)S(1)}, f32[48,512]{1,0:T(8,128)S(1)}) custom-call(f32[3,8,16,512]{3,2,1,0:T(8,128)} %refs_0_.1, f32[8,16,512]{2,1,0:T(8,128)} %refs_1_.1, bf16[512,768]{1,0:T(8,128)(2,1)} %constant.42.clone.refs_2_, bf16[432,192]{1,0:T(8,128)(2,1)} %constant.43.clone.refs_3_, ...), custom_call_target="tpu_custom_call" | custom-call | tf_op jit(solution)/shard_map/force/pallas_call | solution.py:546
  7.7 0.0 copy-start
  7.7 0.0 copy-start.2
  7.7 0.0 copy-start.5
  7.8 0.0 copy-start.7
  7.8 1.9 %collective-permute-start = (f32[48,512]{1,0:T(8,128)S(1)}, f32[48,512]{1,0:T(8,128)S(1)}, u32[]{:S(2)}, u32[]{:S(2)}) collective-permute-start(f32[48,512]{1,0:T(8,128)S(1)} %get-tuple-element.36), channel_id=1, source_target_pairs={{0,1},{1,2},{2,3},{3,4},{4,5},{5,6},{6,7},{7,0},{8,9},{9,10},{10,1... | collective-permute-start | bytes 294920 | tf_op jit(solution)/shard_map/ppermute | solution.py:562
  9.7 0.2 collective-permute-start.1
  9.9 2.9 %collective-permute-done.ml_ref = f32[48,512]{1,0:T(8,128)S(1)} collective-permute-done((f32[48,512]{1,0:T(8,128)S(1)}, f32[48,512]{1,0:T(8,128)S(1)}, u32[]{:S(2)}, u32[]{:S(2)}) %collective-permute-start) | collective-permute-done | bytes 98336 | tf_op jit(solution)/shard_map/ppermute | solution.py:562
  12.8 2.8 %collective-permute-done.1.mr_ref = f32[48,512]{1,0:T(8,128)S(1)} collective-permute-done((f32[48,512]{1,0:T(8,128)S(1)}, f32[48,512]{1,0:T(8,128)S(1)}, u32[]{:S(2)}, u32[]{:S(2)}) %collective-permute-start.1) | collective-permute-done | bytes 98336 | tf_op jit(solution)/shard_map/ppermute | solution.py:562
  15.6 0.0 copy-done.4
  15.6 0.0 copy-done.6
  15.6 0.0 copy-done.10
  15.6 0.0 copy-done.12
  15.6 0.0 copy-done.14
  15.6 1.5 %div.1 = (f32[384,512]{1,0:T(8,128)}, f32[48,512]{1,0:T(8,128)S(1)}, f32[48,512]{1,0:T(8,128)S(1)}, f32[144,512]{1,0:T(8,128)S(1)}, f32[56,512]{1,0:T(8,128)S(1)...) custom-call(f32[384,512]{1,0:T(8,128)S(1)} %get-tuple-element.35.f_ref, ...), custom_call_target="tpu_custom_call" | custom-call | tf_op jit(solution)/shard_map/div/pallas_call | solution.py:546
  17.1 0.1 collective-permute-start.2
  17.2 1.3 %collective-permute-done.2.in_ref.refs_3_ = f32[56,512]{1,0:T(8,128)S(1)} collective-permute-done((f32[56,512]{1,0:T(8,128)S(1)}, f32[56,512]{1,0:T(8,128)S(1)}, u32[]{:S(2)}, u32[]{:S(2)}) %collective-permute-start.2) | collective-permute-done | bytes 114720 | tf_op jit(solution)/shard_map/ppermute | solution.py:567
  18.5 4.7 %collective-permute-start.3 = (f32[56,512]{1,0:T(8,128)S(1)}, f32[56,512]{1,0:T(8,128)S(1)}, u32[]{:S(2)}, u32[]{:S(2)}) collective-permute-start(f32[56,512]{1,0:T(8,128)S(1)} %get-tuple-element.46), channel_id=1, source_target_pairs={{0,1},{1,0},{2,3},{3,2},{4,5},{5,4},{6,7},{7,6},{8,16},{9,17},{10,... | collective-permute-start | bytes 344072 | tf_op jit(solution)/shard_map/ppermute | solution.py:578
  23.2 0.7 %collective-permute-start.5 = (f32[48,512]{1,0:T(8,128)S(1)}, f32[48,512]{1,0:T(8,128)S(1)}, u32[]{:S(2)}, u32[]{:S(2)}) collective-permute-start(f32[48,512]{1,0:T(8,128)S(1)} %get-tuple-element.49), channel_id=1, source_target_pairs={{0,1},{1,0},{2,3},{3,2},{4,5},{5,4},{6,7},{7,6},{8,16},{9,17},{10,... | collective-permute-start | bytes 294920 | tf_op jit(solution)/shard_map/ppermute | solution.py:578
  24.0 2.5 %collective-permute-done.3.out_msg_ref.refs_4_ = f32[56,512]{1,0:T(8,128)S(1)} collective-permute-done((f32[56,512]{1,0:T(8,128)S(1)}, f32[56,512]{1,0:T(8,128)S(1)}, u32[]{:S(2)}, u32[]{:S(2)}) %collective-permute-start.3) | collective-permute-done | bytes 114720 | tf_op jit(solution)/shard_map/ppermute | solution.py:578
  26.5 0.1 collective-permute-start.4
  26.5 1.2 %collective-permute-done.4.refs_5_ = f32[24,512]{1,0:T(8,128)S(1)} collective-permute-done((f32[24,512]{1,0:T(8,128)S(1)}, f32[24,512]{1,0:T(8,128)S(1)}, u32[]{:S(2)}, u32[]{:S(2)}) %collective-permute-start.4) | collective-permute-done | bytes 49184 | tf_op jit(solution)/shard_map/ppermute | solution.py:567
  27.8 0.0 copy-done.1
  27.8 0.0 copy-done
  27.8 0.0 copy-done.2
  27.8 0.0 copy-done.5
  27.8 0.0 copy-start.3
  27.8 0.0 copy-start.13
  27.8 0.0 copy-start.15
  27.8 0.0 copy-start.9
  27.8 0.0 copy-start.11
  27.9 1.6 %first_pass.1 = (f32[208,512]{1,0:T(8,128)S(1)}, f32[128,512]{1,0:T(8,128)S(1)}) custom-call(f32[144,512]{1,0:T(8,128)S(1)} %get-tuple-element.38.refs_0_, f32[40,512]{1,0:T(8,128)S(1)} %get-tuple-element.39.refs_1_, f32[40,512]{1,0:T(8,128)S(1)} %get-tuple-element.40.refs_2_, f32[56,512]{1,0:T(8,128)S(1)} %collective-permute-done.2.in_ref.refs_3_, ...), custom_call_target="tpu_custom_call" | custom-call | tf_op jit(solution)/shard_map/first_pass/pallas_call | solution.py:546
  29.5 0.0 copy-start.8
  29.5 1.4 %collective-permute-done.5.refs_0_.f_out_ref = f32[48,512]{1,0:T(8,128)S(1)} collective-permute-done((f32[48,512]{1,0:T(8,128)S(1)}, f32[48,512]{1,0:T(8,128)S(1)}, u32[]{:S(2)}, u32[]{:S(2)}) %collective-permute-start.5) | collective-permute-done | bytes 98336 | tf_op jit(solution)/shard_map/ppermute | solution.py:578
  30.9 0.0 copy-done.13
  30.9 0.5 stiff_msg.1
  31.4 0.9 %collective-permute-start.6 = (f32[32,512]{1,0:T(8,128)S(1)}, f32[32,512]{1,0:T(8,128)S(1)}, u32[]{:S(2)}, u32[]{:S(2)}) collective-permute-start(f32[32,512]{1,0:T(8,128)S(1)} %get-tuple-element.50), channel_id=1, source_target_pairs={{0,1},{1,2},{2,3},{3,4},{4,5},{5,6},{6,7},{7,0},{8,9},{9,10},{10,1... | collective-permute-start | bytes 196616 | tf_op jit(solution)/shard_map/ppermute | solution.py:562
  32.3 1.2 %collective-permute-start.7 = (f32[32,512]{1,0:T(8,128)S(1)}, f32[32,512]{1,0:T(8,128)S(1)}, u32[]{:S(2)}, u32[]{:S(2)}) collective-permute-start(f32[32,512]{1,0:T(8,128)S(1)} %get-tuple-element.51), channel_id=1, source_target_pairs={{1,0},{2,1},{3,2},{4,3},{5,4},{6,5},{7,6},{0,7},{9,8},{10,9},{11,1... | collective-permute-start | bytes 196616 | tf_op jit(solution)/shard_map/ppermute | solution.py:562
  33.5 2.6 %collective-permute-done.6.ml_ref = f32[32,512]{1,0:T(8,128)S(1)} collective-permute-done((f32[32,512]{1,0:T(8,128)S(1)}, f32[32,512]{1,0:T(8,128)S(1)}, u32[]{:S(2)}, u32[]{:S(2)}) %collective-permute-start.6) | collective-permute-done | bytes 65568 | tf_op jit(solution)/shard_map/ppermute | solution.py:562
  36.1 1.4 %collective-permute-done.7.mr_ref = f32[32,512]{1,0:T(8,128)S(1)} collective-permute-done((f32[32,512]{1,0:T(8,128)S(1)}, f32[32,512]{1,0:T(8,128)S(1)}, u32[]{:S(2)}, u32[]{:S(2)}) %collective-permute-start.7) | collective-permute-done | bytes 65568 | tf_op jit(solution)/shard_map/ppermute | solution.py:562
  37.4 1.1 %stiff.1 = (f32[128,512]{1,0:T(8,128)S(1)}, f32[144,512]{1,0:T(8,128)S(1)}, f32[56,512]{1,0:T(8,128)S(1)}, f32[56,512]{1,0:T(8,128)S(1)}, f32[40,512]{1,0:T(8,12...) custom-call(f32[128,512]{1,0:T(8,128)S(1)} %get-tuple-element.48.g_ref, ...), custom_call_target="tpu_custom_call" | custom-call | tf_op jit(solution)/shard_map/stiff/pallas_call | solution.py:546
  38.5 0.1 collective-permute-start.8
  38.6 1.3 %collective-permute-done.8.in_ref.refs_3_ = f32[56,512]{1,0:T(8,128)S(1)} collective-permute-done((f32[56,512]{1,0:T(8,128)S(1)}, f32[56,512]{1,0:T(8,128)S(1)}, u32[]{:S(2)}, u32[]{:S(2)}) %collective-permute-start.8) | collective-permute-done | bytes 114720 | tf_op jit(solution)/shard_map/ppermute | solution.py:567
  40.0 3.9 %collective-permute-start.9 = (f32[56,512]{1,0:T(8,128)S(1)}, f32[56,512]{1,0:T(8,128)S(1)}, u32[]{:S(2)}, u32[]{:S(2)}) collective-permute-start(f32[56,512]{1,0:T(8,128)S(1)} %stiff_out.1), channel_id=1, source_target_pairs={{0,1},{1,0},{2,3},{3,2},{4,5},{5,4},{6,7},{7,6},{8,16},{9,17},{10,... | collective-permute-start | bytes 344072 | tf_op jit(solution)/shard_map/ppermute | solution.py:578
  43.9 4.0 %collective-permute-done.9.out_msg_ref.refs_4_ = f32[56,512]{1,0:T(8,128)S(1)} collective-permute-done((f32[56,512]{1,0:T(8,128)S(1)}, f32[56,512]{1,0:T(8,128)S(1)}, u32[]{:S(2)}, u32[]{:S(2)}) %collective-permute-start.9) | collective-permute-done | bytes 114720 | tf_op jit(solution)/shard_map/ppermute | solution.py:578
  47.9 0.3 collective-permute-start.10
  48.2 1.2 %collective-permute-done.10.refs_5_ = f32[24,512]{1,0:T(8,128)S(1)} collective-permute-done((f32[24,512]{1,0:T(8,128)S(1)}, f32[24,512]{1,0:T(8,128)S(1)}, u32[]{:S(2)}, u32[]{:S(2)}) %collective-permute-start.10) | collective-permute-done | bytes 49184 | tf_op jit(solution)/shard_map/ppermute | solution.py:567
  49.4 1.7 %second_pass.1 = (f32[128,512]{1,0:T(8,128)S(1)}, f32[8,512]{1,0:T(8,128)S(1)}, f32[8,512]{1,0:T(8,128)S(1)}) custom-call(f32[208,512]{1,0:T(8,128)S(1)} %get-tuple-element.47.t_ref, f32[144,512]{1,0:T(8,128)S(1)} %get-tuple-element.52.refs_0_, f32[40,512]{1,0:T(8,128)S(1)} %get-tuple-element.53.refs_1_, f32[40,512]{1,0:T(8,128)S(1)} %get-tuple-element.54.refs_2_, ...), custom_call_target="tpu_custom_call" | custom-call | tf_op jit(solution)/shard_map/second_pass/pallas_call | solution.py:546
  51.0 1.4 %collective-permute-start.11 = (f32[8,512]{1,0:T(8,128)S(1)}, f32[8,512]{1,0:T(8,128)S(1)}, u32[]{:S(2)}, u32[]{:S(2)}) collective-permute-start(f32[8,512]{1,0:T(8,128)S(1)} %get-tuple-element.60), channel_id=1, source_target_pairs={{0,1},{1,2},{2,3},{3,4},{4,5},{5,6},{6,7},{7,0},{8,9},{9,10},{10,1... | collective-permute-start | bytes 49160 | tf_op jit(solution)/shard_map/ppermute | solution.py:562
  52.4 0.7 %collective-permute-start.12 = (f32[8,512]{1,0:T(8,128)S(1)}, f32[8,512]{1,0:T(8,128)S(1)}, u32[]{:S(2)}, u32[]{:S(2)}) collective-permute-start(f32[8,512]{1,0:T(8,128)S(1)} %get-tuple-element.61), channel_id=1, source_target_pairs={{1,0},{2,1},{3,2},{4,3},{5,4},{6,5},{7,6},{0,7},{9,8},{10,9},{11,1... | collective-permute-start | bytes 49160 | tf_op jit(solution)/shard_map/ppermute | solution.py:562
  53.1 1.7 %collective-permute-done.11.ml_ref = f32[8,512]{1,0:T(8,128)S(1)} collective-permute-done((f32[8,512]{1,0:T(8,128)S(1)}, f32[8,512]{1,0:T(8,128)S(1)}, u32[]{:S(2)}, u32[]{:S(2)}) %collective-permute-start.11) | collective-permute-done | bytes 16416 | tf_op jit(solution)/shard_map/ppermute | solution.py:562
  54.8 2.2 %collective-permute-done.12.mr_ref = f32[8,512]{1,0:T(8,128)S(1)} collective-permute-done((f32[8,512]{1,0:T(8,128)S(1)}, f32[8,512]{1,0:T(8,128)S(1)}, u32[]{:S(2)}, u32[]{:S(2)}) %collective-permute-start.12) | collective-permute-done | bytes 16416 | tf_op jit(solution)/shard_map/ppermute | solution.py:562
  57.0 0.1 last_x.1
  57.1 0.1 collective-permute-start.14
  57.2 3.8 %collective-permute-start.13 = (f32[16,512]{1,0:T(8,128)S(1)}, f32[16,512]{1,0:T(8,128)S(1)}, u32[]{:S(2)}, u32[]{:S(2)}) collective-permute-start(f32[16,512]{1,0:T(8,128)S(1)} %get-tuple-element.62), channel_id=1, source_target_pairs={{0,1},{1,0},{2,3},{3,2},{4,5},{5,4},{6,7},{7,6},{8,16},{9,17},{10,... | collective-permute-start | bytes 98312 | tf_op jit(solution)/shard_map/ppermute | solution.py:578
  61.0 3.2 %collective-permute-done.13.out_msg_ref = f32[16,512]{1,0:T(8,128)S(1)} collective-permute-done((f32[16,512]{1,0:T(8,128)S(1)}, f32[16,512]{1,0:T(8,128)S(1)}, u32[]{:S(2)}, u32[]{:S(2)}) %collective-permute-start.13) | collective-permute-done | bytes 32800 | tf_op jit(solution)/shard_map/ppermute | solution.py:578
  64.2 0.0 collective-permute-done.14.in_ref
  64.2 0.9 %last_z.1 = (f32[128,512]{1,0:T(8,128)}, f32[384,512]{1,0:T(8,128)}) custom-call(f32[16,512]{1,0:T(8,128)S(1)} %collective-permute-done.13.out_msg_ref, f32[64,512]{1,0:T(8,128)S(1)} %collective-permute-done.14.in_ref, f32[48,512]{1,0:T(8,128)S(1)} %collective-permute-done.5.refs_0_.f_out_ref, ...), custom_call_target="tpu_custom_call", output_to_operand_aliasing={{1}: (6, {})} | custom-call | tf_op jit(solution)/shard_map/last_z/pallas_call | solution.py:546
  (10 shorter events, 0.1 us)
Async XLA Ops:
  0.6 14.9 %copy-start.4 = (bf16[512,256]{1,0:T(8,128)(2,1)S(1)}, bf16[512,256]{1,0:T(8,128)(2,1)}, u32[]{:S(2)}) copy-start(bf16[512,256]{1,0:T(8,128)(2,1)} %constant.54.clone.refs_8_.wd_y) | copy-start | bytes 786436
  0.6 14.9 %copy-start.6 = (bf16[144,432]{1,0:T(8,128)(2,1)S(1)}, bf16[144,432]{1,0:T(8,128)(2,1)}, u32[]{:S(2)}) copy-start(bf16[144,432]{1,0:T(8,128)(2,1)} %constant.47.clone.xe_w) | copy-start | bytes 373252
  0.7 14.9 %copy-start.10 = (bf16[144,864]{1,0:T(8,128)(2,1)S(1)}, bf16[144,864]{1,0:T(8,128)(2,1)}, u32[]{:S(2)}) copy-start(bf16[144,864]{1,0:T(8,128)(2,1)} %constant.52.clone.z_div) | copy-start | bytes 746500
  0.7 14.9 %copy-start.12 = (bf16[144,432]{1,0:T(8,128)(2,1)S(1)}, bf16[144,432]{1,0:T(8,128)(2,1)}, u32[]{:S(2)}) copy-start(bf16[144,432]{1,0:T(8,128)(2,1)} %constant.49.clone.xe_wd) | copy-start | bytes 373252
  0.7 14.9 %copy-start.14 = (f32[1,512]{1,0:T(1,128)S(1)}, f32[1,512]{1,0:T(1,128)}, u32[]{:S(2)}) copy-start(f32[1,512]{1,0:T(1,128)} %constant.56.clone.refs_9_.w_y) | copy-start | bytes 6148
  0.7 27.1 %copy-start.1 = (bf16[1024,640]{1,0:T(8,128)(2,1)S(1)}, bf16[1024,640]{1,0:T(8,128)(2,1)}, u32[]{:S(2)}) copy-start(bf16[1024,640]{1,0:T(8,128)(2,1)} %constant.60.clone.refs_7_) | copy-start | bytes 3932164
  7.7 20.1 %copy-start = (bf16[1280,512]{1,0:T(8,128)(2,1)S(1)}, bf16[1280,512]{1,0:T(8,128)(2,1)}, u32[]{:S(2)}) copy-start(bf16[1280,512]{1,0:T(8,128)(2,1)} %constant.61.clone.refs_10_) | copy-start | bytes 3932164
  7.7 20.0 %copy-start.2 = (f32[208,640]{1,0:T(8,128)S(1)}, f32[208,640]{1,0:T(8,128)}, u32[]{:S(2)}) copy-start(f32[208,640]{1,0:T(8,128)} %constant.62.clone.refs_8_) | copy-start | bytes 1597444
  7.7 20.0 %copy-start.5 = (bf16[128,624]{1,0:T(8,128)(2,1)S(1)}, bf16[128,624]{1,0:T(8,128)(2,1)}, u32[]{:S(2)}) copy-start(bf16[128,624]{1,0:T(8,128)(2,1)} %constant.59.clone.refs_9_) | copy-start | bytes 479236
  7.8 20.0 %copy-start.7 = (bf16[208,1152]{1,0:T(8,128)(2,1)S(1)}, bf16[208,1152]{1,0:T(8,128)(2,1)}, u32[]{:S(2)}) copy-start(bf16[208,1152]{1,0:T(8,128)(2,1)} %constant.57.clone.refs_6_) | copy-start | bytes 1437700
  7.8 5.0 %collective-permute-start = (f32[48,512]{1,0:T(8,128)S(1)}, f32[48,512]{1,0:T(8,128)S(1)}, u32[]{:S(2)}, u32[]{:S(2)}) collective-permute-start(f32[48,512]{1,0:T(8,128)S(1)} %get-tuple-element.36), channel_id=1, source_target_pairs={{0,1},{1,2},{2,3},{3,4},{4,5},{5,6},{6,7},{7,0},{8,9},{9,10},{10,1... | collective-permute-start | bytes 294920 | tf_op jit(solution)/shard_map/ppermute | solution.py:562
  9.7 5.9 %collective-permute-start.1 = (f32[48,512]{1,0:T(8,128)S(1)}, f32[48,512]{1,0:T(8,128)S(1)}, u32[]{:S(2)}, u32[]{:S(2)}) collective-permute-start(f32[48,512]{1,0:T(8,128)S(1)} %get-tuple-element.37), channel_id=1, source_target_pairs={{1,0},{2,1},{3,2},{4,3},{5,4},{6,5},{7,6},{0,7},{9,8},{10,9},{11,1... | collective-permute-start | bytes 294920 | tf_op jit(solution)/shard_map/ppermute | solution.py:562
  17.1 1.4 %collective-permute-start.2 = (f32[56,512]{1,0:T(8,128)S(1)}, f32[56,512]{1,0:T(8,128)S(1)}, u32[]{:S(2)}, u32[]{:S(2)}) collective-permute-start(f32[56,512]{1,0:T(8,128)S(1)} %get-tuple-element.41), channel_id=1, source_target_pairs={{0,8},{8,0},{16,24},{24,16},{32,40},{40,32},{48,56},{56,48},{64,72... | collective-permute-start | bytes 344072 | tf_op jit(solution)/shard_map/ppermute | solution.py:567
  18.5 7.9 %collective-permute-start.3 = (f32[56,512]{1,0:T(8,128)S(1)}, f32[56,512]{1,0:T(8,128)S(1)}, u32[]{:S(2)}, u32[]{:S(2)}) collective-permute-start(f32[56,512]{1,0:T(8,128)S(1)} %get-tuple-element.46), channel_id=1, source_target_pairs={{0,1},{1,0},{2,3},{3,2},{4,5},{5,4},{6,7},{7,6},{8,16},{9,17},{10,... | collective-permute-start | bytes 344072 | tf_op jit(solution)/shard_map/ppermute | solution.py:578
  23.2 7.7 %collective-permute-start.5 = (f32[48,512]{1,0:T(8,128)S(1)}, f32[48,512]{1,0:T(8,128)S(1)}, u32[]{:S(2)}, u32[]{:S(2)}) collective-permute-start(f32[48,512]{1,0:T(8,128)S(1)} %get-tuple-element.49), channel_id=1, source_target_pairs={{0,1},{1,0},{2,3},{3,2},{4,5},{5,4},{6,7},{7,6},{8,16},{9,17},{10,... | collective-permute-start | bytes 294920 | tf_op jit(solution)/shard_map/ppermute | solution.py:578
  26.5 1.3 %collective-permute-start.4 = (f32[24,512]{1,0:T(8,128)S(1)}, f32[24,512]{1,0:T(8,128)S(1)}, u32[]{:S(2)}, u32[]{:S(2)}) collective-permute-start(f32[24,512]{1,0:T(8,128)S(1)} %div_out_far.1), channel_id=1, source_target_pairs={{0,8},{8,0},{16,24},{24,16},{32,40},{40,32},{48,56},{56,48},{64,72... | collective-permute-start | bytes 147464 | tf_op jit(solution)/shard_map/ppermute | solution.py:567
  27.8 3.1 %copy-start.3 = (bf16[512,256]{1,0:T(8,128)(2,1)S(1)}, bf16[512,256]{1,0:T(8,128)(2,1)}, u32[]{:S(2)}) copy-start(bf16[512,256]{1,0:T(8,128)(2,1)} %constant.55.clone.k_y) | copy-start | bytes 786436
  27.8 3.1 %copy-start.13 = (bf16[32,384]{1,0:T(8,128)(2,1)S(1)}, bf16[32,384]{1,0:T(8,128)(2,1)}, u32[]{:S(2)}) copy-start(bf16[32,384]{1,0:T(8,128)(2,1)} %constant.46.clone.refs_6_.xm_w) | copy-start | bytes 73732
  27.8 3.1 %copy-start.15 = (bf16[32,384]{1,0:T(8,128)(2,1)S(1)}, bf16[32,384]{1,0:T(8,128)(2,1)}, u32[]{:S(2)}) copy-start(bf16[32,384]{1,0:T(8,128)(2,1)} %constant.50.clone.xm_k) | copy-start | bytes 73732
  27.8 9.6 %copy-start.9 = (bf16[144,864]{1,0:T(8,128)(2,1)S(1)}, bf16[144,864]{1,0:T(8,128)(2,1)}, u32[]{:S(2)}) copy-start(bf16[144,864]{1,0:T(8,128)(2,1)} %constant.53.clone.z_st) | copy-start | bytes 746500
  27.8 9.6 %copy-start.11 = (bf16[144,432]{1,0:T(8,128)(2,1)S(1)}, bf16[144,432]{1,0:T(8,128)(2,1)}, u32[]{:S(2)}) copy-start(bf16[144,432]{1,0:T(8,128)(2,1)} %constant.51.clone.xe_k) | copy-start | bytes 373252
  29.5 19.9 %copy-start.8 = (bf16[208,1152]{1,0:T(8,128)(2,1)S(1)}, bf16[208,1152]{1,0:T(8,128)(2,1)}, u32[]{:S(2)}) copy-start(bf16[208,1152]{1,0:T(8,128)(2,1)} %constant.58.clone.refs_6_) | copy-start | bytes 1437700
  31.4 4.7 %collective-permute-start.6 = (f32[32,512]{1,0:T(8,128)S(1)}, f32[32,512]{1,0:T(8,128)S(1)}, u32[]{:S(2)}, u32[]{:S(2)}) collective-permute-start(f32[32,512]{1,0:T(8,128)S(1)} %get-tuple-element.50), channel_id=1, source_target_pairs={{0,1},{1,2},{2,3},{3,4},{4,5},{5,6},{6,7},{7,0},{8,9},{9,10},{10,1... | collective-permute-start | bytes 196616 | tf_op jit(solution)/shard_map/ppermute | solution.py:562
  32.3 5.2 %collective-permute-start.7 = (f32[32,512]{1,0:T(8,128)S(1)}, f32[32,512]{1,0:T(8,128)S(1)}, u32[]{:S(2)}, u32[]{:S(2)}) collective-permute-start(f32[32,512]{1,0:T(8,128)S(1)} %get-tuple-element.51), channel_id=1, source_target_pairs={{1,0},{2,1},{3,2},{4,3},{5,4},{6,5},{7,6},{0,7},{9,8},{10,9},{11,1... | collective-permute-start | bytes 196616 | tf_op jit(solution)/shard_map/ppermute | solution.py:562
  38.5 1.4 %collective-permute-start.8 = (f32[56,512]{1,0:T(8,128)S(1)}, f32[56,512]{1,0:T(8,128)S(1)}, u32[]{:S(2)}, u32[]{:S(2)}) collective-permute-start(f32[56,512]{1,0:T(8,128)S(1)} %get-tuple-element.55), channel_id=1, source_target_pairs={{0,8},{8,0},{16,24},{24,16},{32,40},{40,32},{48,56},{56,48},{64,72... | collective-permute-start | bytes 344072 | tf_op jit(solution)/shard_map/ppermute | solution.py:567
  40.0 7.9 %collective-permute-start.9 = (f32[56,512]{1,0:T(8,128)S(1)}, f32[56,512]{1,0:T(8,128)S(1)}, u32[]{:S(2)}, u32[]{:S(2)}) collective-permute-start(f32[56,512]{1,0:T(8,128)S(1)} %stiff_out.1), channel_id=1, source_target_pairs={{0,1},{1,0},{2,3},{3,2},{4,5},{5,4},{6,7},{7,6},{8,16},{9,17},{10,... | collective-permute-start | bytes 344072 | tf_op jit(solution)/shard_map/ppermute | solution.py:578
  47.9 1.5 %collective-permute-start.10 = (f32[24,512]{1,0:T(8,128)S(1)}, f32[24,512]{1,0:T(8,128)S(1)}, u32[]{:S(2)}, u32[]{:S(2)}) collective-permute-start(f32[24,512]{1,0:T(8,128)S(1)} %stiff_out_far.1), channel_id=1, source_target_pairs={{0,8},{8,0},{16,24},{24,16},{32,40},{40,32},{48,56},{56,48},{64,72... | collective-permute-start | bytes 147464 | tf_op jit(solution)/shard_map/ppermute | solution.py:567
  51.0 3.8 %collective-permute-start.11 = (f32[8,512]{1,0:T(8,128)S(1)}, f32[8,512]{1,0:T(8,128)S(1)}, u32[]{:S(2)}, u32[]{:S(2)}) collective-permute-start(f32[8,512]{1,0:T(8,128)S(1)} %get-tuple-element.60), channel_id=1, source_target_pairs={{0,1},{1,2},{2,3},{3,4},{4,5},{5,6},{6,7},{7,0},{8,9},{9,10},{10,1... | collective-permute-start | bytes 49160 | tf_op jit(solution)/shard_map/ppermute | solution.py:562
  52.4 4.6 %collective-permute-start.12 = (f32[8,512]{1,0:T(8,128)S(1)}, f32[8,512]{1,0:T(8,128)S(1)}, u32[]{:S(2)}, u32[]{:S(2)}) collective-permute-start(f32[8,512]{1,0:T(8,128)S(1)} %get-tuple-element.61), channel_id=1, source_target_pairs={{1,0},{2,1},{3,2},{4,3},{5,4},{6,5},{7,6},{0,7},{9,8},{10,9},{11,1... | collective-permute-start | bytes 49160 | tf_op jit(solution)/shard_map/ppermute | solution.py:562
  57.1 7.1 %collective-permute-start.14 = (f32[64,512]{1,0:T(8,128)S(1)}, f32[64,512]{1,0:T(8,128)S(1)}, u32[]{:S(2)}, u32[]{:S(2)}) collective-permute-start(f32[64,512]{1,0:T(8,128)S(1)} %get-tuple-element.63), channel_id=1, source_target_pairs={{0,8},{8,0},{16,24},{24,16},{32,40},{40,32},{48,56},{56,48},{64,72... | collective-permute-start | bytes 393224 | tf_op jit(solution)/shard_map/ppermute | solution.py:567
  57.2 7.0 %collective-permute-start.13 = (f32[16,512]{1,0:T(8,128)S(1)}, f32[16,512]{1,0:T(8,128)S(1)}, u32[]{:S(2)}, u32[]{:S(2)}) collective-permute-start(f32[16,512]{1,0:T(8,128)S(1)} %get-tuple-element.62), channel_id=1, source_target_pairs={{0,1},{1,0},{2,3},{3,2},{4,5},{5,4},{6,7},{7,6},{8,16},{9,17},{10,... | collective-permute-start | bytes 98312 | tf_op jit(solution)/shard_map/ppermute | solution.py:578

commit v5 on v4

--- a/solution.py
+++ b/solution.py
@@ -323,6 +323,20 @@
     for k, (c, step) in enumerate(((0, 0), (1, 0), (2, 0), (0, 1))):
         r_ref[16 + 8 * k : 24 + 8 * k] = edge(f_ref, 128 * c, 15 - step)
         l_ref[16 + 8 * k : 24 + 8 * k] = edge(f_ref, 128 * c, step)
+    to_pairs(r_ref, l_ref)
+
+
+def to_pairs(r_ref, l_ref):
+    right, left = r_ref[...], l_ref[...]
+    odd = lax.axis_index("narrow") % 2 == 1
+    r_ref[...] = jnp.where(odd, right, left)
+    l_ref[...] = jnp.where(odd, left, right)
+
+
+def from_pairs(far_ref, near_ref):
+    far, near = far_ref[...], near_ref[...]
+    odd = lax.axis_index("narrow") % 2 == 1
+    return jnp.where(odd, near, far), jnp.where(odd, far, near)
 
 
 def edge(ref, base, x):
@@ -381,7 +395,8 @@
     force_ref, f_up_ref, f_down_ref, u_ref, *faces = refs[:9]
     h0_ref, h12_ref, fx_ref, sem = refs[9:]
     _, _, has_l, has_r = flags()
-    ml, mr = ml_ref[...] * has_l, mr_ref[...] * has_r
+    ml, mr = from_pairs(ml_ref, mr_ref)
+    ml, mr = ml * has_l, mr * has_r
     fx_ref[...] = f_ref[...]
     full = []
     for c in range(3):
@@ -473,13 +488,15 @@
     l_ref[16:24] = edge(g_ref, 0, 0)
     r_ref[24:] = edge(g_ref, 0, 14)
     l_ref[24:] = edge(g_ref, 0, 1)
+    to_pairs(r_ref, l_ref)
 
 
 def stiff_kernel(ends, g_ref, ml_ref, mr_ref, xe_w, xe_k, z_st, k_y, w_y, *refs):
     gx_ref, u_ref, *faces = refs[:7]
     p_ref, q_ref = refs[7:]
     _, _, has_l, has_r = flags()
-    ml, mr = ml_ref[...] * has_l, mr_ref[...] * has_r
+    ml, mr = from_pairs(ml_ref, mr_ref)
+    ml, mr = ml * has_l, mr * has_r
     gx_ref[...] = g_ref[...]
     add_edge(gx_ref, 0, 0, ml[16:24])
     add_edge(gx_ref, 0, 15, mr[16:24])
@@ -500,13 +517,15 @@
     g_ref[...] = box(t_ref[...] - join(*join_refs), *box_refs)
     r_ref[...] = edge(g_ref, 0, 15)
     l_ref[...] = edge(g_ref, 0, 0)
+    to_pairs(r_ref, l_ref)
 
 
 def last_x_kernel(g_ref, gx_ref, ml_ref, mr_ref, f_up, f_down, out_ref, in_msg_ref, out_msg_ref):
     _, _, has_l, has_r = flags()
     out_ref[...] = g_ref[...] + gx_ref[...]
-    add_edge(out_ref, 0, 0, ml_ref[...] * has_l)
-    add_edge(out_ref, 0, 15, mr_ref[...] * has_r)
+    ml, mr = from_pairs(ml_ref, mr_ref)
+    add_edge(out_ref, 0, 0, ml * has_l)
+    add_edge(out_ref, 0, 15, mr * has_r)
     odd = is_odd()
     up, down = out_ref[112:], out_ref[:16]
     out_msg_ref[...] = jnp.where(odd, up, down)
@@ -555,11 +574,16 @@
     )(*args)
 
 
-def exchange_x(rightward, leftward):
-    n = lax.axis_size("narrow")
-    right = [(i, (i + 1) % n) for i in range(n)]
-    left = [(j, i) for i, j in right]
-    return lax.ppermute(rightward, "narrow", right), lax.ppermute(leftward, "narrow", left)
+def exchange_x(far, near):
+    nz, nx = lax.axis_size("wide"), lax.axis_size("narrow")
+    pairs = []
+    for z in range(nz):
+        for k in range(nx):
+            to = k - 1 + 2 * (k % 2)
+            other = (z, to) if 0 <= to < nx else (z + 1 - 2 * (z % 2), k)
+            pairs.append((z * nx + k, other[0] * nx + other[1]))
+    far = lax.ppermute(far, ("wide", "narrow"), pairs)
+    return far, lax.ppermute(near, "narrow", [(k, k + 1 - 2 * (k % 2)) for k in range(nx)])
 
 
 def other_core(x):

time: 65.4 us -> 64 us (0.979)
  waiting for transfers between devices: 29.7 us -> 28.1 us
    ppermute x6, waiting for transfers between devices: 13.6 us -> 12.6 us  [the longest x3 10.6 us: exchange_x(): far = lax.ppermute(far, ('wide', 'narrow'), pairs)]
where the time goes in v5:
time: 64 us; the launch traced here: 63.8 us
  waiting for transfers between devices  28.1 us (44%)
  starting transfers between devices  20.2 us (32%)
  Pallas kernels  14.3 us (22%)
  between operations  1.08 us (2%)
    pallas_call x12, Pallas kernels, call(): pl.pallas_call(kernel, out_shape=[shape(o) for o in outs], in_specs=[spec...  14.3 us
    ppermute x4, starting transfers between devices, next_chip(): return lax.ppermute(x, ('wide', 'narrow'), pairs)  13.7 us
    ppermute x3, waiting for transfers between devices, exchange_x(): far = lax.ppermute(far, ('wide', 'narrow'), pairs)  10.6 us
    ppermute x4, waiting for transfers between devices, next_chip(): return lax.ppermute(x, ('wide', 'narrow'), pairs)  10.4 us
    ppermute x3, starting transfers between devices, exchange_x(): far = lax.ppermute(far, ('wide', 'narrow'), pairs)  5.91 us
    ppermute x5, waiting for transfers between devices, other_core(): return lax.ppermute(x, 'wide', [(i, i + 1 - 2 * (i % 2)) for i in range(n)])  5.06 us
    ppermute x3, waiting for transfers between devices, exchange_x(): lax.ppermute(near, 'narrow', [(k, k + 1 - 2 * (k % 2)) for k in range(nx)])  2.04 us
  transfers between devices with their start and end apart: 15, of which 14 were waited for; matrix products, arithmetic and copies ran while one was open for 0% of the time, Pallas kernels for 3%

profile of v5, /device:TPU:6, one launch (start us, length us, event | category | flops | bytes accessed | tf_op | source)
XLA Modules:
  0.0 63.8 jit_solution(3702130912589070339)
XLA Ops:
  0.6 0.0 copy-start.4
  0.6 0.0 copy-start.6
  0.7 0.0 copy-start.10
  0.7 0.0 copy-start.12
  0.7 0.0 copy-start.14
  0.7 0.0 copy-start.1
  0.7 7.0 %force.1 = (f32[384,512]{1,0:T(8,128)S(1)}, f32[48,512]{1,0:T(8,128)S(1)}, f32[48,512]{1,0:T(8,128)S(1)}) custom-call(f32[3,8,16,512]{3,2,1,0:T(8,128)} %refs_0_.1, f32[8,16,512]{2,1,0:T(8,128)} %refs_1_.1, bf16[512,768]{1,0:T(8,128)(2,1)} %constant.42.clone.refs_2_, bf16[432,192]{1,0:T(8,128)(2,1)} %constant.43.clone.refs_3_, ...), custom_call_target="tpu_custom_call" | custom-call | tf_op jit(solution)/shard_map/force/pallas_call | solution.py:565
  7.7 0.0 copy-start
  7.7 0.0 copy-start.2
  7.7 0.0 copy-start.5
  7.8 0.0 copy-start.7
  7.8 1.9 %collective-permute-start = (f32[48,512]{1,0:T(8,128)S(1)}, f32[48,512]{1,0:T(8,128)S(1)}, u32[]{:S(2)}, u32[]{:S(2)}) collective-permute-start(f32[48,512]{1,0:T(8,128)S(1)} %get-tuple-element.36), channel_id=1, source_target_pairs={{0,8},{1,2},{2,1},{3,4},{4,3},{5,6},{6,5},{7,15},{8,0},{9,10},{10,... | collective-permute-start | bytes 294920 | tf_op jit(solution)/shard_map/ppermute | solution.py:585
  9.7 0.0 collective-permute-start.1
  9.7 4.2 %collective-permute-done.ml_ref = f32[48,512]{1,0:T(8,128)S(1)} collective-permute-done((f32[48,512]{1,0:T(8,128)S(1)}, f32[48,512]{1,0:T(8,128)S(1)}, u32[]{:S(2)}, u32[]{:S(2)}) %collective-permute-start) | collective-permute-done | bytes 98336 | tf_op jit(solution)/shard_map/ppermute | solution.py:585
  13.9 0.4 collective-permute-done.1.mr_ref
  14.3 0.0 copy-done.4
  14.3 0.0 copy-done.6
  14.3 0.0 copy-done.10
  14.3 0.0 copy-done.12
  14.3 0.0 copy-done.14
  14.3 1.4 %div.1 = (f32[384,512]{1,0:T(8,128)}, f32[48,512]{1,0:T(8,128)S(1)}, f32[48,512]{1,0:T(8,128)S(1)}, f32[144,512]{1,0:T(8,128)S(1)}, f32[56,512]{1,0:T(8,128)S(1)...) custom-call(f32[384,512]{1,0:T(8,128)S(1)} %get-tuple-element.35.f_ref, ...), custom_call_target="tpu_custom_call" | custom-call | tf_op jit(solution)/shard_map/div/pallas_call | solution.py:565
  15.8 0.1 collective-permute-start.2
  15.9 1.3 %collective-permute-done.2.in_ref.refs_3_ = f32[56,512]{1,0:T(8,128)S(1)} collective-permute-done((f32[56,512]{1,0:T(8,128)S(1)}, f32[56,512]{1,0:T(8,128)S(1)}, u32[]{:S(2)}, u32[]{:S(2)}) %collective-permute-start.2) | collective-permute-done | bytes 114720 | tf_op jit(solution)/shard_map/ppermute | solution.py:591
  17.2 4.6 %collective-permute-start.3 = (f32[56,512]{1,0:T(8,128)S(1)}, f32[56,512]{1,0:T(8,128)S(1)}, u32[]{:S(2)}, u32[]{:S(2)}) collective-permute-start(f32[56,512]{1,0:T(8,128)S(1)} %get-tuple-element.46), channel_id=1, source_target_pairs={{0,1},{1,0},{2,3},{3,2},{4,5},{5,4},{6,7},{7,6},{8,16},{9,17},{10,... | collective-permute-start | bytes 344072 | tf_op jit(solution)/shard_map/ppermute | solution.py:602
  21.8 0.9 %collective-permute-start.5 = (f32[48,512]{1,0:T(8,128)S(1)}, f32[48,512]{1,0:T(8,128)S(1)}, u32[]{:S(2)}, u32[]{:S(2)}) collective-permute-start(f32[48,512]{1,0:T(8,128)S(1)} %get-tuple-element.49), channel_id=1, source_target_pairs={{0,1},{1,0},{2,3},{3,2},{4,5},{5,4},{6,7},{7,6},{8,16},{9,17},{10,... | collective-permute-start | bytes 294920 | tf_op jit(solution)/shard_map/ppermute | solution.py:602
  22.7 2.5 %collective-permute-done.3.out_msg_ref.refs_4_ = f32[56,512]{1,0:T(8,128)S(1)} collective-permute-done((f32[56,512]{1,0:T(8,128)S(1)}, f32[56,512]{1,0:T(8,128)S(1)}, u32[]{:S(2)}, u32[]{:S(2)}) %collective-permute-start.3) | collective-permute-done | bytes 114720 | tf_op jit(solution)/shard_map/ppermute | solution.py:602
  25.2 0.1 collective-permute-start.4
  25.3 1.2 %collective-permute-done.4.refs_5_ = f32[24,512]{1,0:T(8,128)S(1)} collective-permute-done((f32[24,512]{1,0:T(8,128)S(1)}, f32[24,512]{1,0:T(8,128)S(1)}, u32[]{:S(2)}, u32[]{:S(2)}) %collective-permute-start.4) | collective-permute-done | bytes 49184 | tf_op jit(solution)/shard_map/ppermute | solution.py:591
  26.5 0.0 copy-done.2
  26.5 0.0 copy-done.5
  26.5 0.0 copy-done.7
  26.5 0.0 copy-start.3
  26.5 0.0 copy-start.13
  26.5 0.0 copy-start.15
  26.5 0.0 copy-start.9
  26.6 0.0 copy-start.11
  26.6 1.6 %first_pass.1 = (f32[208,512]{1,0:T(8,128)S(1)}, f32[128,512]{1,0:T(8,128)S(1)}) custom-call(f32[144,512]{1,0:T(8,128)S(1)} %get-tuple-element.38.refs_0_, f32[40,512]{1,0:T(8,128)S(1)} %get-tuple-element.39.refs_1_, f32[40,512]{1,0:T(8,128)S(1)} %get-tuple-element.40.refs_2_, f32[56,512]{1,0:T(8,128)S(1)} %collective-permute-done.2.in_ref.refs_3_, ...), custom_call_target="tpu_custom_call" | custom-call | tf_op jit(solution)/shard_map/first_pass/pallas_call | solution.py:565
  28.2 0.0 copy-start.8
  28.2 1.3 %collective-permute-done.5.refs_0_.f_out_ref = f32[48,512]{1,0:T(8,128)S(1)} collective-permute-done((f32[48,512]{1,0:T(8,128)S(1)}, f32[48,512]{1,0:T(8,128)S(1)}, u32[]{:S(2)}, u32[]{:S(2)}) %collective-permute-start.5) | collective-permute-done | bytes 98336 | tf_op jit(solution)/shard_map/ppermute | solution.py:602
  29.5 0.0 copy-done.3
  29.5 0.5 stiff_msg.1
  30.0 2.4 %collective-permute-start.6 = (f32[32,512]{1,0:T(8,128)S(1)}, f32[32,512]{1,0:T(8,128)S(1)}, u32[]{:S(2)}, u32[]{:S(2)}) collective-permute-start(f32[32,512]{1,0:T(8,128)S(1)} %get-tuple-element.50), channel_id=1, source_target_pairs={{0,8},{1,2},{2,1},{3,4},{4,3},{5,6},{6,5},{7,15},{8,0},{9,10},{10,... | collective-permute-start | bytes 196616 | tf_op jit(solution)/shard_map/ppermute | solution.py:585
  32.3 0.0 collective-permute-start.7
  32.3 3.1 %collective-permute-done.6.ml_ref = f32[32,512]{1,0:T(8,128)S(1)} collective-permute-done((f32[32,512]{1,0:T(8,128)S(1)}, f32[32,512]{1,0:T(8,128)S(1)}, u32[]{:S(2)}, u32[]{:S(2)}) %collective-permute-start.6) | collective-permute-done | bytes 65568 | tf_op jit(solution)/shard_map/ppermute | solution.py:585
  35.4 1.1 %collective-permute-done.7.mr_ref = f32[32,512]{1,0:T(8,128)S(1)} collective-permute-done((f32[32,512]{1,0:T(8,128)S(1)}, f32[32,512]{1,0:T(8,128)S(1)}, u32[]{:S(2)}, u32[]{:S(2)}) %collective-permute-start.7) | collective-permute-done | bytes 65568 | tf_op jit(solution)/shard_map/ppermute | solution.py:586
  36.6 0.0 copy-done.11
  36.6 1.1 %stiff.1 = (f32[128,512]{1,0:T(8,128)S(1)}, f32[144,512]{1,0:T(8,128)S(1)}, f32[56,512]{1,0:T(8,128)S(1)}, f32[56,512]{1,0:T(8,128)S(1)}, f32[40,512]{1,0:T(8,12...) custom-call(f32[128,512]{1,0:T(8,128)S(1)} %get-tuple-element.48.g_ref, ...), custom_call_target="tpu_custom_call" | custom-call | tf_op jit(solution)/shard_map/stiff/pallas_call | solution.py:565
  37.7 0.1 collective-permute-start.8
  37.8 1.3 %collective-permute-done.8.in_ref.refs_3_ = f32[56,512]{1,0:T(8,128)S(1)} collective-permute-done((f32[56,512]{1,0:T(8,128)S(1)}, f32[56,512]{1,0:T(8,128)S(1)}, u32[]{:S(2)}, u32[]{:S(2)}) %collective-permute-start.8) | collective-permute-done | bytes 114720 | tf_op jit(solution)/shard_map/ppermute | solution.py:591
  39.1 3.8 %collective-permute-start.9 = (f32[56,512]{1,0:T(8,128)S(1)}, f32[56,512]{1,0:T(8,128)S(1)}, u32[]{:S(2)}, u32[]{:S(2)}) collective-permute-start(f32[56,512]{1,0:T(8,128)S(1)} %stiff_out.1), channel_id=1, source_target_pairs={{0,1},{1,0},{2,3},{3,2},{4,5},{5,4},{6,7},{7,6},{8,16},{9,17},{10,... | collective-permute-start | bytes 344072 | tf_op jit(solution)/shard_map/ppermute | solution.py:602
  42.9 4.1 %collective-permute-done.9.out_msg_ref.refs_4_ = f32[56,512]{1,0:T(8,128)S(1)} collective-permute-done((f32[56,512]{1,0:T(8,128)S(1)}, f32[56,512]{1,0:T(8,128)S(1)}, u32[]{:S(2)}, u32[]{:S(2)}) %collective-permute-start.9) | collective-permute-done | bytes 114720 | tf_op jit(solution)/shard_map/ppermute | solution.py:602
  47.0 0.3 collective-permute-start.10
  47.3 1.2 %collective-permute-done.10.refs_5_ = f32[24,512]{1,0:T(8,128)S(1)} collective-permute-done((f32[24,512]{1,0:T(8,128)S(1)}, f32[24,512]{1,0:T(8,128)S(1)}, u32[]{:S(2)}, u32[]{:S(2)}) %collective-permute-start.10) | collective-permute-done | bytes 49184 | tf_op jit(solution)/shard_map/ppermute | solution.py:591
  48.5 1.7 %second_pass.1 = (f32[128,512]{1,0:T(8,128)S(1)}, f32[8,512]{1,0:T(8,128)S(1)}, f32[8,512]{1,0:T(8,128)S(1)}) custom-call(f32[208,512]{1,0:T(8,128)S(1)} %get-tuple-element.47.t_ref, f32[144,512]{1,0:T(8,128)S(1)} %get-tuple-element.52.refs_0_, f32[40,512]{1,0:T(8,128)S(1)} %get-tuple-element.53.refs_1_, f32[40,512]{1,0:T(8,128)S(1)} %get-tuple-element.54.refs_2_, ...), custom_call_target="tpu_custom_call" | custom-call | tf_op jit(solution)/shard_map/second_pass/pallas_call | solution.py:565
  50.2 1.6 %collective-permute-start.11 = (f32[8,512]{1,0:T(8,128)S(1)}, f32[8,512]{1,0:T(8,128)S(1)}, u32[]{:S(2)}, u32[]{:S(2)}) collective-permute-start(f32[8,512]{1,0:T(8,128)S(1)} %get-tuple-element.60), channel_id=1, source_target_pairs={{0,8},{1,2},{2,1},{3,4},{4,3},{5,6},{6,5},{7,15},{8,0},{9,10},{10,... | collective-permute-start | bytes 49160 | tf_op jit(solution)/shard_map/ppermute | solution.py:585
  51.8 0.0 collective-permute-start.12
  51.8 3.2 %collective-permute-done.11.ml_ref = f32[8,512]{1,0:T(8,128)S(1)} collective-permute-done((f32[8,512]{1,0:T(8,128)S(1)}, f32[8,512]{1,0:T(8,128)S(1)}, u32[]{:S(2)}, u32[]{:S(2)}) %collective-permute-start.11) | collective-permute-done | bytes 16416 | tf_op jit(solution)/shard_map/ppermute | solution.py:585
  55.0 0.5 collective-permute-done.12.mr_ref
  55.6 0.1 last_x.1
  55.6 0.1 collective-permute-start.14
  55.7 4.5 %collective-permute-start.13 = (f32[16,512]{1,0:T(8,128)S(1)}, f32[16,512]{1,0:T(8,128)S(1)}, u32[]{:S(2)}, u32[]{:S(2)}) collective-permute-start(f32[16,512]{1,0:T(8,128)S(1)} %get-tuple-element.62), channel_id=1, source_target_pairs={{0,1},{1,0},{2,3},{3,2},{4,5},{5,4},{6,7},{7,6},{8,16},{9,17},{10,... | collective-permute-start | bytes 98312 | tf_op jit(solution)/shard_map/ppermute | solution.py:602
  60.2 2.6 %collective-permute-done.13.out_msg_ref = f32[16,512]{1,0:T(8,128)S(1)} collective-permute-done((f32[16,512]{1,0:T(8,128)S(1)}, f32[16,512]{1,0:T(8,128)S(1)}, u32[]{:S(2)}, u32[]{:S(2)}) %collective-permute-start.13) | collective-permute-done | bytes 32800 | tf_op jit(solution)/shard_map/ppermute | solution.py:602
  62.8 0.0 collective-permute-done.14.in_ref
  62.8 0.9 %last_z.1 = (f32[128,512]{1,0:T(8,128)}, f32[384,512]{1,0:T(8,128)}) custom-call(f32[16,512]{1,0:T(8,128)S(1)} %collective-permute-done.13.out_msg_ref, f32[64,512]{1,0:T(8,128)S(1)} %collective-permute-done.14.in_ref, f32[48,512]{1,0:T(8,128)S(1)} %collective-permute-done.5.refs_0_.f_out_ref, ...), custom_call_target="tpu_custom_call", output_to_operand_aliasing={{1}: (6, {})} | custom-call | tf_op jit(solution)/shard_map/last_z/pallas_call | solution.py:565
  (10 shorter events, 0.1 us)
Async XLA Ops:
  0.6 13.7 %copy-start.4 = (bf16[512,256]{1,0:T(8,128)(2,1)S(1)}, bf16[512,256]{1,0:T(8,128)(2,1)}, u32[]{:S(2)}) copy-start(bf16[512,256]{1,0:T(8,128)(2,1)} %constant.54.clone.refs_8_.wd_y) | copy-start | bytes 786436
  0.6 13.7 %copy-start.6 = (bf16[144,432]{1,0:T(8,128)(2,1)S(1)}, bf16[144,432]{1,0:T(8,128)(2,1)}, u32[]{:S(2)}) copy-start(bf16[144,432]{1,0:T(8,128)(2,1)} %constant.47.clone.xe_w) | copy-start | bytes 373252
  0.7 13.7 %copy-start.10 = (bf16[144,864]{1,0:T(8,128)(2,1)S(1)}, bf16[144,864]{1,0:T(8,128)(2,1)}, u32[]{:S(2)}) copy-start(bf16[144,864]{1,0:T(8,128)(2,1)} %constant.52.clone.z_div) | copy-start | bytes 746500
  0.7 13.7 %copy-start.12 = (bf16[144,432]{1,0:T(8,128)(2,1)S(1)}, bf16[144,432]{1,0:T(8,128)(2,1)}, u32[]{:S(2)}) copy-start(bf16[144,432]{1,0:T(8,128)(2,1)} %constant.49.clone.xe_wd) | copy-start | bytes 373252
  0.7 13.7 %copy-start.14 = (f32[1,512]{1,0:T(1,128)S(1)}, f32[1,512]{1,0:T(1,128)}, u32[]{:S(2)}) copy-start(f32[1,512]{1,0:T(1,128)} %constant.56.clone.refs_9_.w_y) | copy-start | bytes 6148
  0.7 25.8 %copy-start.1 = (bf16[1024,640]{1,0:T(8,128)(2,1)S(1)}, bf16[1024,640]{1,0:T(8,128)(2,1)}, u32[]{:S(2)}) copy-start(bf16[1024,640]{1,0:T(8,128)(2,1)} %constant.60.clone.refs_7_) | copy-start | bytes 3932164
  7.7 18.8 %copy-start = (bf16[1280,512]{1,0:T(8,128)(2,1)S(1)}, bf16[1280,512]{1,0:T(8,128)(2,1)}, u32[]{:S(2)}) copy-start(bf16[1280,512]{1,0:T(8,128)(2,1)} %constant.61.clone.refs_10_) | copy-start | bytes 3932164
  7.7 18.8 %copy-start.2 = (f32[208,640]{1,0:T(8,128)S(1)}, f32[208,640]{1,0:T(8,128)}, u32[]{:S(2)}) copy-start(f32[208,640]{1,0:T(8,128)} %constant.62.clone.refs_8_) | copy-start | bytes 1597444
  7.7 18.7 %copy-start.5 = (bf16[128,624]{1,0:T(8,128)(2,1)S(1)}, bf16[128,624]{1,0:T(8,128)(2,1)}, u32[]{:S(2)}) copy-start(bf16[128,624]{1,0:T(8,128)(2,1)} %constant.59.clone.refs_9_) | copy-start | bytes 479236
  7.8 18.7 %copy-start.7 = (bf16[208,1152]{1,0:T(8,128)(2,1)S(1)}, bf16[208,1152]{1,0:T(8,128)(2,1)}, u32[]{:S(2)}) copy-start(bf16[208,1152]{1,0:T(8,128)(2,1)} %constant.57.clone.refs_6_) | copy-start | bytes 1437700
  7.8 6.2 %collective-permute-start = (f32[48,512]{1,0:T(8,128)S(1)}, f32[48,512]{1,0:T(8,128)S(1)}, u32[]{:S(2)}, u32[]{:S(2)}) collective-permute-start(f32[48,512]{1,0:T(8,128)S(1)} %get-tuple-element.36), channel_id=1, source_target_pairs={{0,8},{1,2},{2,1},{3,4},{4,3},{5,6},{6,5},{7,15},{8,0},{9,10},{10,... | collective-permute-start | bytes 294920 | tf_op jit(solution)/shard_map/ppermute | solution.py:585
  9.7 4.6 %collective-permute-start.1 = (f32[48,512]{1,0:T(8,128)S(1)}, f32[48,512]{1,0:T(8,128)S(1)}, u32[]{:S(2)}, u32[]{:S(2)}) collective-permute-start(f32[48,512]{1,0:T(8,128)S(1)} %get-tuple-element.37), channel_id=1, source_target_pairs={{0,1},{1,0},{2,3},{3,2},{4,5},{5,4},{6,7},{7,6},{8,9},{9,8},{10,11... | collective-permute-start | bytes 294920 | tf_op jit(solution)/shard_map/ppermute | solution.py:586
  15.8 1.4 %collective-permute-start.2 = (f32[56,512]{1,0:T(8,128)S(1)}, f32[56,512]{1,0:T(8,128)S(1)}, u32[]{:S(2)}, u32[]{:S(2)}) collective-permute-start(f32[56,512]{1,0:T(8,128)S(1)} %get-tuple-element.41), channel_id=1, source_target_pairs={{0,8},{8,0},{16,24},{24,16},{32,40},{40,32},{48,56},{56,48},{64,72... | collective-permute-start | bytes 344072 | tf_op jit(solution)/shard_map/ppermute | solution.py:591
  17.2 7.9 %collective-permute-start.3 = (f32[56,512]{1,0:T(8,128)S(1)}, f32[56,512]{1,0:T(8,128)S(1)}, u32[]{:S(2)}, u32[]{:S(2)}) collective-permute-start(f32[56,512]{1,0:T(8,128)S(1)} %get-tuple-element.46), channel_id=1, source_target_pairs={{0,1},{1,0},{2,3},{3,2},{4,5},{5,4},{6,7},{7,6},{8,16},{9,17},{10,... | collective-permute-start | bytes 344072 | tf_op jit(solution)/shard_map/ppermute | solution.py:602
  21.8 7.7 %collective-permute-start.5 = (f32[48,512]{1,0:T(8,128)S(1)}, f32[48,512]{1,0:T(8,128)S(1)}, u32[]{:S(2)}, u32[]{:S(2)}) collective-permute-start(f32[48,512]{1,0:T(8,128)S(1)} %get-tuple-element.49), channel_id=1, source_target_pairs={{0,1},{1,0},{2,3},{3,2},{4,5},{5,4},{6,7},{7,6},{8,16},{9,17},{10,... | collective-permute-start | bytes 294920 | tf_op jit(solution)/shard_map/ppermute | solution.py:602
  25.2 1.3 %collective-permute-start.4 = (f32[24,512]{1,0:T(8,128)S(1)}, f32[24,512]{1,0:T(8,128)S(1)}, u32[]{:S(2)}, u32[]{:S(2)}) collective-permute-start(f32[24,512]{1,0:T(8,128)S(1)} %div_out_far.1), channel_id=1, source_target_pairs={{0,8},{8,0},{16,24},{24,16},{32,40},{40,32},{48,56},{56,48},{64,72... | collective-permute-start | bytes 147464 | tf_op jit(solution)/shard_map/ppermute | solution.py:591
  26.5 3.0 %copy-start.3 = (bf16[512,256]{1,0:T(8,128)(2,1)S(1)}, bf16[512,256]{1,0:T(8,128)(2,1)}, u32[]{:S(2)}) copy-start(bf16[512,256]{1,0:T(8,128)(2,1)} %constant.55.clone.k_y) | copy-start | bytes 786436
  26.5 3.0 %copy-start.13 = (bf16[32,384]{1,0:T(8,128)(2,1)S(1)}, bf16[32,384]{1,0:T(8,128)(2,1)}, u32[]{:S(2)}) copy-start(bf16[32,384]{1,0:T(8,128)(2,1)} %constant.46.clone.refs_6_.xm_w) | copy-start | bytes 73732
  26.5 3.0 %copy-start.15 = (bf16[32,384]{1,0:T(8,128)(2,1)S(1)}, bf16[32,384]{1,0:T(8,128)(2,1)}, u32[]{:S(2)}) copy-start(bf16[32,384]{1,0:T(8,128)(2,1)} %constant.50.clone.xm_k) | copy-start | bytes 73732
  26.5 10.0 %copy-start.9 = (bf16[144,864]{1,0:T(8,128)(2,1)S(1)}, bf16[144,864]{1,0:T(8,128)(2,1)}, u32[]{:S(2)}) copy-start(bf16[144,864]{1,0:T(8,128)(2,1)} %constant.53.clone.z_st) | copy-start | bytes 746500
  26.6 10.0 %copy-start.11 = (bf16[144,432]{1,0:T(8,128)(2,1)S(1)}, bf16[144,432]{1,0:T(8,128)(2,1)}, u32[]{:S(2)}) copy-start(bf16[144,432]{1,0:T(8,128)(2,1)} %constant.51.clone.xe_k) | copy-start | bytes 373252
  28.2 20.3 %copy-start.8 = (bf16[208,1152]{1,0:T(8,128)(2,1)S(1)}, bf16[208,1152]{1,0:T(8,128)(2,1)}, u32[]{:S(2)}) copy-start(bf16[208,1152]{1,0:T(8,128)(2,1)} %constant.58.clone.refs_6_) | copy-start | bytes 1437700
  30.0 5.5 %collective-permute-start.6 = (f32[32,512]{1,0:T(8,128)S(1)}, f32[32,512]{1,0:T(8,128)S(1)}, u32[]{:S(2)}, u32[]{:S(2)}) collective-permute-start(f32[32,512]{1,0:T(8,128)S(1)} %get-tuple-element.50), channel_id=1, source_target_pairs={{0,8},{1,2},{2,1},{3,4},{4,3},{5,6},{6,5},{7,15},{8,0},{9,10},{10,... | collective-permute-start | bytes 196616 | tf_op jit(solution)/shard_map/ppermute | solution.py:585
  32.3 4.3 %collective-permute-start.7 = (f32[32,512]{1,0:T(8,128)S(1)}, f32[32,512]{1,0:T(8,128)S(1)}, u32[]{:S(2)}, u32[]{:S(2)}) collective-permute-start(f32[32,512]{1,0:T(8,128)S(1)} %get-tuple-element.51), channel_id=1, source_target_pairs={{0,1},{1,0},{2,3},{3,2},{4,5},{5,4},{6,7},{7,6},{8,9},{9,8},{10,11... | collective-permute-start | bytes 196616 | tf_op jit(solution)/shard_map/ppermute | solution.py:586
  37.7 1.4 %collective-permute-start.8 = (f32[56,512]{1,0:T(8,128)S(1)}, f32[56,512]{1,0:T(8,128)S(1)}, u32[]{:S(2)}, u32[]{:S(2)}) collective-permute-start(f32[56,512]{1,0:T(8,128)S(1)} %get-tuple-element.55), channel_id=1, source_target_pairs={{0,8},{8,0},{16,24},{24,16},{32,40},{40,32},{48,56},{56,48},{64,72... | collective-permute-start | bytes 344072 | tf_op jit(solution)/shard_map/ppermute | solution.py:591
  39.1 7.9 %collective-permute-start.9 = (f32[56,512]{1,0:T(8,128)S(1)}, f32[56,512]{1,0:T(8,128)S(1)}, u32[]{:S(2)}, u32[]{:S(2)}) collective-permute-start(f32[56,512]{1,0:T(8,128)S(1)} %stiff_out.1), channel_id=1, source_target_pairs={{0,1},{1,0},{2,3},{3,2},{4,5},{5,4},{6,7},{7,6},{8,16},{9,17},{10,... | collective-permute-start | bytes 344072 | tf_op jit(solution)/shard_map/ppermute | solution.py:602
  47.0 1.5 %collective-permute-start.10 = (f32[24,512]{1,0:T(8,128)S(1)}, f32[24,512]{1,0:T(8,128)S(1)}, u32[]{:S(2)}, u32[]{:S(2)}) collective-permute-start(f32[24,512]{1,0:T(8,128)S(1)} %stiff_out_far.1), channel_id=1, source_target_pairs={{0,8},{8,0},{16,24},{24,16},{32,40},{40,32},{48,56},{56,48},{64,72... | collective-permute-start | bytes 147464 | tf_op jit(solution)/shard_map/ppermute | solution.py:591
  50.2 4.9 %collective-permute-start.11 = (f32[8,512]{1,0:T(8,128)S(1)}, f32[8,512]{1,0:T(8,128)S(1)}, u32[]{:S(2)}, u32[]{:S(2)}) collective-permute-start(f32[8,512]{1,0:T(8,128)S(1)} %get-tuple-element.60), channel_id=1, source_target_pairs={{0,8},{1,2},{2,1},{3,4},{4,3},{5,6},{6,5},{7,15},{8,0},{9,10},{10,... | collective-permute-start | bytes 49160 | tf_op jit(solution)/shard_map/ppermute | solution.py:585
  51.8 3.7 %collective-permute-start.12 = (f32[8,512]{1,0:T(8,128)S(1)}, f32[8,512]{1,0:T(8,128)S(1)}, u32[]{:S(2)}, u32[]{:S(2)}) collective-permute-start(f32[8,512]{1,0:T(8,128)S(1)} %get-tuple-element.61), channel_id=1, source_target_pairs={{0,1},{1,0},{2,3},{3,2},{4,5},{5,4},{6,7},{7,6},{8,9},{9,8},{10,11... | collective-permute-start | bytes 49160 | tf_op jit(solution)/shard_map/ppermute | solution.py:586
  55.6 7.1 %collective-permute-start.14 = (f32[64,512]{1,0:T(8,128)S(1)}, f32[64,512]{1,0:T(8,128)S(1)}, u32[]{:S(2)}, u32[]{:S(2)}) collective-permute-start(f32[64,512]{1,0:T(8,128)S(1)} %get-tuple-element.63), channel_id=1, source_target_pairs={{0,8},{8,0},{16,24},{24,16},{32,40},{40,32},{48,56},{56,48},{64,72... | collective-permute-start | bytes 393224 | tf_op jit(solution)/shard_map/ppermute | solution.py:591
  55.7 7.0 %collective-permute-start.13 = (f32[16,512]{1,0:T(8,128)S(1)}, f32[16,512]{1,0:T(8,128)S(1)}, u32[]{:S(2)}, u32[]{:S(2)}) collective-permute-start(f32[16,512]{1,0:T(8,128)S(1)} %get-tuple-element.62), channel_id=1, source_target_pairs={{0,1},{1,0},{2,3},{3,2},{4,5},{5,4},{6,7},{7,6},{8,16},{9,17},{10,... | collective-permute-start | bytes 98312 | tf_op jit(solution)/shard_map/ppermute | solution.py:602

commit v6 on v5

--- a/solution.py
+++ b/solution.py
@@ -430,9 +430,10 @@
     out_ref[48:52] += jnp.concatenate([ca * far_l, cb * far_l, ca * far_r, cb * far_r], axis=0)
 
 
-def outer_force_kernel(coefs, f_up, f_down, up_ref, down_ref, in_ref, out_ref, f_out_ref):
+def outer_force_kernel(coefs, f_up, f_down, up_ref, down_ref, in_ref, out_ref, f_out_ref, f_in_ref):
     outer_kernel(coefs, up_ref, down_ref, in_ref, out_ref)
     f_out_ref[...] = jnp.where(is_odd(), f_up[...], f_down[...])
+    f_in_ref[...] = jnp.where(is_odd(), f_down[...], f_up[...])
 
 
 def far_kernel(out_msg_ref, far_ref):
@@ -520,7 +521,7 @@
     to_pairs(r_ref, l_ref)
 
 
-def last_x_kernel(g_ref, gx_ref, ml_ref, mr_ref, f_up, f_down, out_ref, in_msg_ref, out_msg_ref):
+def last_x_kernel(g_ref, gx_ref, ml_ref, mr_ref, out_ref, out_msg_ref, in_msg_ref):
     _, _, has_l, has_r = flags()
     out_ref[...] = g_ref[...] + gx_ref[...]
     ml, mr = from_pairs(ml_ref, mr_ref)
@@ -529,16 +530,16 @@
     odd = is_odd()
     up, down = out_ref[112:], out_ref[:16]
     out_msg_ref[...] = jnp.where(odd, up, down)
-    in_msg_ref[:16] = jnp.where(odd, down, up)
-    in_msg_ref[16:] = jnp.where(odd, f_down[...], f_up[...])
+    in_msg_ref[...] = jnp.where(odd, down, up)
 
 
 def last_z_kernel(
-    out_msg_ref, in_ref, f_out_ref, g_ref, f_up, f_down, _, out_ref, force_ref, face_ref, p_ref, sem
+    out_msg_ref, in_ref, f_out_ref, f_in_ref, g_ref, f_up, f_down, _, out_ref, force_ref, face_ref, p_ref, sem
 ):
     has_b, has_a, _, _ = flags()
     odd = is_odd()
-    inner, flag = in_ref[...], jnp.where(odd, has_a, has_b)
+    flag = jnp.where(odd, has_a, has_b)
+    inner = jnp.concatenate([in_ref[...], f_in_ref[...]], axis=0)
     outer = jnp.concatenate([out_msg_ref[...], f_out_ref[...]], axis=0) * flag
     below, above = jnp.where(odd, inner, outer), jnp.where(odd, outer, inner)
     p_ref[...] = g_ref[...]
@@ -605,11 +606,12 @@
 def meet(up, down, inner_msg, coefs, name, force_faces=()):
     inner = other_core(inner_msg)
     coefs = [[float(t) for t in row] for row in coefs]
-    kernel, outs = (outer_force_kernel, (56, 48)) if force_faces else (outer_kernel, (56,))
+    kernel, outs = (outer_force_kernel, (56, 48, 48)) if force_faces else (outer_kernel, (56,))
     msgs = call(functools.partial(kernel, coefs), name, outs, *force_faces, up, down, inner)
     outer = next_chip(msgs[0])
     (far,) = call(far_kernel, name + "_far", (24,), outer)
-    return inner, outer, other_core(far), *map(next_chip, msgs[1:])
+    faces = [next_chip(msgs[1]), other_core(msgs[2])] if force_faces else []
+    return inner, outer, other_core(far), *faces
 
 
 def shards(velocity, bfield):
@@ -648,7 +650,7 @@
         sems=1,
         hbm_out=(0,),
     )
-    inner, outer, far, f_out = meet(up, down, inner, picks[0], "div_out", (f_up, f_down))
+    inner, outer, far, f_out, f_in = meet(up, down, inner, picks[0], "div_out", (f_up, f_down))
     box_consts = consts("ybox_in", "inv", "box_out", "ybox_out")
     spectral, g = call(
         first_kernel,
@@ -664,7 +666,7 @@
         *box_consts,
     )
     msg_consts = consts("xm_w", "xm_k", "k_y", "w_y")
-    right, left = call(stiff_msg_kernel, "stiff_msg", (32, 32), g, *msg_consts, f_out)
+    right, left = call(stiff_msg_kernel, "stiff_msg", (32, 32), g, *msg_consts, f_out, f_in)
     from_l, from_r = exchange_x(right, left)
     gx, u, up, down, up_face, down_face, inner = call(
         functools.partial(stiff_kernel, ends),
@@ -692,8 +694,8 @@
         *box_consts,
     )
     from_l, from_r = exchange_x(right, left)
-    total, inner, outer = call(
-        last_x_kernel, "last_x", (128, 64, 16), g, gx, from_l, from_r, f_up, f_down
+    total, outer, inner = call(
+        last_x_kernel, "last_x", (128, 16, 16), g, gx, from_l, from_r
     )
     outer, inner = next_chip(outer), other_core(inner)
     pressure, force = call(
@@ -703,15 +705,16 @@
         outer,
         inner,
         f_out,
+        f_in,
         total,
         f_up,
         f_down,
         force,
         scratch=(96, 128),
         sems=7,
-        hbm_in=(6,),
+        hbm_in=(7,),
         hbm_out=(0, 1),
-        alias={6: 1},
+        alias={7: 1},
     )
     return force.reshape(3, 8, 16, 512), pressure.reshape(8, 16, 512)
 

time: 64 us -> 63.8 us (level)
  starting transfers between devices: 20.2 us -> 18.6 us
  waiting for transfers between devices: 28.1 us -> 29.6 us
    ppermute x4, waiting for transfers between devices: 10.4 us -> 12 us  [next_chip(): return lax.ppermute(x, ('wide', 'narrow'), pairs)]
    ppermute x4, starting transfers between devices: 13.7 us -> 12.2 us  [next_chip(): return lax.ppermute(x, ('wide', 'narrow'), pairs)]
    ppermute x5 -> x6, waiting for transfers between devices: 5.06 us -> 5.06 us  [other_core(): return lax.ppermute(x, 'wide', [(i, i + 1 - 2 * (i % 2)) for i in range(n)])]
  transfers between devices with their start and end apart: 15 -> 16, of which waited for: 14 -> 14; matrix products, arithmetic and copies ran while one was open for 0% -> 0% of each run, Pallas kernels for 3% -> 3%
where the time goes in v6:
time: 63.8 us; the launch traced here: 63.7 us
  waiting for transfers between devices  29.6 us (46%)
  starting transfers between devices  18.6 us (29%)
  Pallas kernels  14.3 us (22%)
  between operations  1.08 us (2%)
    pallas_call x12, Pallas kernels, call(): pl.pallas_call(kernel, out_shape=[shape(o) for o in outs], in_specs=[spec...  14.3 us
    ppermute x4, starting transfers between devices, next_chip(): return lax.ppermute(x, ('wide', 'narrow'), pairs)  12.2 us
    ppermute x4, waiting for transfers between devices, next_chip(): return lax.ppermute(x, ('wide', 'narrow'), pairs)  12 us
    ppermute x3, waiting for transfers between devices, exchange_x(): far = lax.ppermute(far, ('wide', 'narrow'), pairs)  10.6 us
    ppermute x3, starting transfers between devices, exchange_x(): far = lax.ppermute(far, ('wide', 'narrow'), pairs)  5.88 us
    ppermute x6, waiting for transfers between devices, other_core(): return lax.ppermute(x, 'wide', [(i, i + 1 - 2 * (i % 2)) for i in range(n)])  5.06 us
    ppermute x3, waiting for transfers between devices, exchange_x(): lax.ppermute(near, 'narrow', [(k, k + 1 - 2 * (k % 2)) for k in range(nx)])  1.98 us
  transfers between devices with their start and end apart: 16, of which 14 were waited for; matrix products, arithmetic and copies ran while one was open for 0% of the time, Pallas kernels for 3%

profile of v6, /device:TPU:6, one launch (start us, length us, event | category | flops | bytes accessed | tf_op | source)
XLA Modules:
  0.0 63.7 jit_solution(7487875972398721432)
XLA Ops:
  0.6 0.0 copy-start.4
  0.6 0.0 copy-start.6
  0.7 0.0 copy-start.10
  0.7 0.0 copy-start.12
  0.7 0.0 copy-start.14
  0.7 0.0 copy-start.1
  0.7 7.0 %force.1 = (f32[384,512]{1,0:T(8,128)S(1)}, f32[48,512]{1,0:T(8,128)S(1)}, f32[48,512]{1,0:T(8,128)S(1)}) custom-call(f32[3,8,16,512]{3,2,1,0:T(8,128)} %refs_0_.1, f32[8,16,512]{2,1,0:T(8,128)} %refs_1_.1, bf16[512,768]{1,0:T(8,128)(2,1)} %constant.42.clone.refs_2_, bf16[432,192]{1,0:T(8,128)(2,1)} %constant.43.clone.refs_3_, ...), custom_call_target="tpu_custom_call" | custom-call | tf_op jit(solution)/shard_map/force/pallas_call | solution.py:566
  7.7 0.0 copy-start
  7.7 0.0 copy-start.2
  7.7 0.0 copy-start.5
  7.8 0.0 copy-start.7
  7.8 1.9 %collective-permute-start = (f32[48,512]{1,0:T(8,128)S(1)}, f32[48,512]{1,0:T(8,128)S(1)}, u32[]{:S(2)}, u32[]{:S(2)}) collective-permute-start(f32[48,512]{1,0:T(8,128)S(1)} %get-tuple-element.37), channel_id=1, source_target_pairs={{0,8},{1,2},{2,1},{3,4},{4,3},{5,6},{6,5},{7,15},{8,0},{9,10},{10,... | collective-permute-start | bytes 294920 | tf_op jit(solution)/shard_map/ppermute | solution.py:586
  9.7 0.0 collective-permute-start.1
  9.7 4.2 %collective-permute-done.ml_ref = f32[48,512]{1,0:T(8,128)S(1)} collective-permute-done((f32[48,512]{1,0:T(8,128)S(1)}, f32[48,512]{1,0:T(8,128)S(1)}, u32[]{:S(2)}, u32[]{:S(2)}) %collective-permute-start) | collective-permute-done | bytes 98336 | tf_op jit(solution)/shard_map/ppermute | solution.py:586
  13.9 0.4 collective-permute-done.1.mr_ref
  14.3 0.0 copy-done.4
  14.3 0.0 copy-done.6
  14.3 0.0 copy-done.10
  14.3 0.0 copy-done.12
  14.3 0.0 copy-done.14
  14.3 1.4 %div.1 = (f32[384,512]{1,0:T(8,128)}, f32[48,512]{1,0:T(8,128)S(1)}, f32[48,512]{1,0:T(8,128)S(1)}, f32[144,512]{1,0:T(8,128)S(1)}, f32[56,512]{1,0:T(8,128)S(1)...) custom-call(f32[384,512]{1,0:T(8,128)S(1)} %get-tuple-element.36.f_ref, ...), custom_call_target="tpu_custom_call" | custom-call | tf_op jit(solution)/shard_map/div/pallas_call | solution.py:566
  15.8 0.1 collective-permute-start.2
  15.9 1.3 %collective-permute-done.2.in_ref.refs_3_ = f32[56,512]{1,0:T(8,128)S(1)} collective-permute-done((f32[56,512]{1,0:T(8,128)S(1)}, f32[56,512]{1,0:T(8,128)S(1)}, u32[]{:S(2)}, u32[]{:S(2)}) %collective-permute-start.2) | collective-permute-done | bytes 114720 | tf_op jit(solution)/shard_map/ppermute | solution.py:592
  17.3 4.6 %collective-permute-start.3 = (f32[56,512]{1,0:T(8,128)S(1)}, f32[56,512]{1,0:T(8,128)S(1)}, u32[]{:S(2)}, u32[]{:S(2)}) collective-permute-start(f32[56,512]{1,0:T(8,128)S(1)} %get-tuple-element.47), channel_id=1, source_target_pairs={{0,1},{1,0},{2,3},{3,2},{4,5},{5,4},{6,7},{7,6},{8,16},{9,17},{10,... | collective-permute-start | bytes 344072 | tf_op jit(solution)/shard_map/ppermute | solution.py:603
  21.8 0.9 %collective-permute-start.5 = (f32[48,512]{1,0:T(8,128)S(1)}, f32[48,512]{1,0:T(8,128)S(1)}, u32[]{:S(2)}, u32[]{:S(2)}) collective-permute-start(f32[48,512]{1,0:T(8,128)S(1)} %get-tuple-element.50), channel_id=1, source_target_pairs={{0,1},{1,0},{2,3},{3,2},{4,5},{5,4},{6,7},{7,6},{8,16},{9,17},{10,... | collective-permute-start | bytes 294920 | tf_op jit(solution)/shard_map/ppermute | solution.py:603
  22.7 0.0 collective-permute-start.6
  22.7 2.5 %collective-permute-done.3.out_msg_ref.refs_4_ = f32[56,512]{1,0:T(8,128)S(1)} collective-permute-done((f32[56,512]{1,0:T(8,128)S(1)}, f32[56,512]{1,0:T(8,128)S(1)}, u32[]{:S(2)}, u32[]{:S(2)}) %collective-permute-start.3) | collective-permute-done | bytes 114720 | tf_op jit(solution)/shard_map/ppermute | solution.py:603
  25.2 0.1 collective-permute-start.4
  25.3 1.2 %collective-permute-done.4.refs_5_ = f32[24,512]{1,0:T(8,128)S(1)} collective-permute-done((f32[24,512]{1,0:T(8,128)S(1)}, f32[24,512]{1,0:T(8,128)S(1)}, u32[]{:S(2)}, u32[]{:S(2)}) %collective-permute-start.4) | collective-permute-done | bytes 49184 | tf_op jit(solution)/shard_map/ppermute | solution.py:592
  26.5 0.0 copy-done.1
  26.5 0.0 copy-done
  26.5 0.0 copy-start.3
  26.5 0.0 copy-start.13
  26.5 0.0 copy-start.15
  26.6 0.0 copy-start.9
  26.6 0.0 copy-start.11
  26.6 1.6 %first_pass.1 = (f32[208,512]{1,0:T(8,128)S(1)}, f32[128,512]{1,0:T(8,128)S(1)}) custom-call(f32[144,512]{1,0:T(8,128)S(1)} %get-tuple-element.39.refs_0_, f32[40,512]{1,0:T(8,128)S(1)} %get-tuple-element.40.refs_1_, f32[40,512]{1,0:T(8,128)S(1)} %get-tuple-element.41.refs_2_, f32[56,512]{1,0:T(8,128)S(1)} %collective-permute-done.2.in_ref.refs_3_, ...), custom_call_target="tpu_custom_call" | custom-call | tf_op jit(solution)/shard_map/first_pass/pallas_call | solution.py:566
  28.2 1.3 %collective-permute-done.5.refs_0_.f_out_ref = f32[48,512]{1,0:T(8,128)S(1)} collective-permute-done((f32[48,512]{1,0:T(8,128)S(1)}, f32[48,512]{1,0:T(8,128)S(1)}, u32[]{:S(2)}, u32[]{:S(2)}) %collective-permute-start.5) | collective-permute-done | bytes 98336 | tf_op jit(solution)/shard_map/ppermute | solution.py:603
  29.5 0.0 collective-permute-done.6.refs_1_.f_in_ref
  29.5 0.0 copy-start.8
  29.5 0.5 stiff_msg.1
  30.0 2.3 %collective-permute-start.7 = (f32[32,512]{1,0:T(8,128)S(1)}, f32[32,512]{1,0:T(8,128)S(1)}, u32[]{:S(2)}, u32[]{:S(2)}) collective-permute-start(f32[32,512]{1,0:T(8,128)S(1)} %get-tuple-element.52), channel_id=1, source_target_pairs={{0,8},{1,2},{2,1},{3,4},{4,3},{5,6},{6,5},{7,15},{8,0},{9,10},{10,... | collective-permute-start | bytes 196616 | tf_op jit(solution)/shard_map/ppermute | solution.py:586
  32.3 0.0 collective-permute-start.8
  32.3 3.2 %collective-permute-done.7.ml_ref = f32[32,512]{1,0:T(8,128)S(1)} collective-permute-done((f32[32,512]{1,0:T(8,128)S(1)}, f32[32,512]{1,0:T(8,128)S(1)}, u32[]{:S(2)}, u32[]{:S(2)}) %collective-permute-start.7) | collective-permute-done | bytes 65568 | tf_op jit(solution)/shard_map/ppermute | solution.py:586
  35.5 1.1 %collective-permute-done.8.mr_ref = f32[32,512]{1,0:T(8,128)S(1)} collective-permute-done((f32[32,512]{1,0:T(8,128)S(1)}, f32[32,512]{1,0:T(8,128)S(1)}, u32[]{:S(2)}, u32[]{:S(2)}) %collective-permute-start.8) | collective-permute-done | bytes 65568 | tf_op jit(solution)/shard_map/ppermute | solution.py:587
  36.6 1.1 %stiff.1 = (f32[128,512]{1,0:T(8,128)S(1)}, f32[144,512]{1,0:T(8,128)S(1)}, f32[56,512]{1,0:T(8,128)S(1)}, f32[56,512]{1,0:T(8,128)S(1)}, f32[40,512]{1,0:T(8,12...) custom-call(f32[128,512]{1,0:T(8,128)S(1)} %get-tuple-element.49.g_ref, ...), custom_call_target="tpu_custom_call" | custom-call | tf_op jit(solution)/shard_map/stiff/pallas_call | solution.py:566
  37.7 0.1 collective-permute-start.9
  37.8 1.3 %collective-permute-done.9.in_ref.refs_3_ = f32[56,512]{1,0:T(8,128)S(1)} collective-permute-done((f32[56,512]{1,0:T(8,128)S(1)}, f32[56,512]{1,0:T(8,128)S(1)}, u32[]{:S(2)}, u32[]{:S(2)}) %collective-permute-start.9) | collective-permute-done | bytes 114720 | tf_op jit(solution)/shard_map/ppermute | solution.py:592
  39.1 3.7 %collective-permute-start.10 = (f32[56,512]{1,0:T(8,128)S(1)}, f32[56,512]{1,0:T(8,128)S(1)}, u32[]{:S(2)}, u32[]{:S(2)}) collective-permute-start(f32[56,512]{1,0:T(8,128)S(1)} %stiff_out.1), channel_id=1, source_target_pairs={{0,1},{1,0},{2,3},{3,2},{4,5},{5,4},{6,7},{7,6},{8,16},{9,17},{10,... | collective-permute-start | bytes 344072 | tf_op jit(solution)/shard_map/ppermute | solution.py:603
  42.9 4.2 %collective-permute-done.10.out_msg_ref.refs_4_ = f32[56,512]{1,0:T(8,128)S(1)} collective-permute-done((f32[56,512]{1,0:T(8,128)S(1)}, f32[56,512]{1,0:T(8,128)S(1)}, u32[]{:S(2)}, u32[]{:S(2)}) %collective-permute-start.10) | collective-permute-done | bytes 114720 | tf_op jit(solution)/shard_map/ppermute | solution.py:603
  47.1 0.3 collective-permute-start.11
  47.3 1.2 %collective-permute-done.11.refs_5_ = f32[24,512]{1,0:T(8,128)S(1)} collective-permute-done((f32[24,512]{1,0:T(8,128)S(1)}, f32[24,512]{1,0:T(8,128)S(1)}, u32[]{:S(2)}, u32[]{:S(2)}) %collective-permute-start.11) | collective-permute-done | bytes 49184 | tf_op jit(solution)/shard_map/ppermute | solution.py:592
  48.5 0.0 copy-done.8
  48.5 1.7 %second_pass.1 = (f32[128,512]{1,0:T(8,128)S(1)}, f32[8,512]{1,0:T(8,128)S(1)}, f32[8,512]{1,0:T(8,128)S(1)}) custom-call(f32[208,512]{1,0:T(8,128)S(1)} %get-tuple-element.48.t_ref, f32[144,512]{1,0:T(8,128)S(1)} %get-tuple-element.54.refs_0_, f32[40,512]{1,0:T(8,128)S(1)} %get-tuple-element.55.refs_1_, f32[40,512]{1,0:T(8,128)S(1)} %get-tuple-element.56.refs_2_, ...), custom_call_target="tpu_custom_call" | custom-call | tf_op jit(solution)/shard_map/second_pass/pallas_call | solution.py:566
  50.2 1.6 %collective-permute-start.12 = (f32[8,512]{1,0:T(8,128)S(1)}, f32[8,512]{1,0:T(8,128)S(1)}, u32[]{:S(2)}, u32[]{:S(2)}) collective-permute-start(f32[8,512]{1,0:T(8,128)S(1)} %get-tuple-element.62), channel_id=1, source_target_pairs={{0,8},{1,2},{2,1},{3,4},{4,3},{5,6},{6,5},{7,15},{8,0},{9,10},{10,... | collective-permute-start | bytes 49160 | tf_op jit(solution)/shard_map/ppermute | solution.py:586
  51.8 0.0 collective-permute-start.13
  51.8 3.2 %collective-permute-done.12.ml_ref = f32[8,512]{1,0:T(8,128)S(1)} collective-permute-done((f32[8,512]{1,0:T(8,128)S(1)}, f32[8,512]{1,0:T(8,128)S(1)}, u32[]{:S(2)}, u32[]{:S(2)}) %collective-permute-start.12) | collective-permute-done | bytes 16416 | tf_op jit(solution)/shard_map/ppermute | solution.py:586
  55.1 0.5 collective-permute-done.13.mr_ref
  55.6 0.1 last_x.1
  55.6 3.0 %collective-permute-start.14 = (f32[16,512]{1,0:T(8,128)S(1)}, f32[16,512]{1,0:T(8,128)S(1)}, u32[]{:S(2)}, u32[]{:S(2)}) collective-permute-start(f32[16,512]{1,0:T(8,128)S(1)} %get-tuple-element.64), channel_id=1, source_target_pairs={{0,1},{1,0},{2,3},{3,2},{4,5},{5,4},{6,7},{7,6},{8,16},{9,17},{10,... | collective-permute-start | bytes 98312 | tf_op jit(solution)/shard_map/ppermute | solution.py:603
  58.6 0.0 collective-permute-start.15
  58.6 4.0 %collective-permute-done.14.out_msg_ref = f32[16,512]{1,0:T(8,128)S(1)} collective-permute-done((f32[16,512]{1,0:T(8,128)S(1)}, f32[16,512]{1,0:T(8,128)S(1)}, u32[]{:S(2)}, u32[]{:S(2)}) %collective-permute-start.14) | collective-permute-done | bytes 32800 | tf_op jit(solution)/shard_map/ppermute | solution.py:603
  62.7 0.0 collective-permute-done.15.in_ref
  62.7 0.9 %last_z.1 = (f32[128,512]{1,0:T(8,128)}, f32[384,512]{1,0:T(8,128)}) custom-call(f32[16,512]{1,0:T(8,128)S(1)} %collective-permute-done.14.out_msg_ref, f32[16,512]{1,0:T(8,128)S(1)} %collective-permute-done.15.in_ref, f32[48,512]{1,0:T(8,128)S(1)} %collective-permute-done.5.refs_0_.f_out_ref, ...), custom_call_target="tpu_custom_call", output_to_operand_aliasing={{1}: (7, {})} | custom-call | tf_op jit(solution)/shard_map/last_z/pallas_call | solution.py:566
  (12 shorter events, 0.1 us)
Async XLA Ops:
  0.6 13.7 %copy-start.4 = (bf16[512,256]{1,0:T(8,128)(2,1)S(1)}, bf16[512,256]{1,0:T(8,128)(2,1)}, u32[]{:S(2)}) copy-start(bf16[512,256]{1,0:T(8,128)(2,1)} %constant.54.clone.refs_8_.wd_y) | copy-start | bytes 786436
  0.6 13.7 %copy-start.6 = (bf16[144,432]{1,0:T(8,128)(2,1)S(1)}, bf16[144,432]{1,0:T(8,128)(2,1)}, u32[]{:S(2)}) copy-start(bf16[144,432]{1,0:T(8,128)(2,1)} %constant.47.clone.xe_w) | copy-start | bytes 373252
  0.7 13.7 %copy-start.10 = (bf16[144,864]{1,0:T(8,128)(2,1)S(1)}, bf16[144,864]{1,0:T(8,128)(2,1)}, u32[]{:S(2)}) copy-start(bf16[144,864]{1,0:T(8,128)(2,1)} %constant.52.clone.z_div) | copy-start | bytes 746500
  0.7 13.7 %copy-start.12 = (bf16[144,432]{1,0:T(8,128)(2,1)S(1)}, bf16[144,432]{1,0:T(8,128)(2,1)}, u32[]{:S(2)}) copy-start(bf16[144,432]{1,0:T(8,128)(2,1)} %constant.49.clone.xe_wd) | copy-start | bytes 373252
  0.7 13.7 %copy-start.14 = (f32[1,512]{1,0:T(1,128)S(1)}, f32[1,512]{1,0:T(1,128)}, u32[]{:S(2)}) copy-start(f32[1,512]{1,0:T(1,128)} %constant.56.clone.refs_9_.w_y) | copy-start | bytes 6148
  0.7 25.8 %copy-start.1 = (bf16[1024,640]{1,0:T(8,128)(2,1)S(1)}, bf16[1024,640]{1,0:T(8,128)(2,1)}, u32[]{:S(2)}) copy-start(bf16[1024,640]{1,0:T(8,128)(2,1)} %constant.60.clone.refs_7_) | copy-start | bytes 3932164
  7.7 18.8 %copy-start = (bf16[1280,512]{1,0:T(8,128)(2,1)S(1)}, bf16[1280,512]{1,0:T(8,128)(2,1)}, u32[]{:S(2)}) copy-start(bf16[1280,512]{1,0:T(8,128)(2,1)} %constant.61.clone.refs_10_) | copy-start | bytes 3932164
  7.7 18.8 %copy-start.2 = (f32[208,640]{1,0:T(8,128)S(1)}, f32[208,640]{1,0:T(8,128)}, u32[]{:S(2)}) copy-start(f32[208,640]{1,0:T(8,128)} %constant.62.clone.refs_8_) | copy-start | bytes 1597444
  7.7 18.8 %copy-start.5 = (bf16[128,624]{1,0:T(8,128)(2,1)S(1)}, bf16[128,624]{1,0:T(8,128)(2,1)}, u32[]{:S(2)}) copy-start(bf16[128,624]{1,0:T(8,128)(2,1)} %constant.59.clone.refs_9_) | copy-start | bytes 479236
  7.8 18.7 %copy-start.7 = (bf16[208,1152]{1,0:T(8,128)(2,1)S(1)}, bf16[208,1152]{1,0:T(8,128)(2,1)}, u32[]{:S(2)}) copy-start(bf16[208,1152]{1,0:T(8,128)(2,1)} %constant.57.clone.refs_6_) | copy-start | bytes 1437700
  7.8 6.2 %collective-permute-start = (f32[48,512]{1,0:T(8,128)S(1)}, f32[48,512]{1,0:T(8,128)S(1)}, u32[]{:S(2)}, u32[]{:S(2)}) collective-permute-start(f32[48,512]{1,0:T(8,128)S(1)} %get-tuple-element.37), channel_id=1, source_target_pairs={{0,8},{1,2},{2,1},{3,4},{4,3},{5,6},{6,5},{7,15},{8,0},{9,10},{10,... | collective-permute-start | bytes 294920 | tf_op jit(solution)/shard_map/ppermute | solution.py:586
  9.7 4.6 %collective-permute-start.1 = (f32[48,512]{1,0:T(8,128)S(1)}, f32[48,512]{1,0:T(8,128)S(1)}, u32[]{:S(2)}, u32[]{:S(2)}) collective-permute-start(f32[48,512]{1,0:T(8,128)S(1)} %get-tuple-element.38), channel_id=1, source_target_pairs={{0,1},{1,0},{2,3},{3,2},{4,5},{5,4},{6,7},{7,6},{8,9},{9,8},{10,11... | collective-permute-start | bytes 294920 | tf_op jit(solution)/shard_map/ppermute | solution.py:587
  15.8 1.4 %collective-permute-start.2 = (f32[56,512]{1,0:T(8,128)S(1)}, f32[56,512]{1,0:T(8,128)S(1)}, u32[]{:S(2)}, u32[]{:S(2)}) collective-permute-start(f32[56,512]{1,0:T(8,128)S(1)} %get-tuple-element.42), channel_id=1, source_target_pairs={{0,8},{8,0},{16,24},{24,16},{32,40},{40,32},{48,56},{56,48},{64,72... | collective-permute-start | bytes 344072 | tf_op jit(solution)/shard_map/ppermute | solution.py:592
  17.3 7.9 %collective-permute-start.3 = (f32[56,512]{1,0:T(8,128)S(1)}, f32[56,512]{1,0:T(8,128)S(1)}, u32[]{:S(2)}, u32[]{:S(2)}) collective-permute-start(f32[56,512]{1,0:T(8,128)S(1)} %get-tuple-element.47), channel_id=1, source_target_pairs={{0,1},{1,0},{2,3},{3,2},{4,5},{5,4},{6,7},{7,6},{8,16},{9,17},{10,... | collective-permute-start | bytes 344072 | tf_op jit(solution)/shard_map/ppermute | solution.py:603
  21.8 7.7 %collective-permute-start.5 = (f32[48,512]{1,0:T(8,128)S(1)}, f32[48,512]{1,0:T(8,128)S(1)}, u32[]{:S(2)}, u32[]{:S(2)}) collective-permute-start(f32[48,512]{1,0:T(8,128)S(1)} %get-tuple-element.50), channel_id=1, source_target_pairs={{0,1},{1,0},{2,3},{3,2},{4,5},{5,4},{6,7},{7,6},{8,16},{9,17},{10,... | collective-permute-start | bytes 294920 | tf_op jit(solution)/shard_map/ppermute | solution.py:603
  22.7 6.8 %collective-permute-start.6 = (f32[48,512]{1,0:T(8,128)S(1)}, f32[48,512]{1,0:T(8,128)S(1)}, u32[]{:S(2)}, u32[]{:S(2)}) collective-permute-start(f32[48,512]{1,0:T(8,128)S(1)} %get-tuple-element.51), channel_id=1, source_target_pairs={{0,8},{8,0},{16,24},{24,16},{32,40},{40,32},{48,56},{56,48},{64,72... | collective-permute-start | bytes 294920 | tf_op jit(solution)/shard_map/ppermute | solution.py:592
  25.2 1.3 %collective-permute-start.4 = (f32[24,512]{1,0:T(8,128)S(1)}, f32[24,512]{1,0:T(8,128)S(1)}, u32[]{:S(2)}, u32[]{:S(2)}) collective-permute-start(f32[24,512]{1,0:T(8,128)S(1)} %div_out_far.1), channel_id=1, source_target_pairs={{0,8},{8,0},{16,24},{24,16},{32,40},{40,32},{48,56},{56,48},{64,72... | collective-permute-start | bytes 147464 | tf_op jit(solution)/shard_map/ppermute | solution.py:592
  26.5 3.0 %copy-start.3 = (bf16[512,256]{1,0:T(8,128)(2,1)S(1)}, bf16[512,256]{1,0:T(8,128)(2,1)}, u32[]{:S(2)}) copy-start(bf16[512,256]{1,0:T(8,128)(2,1)} %constant.55.clone.k_y) | copy-start | bytes 786436
  26.5 3.0 %copy-start.13 = (bf16[32,384]{1,0:T(8,128)(2,1)S(1)}, bf16[32,384]{1,0:T(8,128)(2,1)}, u32[]{:S(2)}) copy-start(bf16[32,384]{1,0:T(8,128)(2,1)} %constant.46.clone.refs_6_.xm_w) | copy-start | bytes 73732
  26.5 3.0 %copy-start.15 = (bf16[32,384]{1,0:T(8,128)(2,1)S(1)}, bf16[32,384]{1,0:T(8,128)(2,1)}, u32[]{:S(2)}) copy-start(bf16[32,384]{1,0:T(8,128)(2,1)} %constant.50.clone.xm_k) | copy-start | bytes 73732
  26.6 10.1 %copy-start.9 = (bf16[144,864]{1,0:T(8,128)(2,1)S(1)}, bf16[144,864]{1,0:T(8,128)(2,1)}, u32[]{:S(2)}) copy-start(bf16[144,864]{1,0:T(8,128)(2,1)} %constant.53.clone.z_st) | copy-start | bytes 746500
  26.6 10.0 %copy-start.11 = (bf16[144,432]{1,0:T(8,128)(2,1)S(1)}, bf16[144,432]{1,0:T(8,128)(2,1)}, u32[]{:S(2)}) copy-start(bf16[144,432]{1,0:T(8,128)(2,1)} %constant.51.clone.xe_k) | copy-start | bytes 373252
  29.5 19.0 %copy-start.8 = (bf16[208,1152]{1,0:T(8,128)(2,1)S(1)}, bf16[208,1152]{1,0:T(8,128)(2,1)}, u32[]{:S(2)}) copy-start(bf16[208,1152]{1,0:T(8,128)(2,1)} %constant.58.clone.refs_6_) | copy-start | bytes 1437700
  30.0 5.5 %collective-permute-start.7 = (f32[32,512]{1,0:T(8,128)S(1)}, f32[32,512]{1,0:T(8,128)S(1)}, u32[]{:S(2)}, u32[]{:S(2)}) collective-permute-start(f32[32,512]{1,0:T(8,128)S(1)} %get-tuple-element.52), channel_id=1, source_target_pairs={{0,8},{1,2},{2,1},{3,4},{4,3},{5,6},{6,5},{7,15},{8,0},{9,10},{10,... | collective-permute-start | bytes 196616 | tf_op jit(solution)/shard_map/ppermute | solution.py:586
  32.3 4.3 %collective-permute-start.8 = (f32[32,512]{1,0:T(8,128)S(1)}, f32[32,512]{1,0:T(8,128)S(1)}, u32[]{:S(2)}, u32[]{:S(2)}) collective-permute-start(f32[32,512]{1,0:T(8,128)S(1)} %get-tuple-element.53), channel_id=1, source_target_pairs={{0,1},{1,0},{2,3},{3,2},{4,5},{5,4},{6,7},{7,6},{8,9},{9,8},{10,11... | collective-permute-start | bytes 196616 | tf_op jit(solution)/shard_map/ppermute | solution.py:587
  37.7 1.4 %collective-permute-start.9 = (f32[56,512]{1,0:T(8,128)S(1)}, f32[56,512]{1,0:T(8,128)S(1)}, u32[]{:S(2)}, u32[]{:S(2)}) collective-permute-start(f32[56,512]{1,0:T(8,128)S(1)} %get-tuple-element.57), channel_id=1, source_target_pairs={{0,8},{8,0},{16,24},{24,16},{32,40},{40,32},{48,56},{56,48},{64,72... | collective-permute-start | bytes 344072 | tf_op jit(solution)/shard_map/ppermute | solution.py:592
  39.1 7.9 %collective-permute-start.10 = (f32[56,512]{1,0:T(8,128)S(1)}, f32[56,512]{1,0:T(8,128)S(1)}, u32[]{:S(2)}, u32[]{:S(2)}) collective-permute-start(f32[56,512]{1,0:T(8,128)S(1)} %stiff_out.1), channel_id=1, source_target_pairs={{0,1},{1,0},{2,3},{3,2},{4,5},{5,4},{6,7},{7,6},{8,16},{9,17},{10,... | collective-permute-start | bytes 344072 | tf_op jit(solution)/shard_map/ppermute | solution.py:603
  47.1 1.5 %collective-permute-start.11 = (f32[24,512]{1,0:T(8,128)S(1)}, f32[24,512]{1,0:T(8,128)S(1)}, u32[]{:S(2)}, u32[]{:S(2)}) collective-permute-start(f32[24,512]{1,0:T(8,128)S(1)} %stiff_out_far.1), channel_id=1, source_target_pairs={{0,8},{8,0},{16,24},{24,16},{32,40},{40,32},{48,56},{56,48},{64,72... | collective-permute-start | bytes 147464 | tf_op jit(solution)/shard_map/ppermute | solution.py:592
  50.2 4.9 %collective-permute-start.12 = (f32[8,512]{1,0:T(8,128)S(1)}, f32[8,512]{1,0:T(8,128)S(1)}, u32[]{:S(2)}, u32[]{:S(2)}) collective-permute-start(f32[8,512]{1,0:T(8,128)S(1)} %get-tuple-element.62), channel_id=1, source_target_pairs={{0,8},{1,2},{2,1},{3,4},{4,3},{5,6},{6,5},{7,15},{8,0},{9,10},{10,... | collective-permute-start | bytes 49160 | tf_op jit(solution)/shard_map/ppermute | solution.py:586
  51.8 3.7 %collective-permute-start.13 = (f32[8,512]{1,0:T(8,128)S(1)}, f32[8,512]{1,0:T(8,128)S(1)}, u32[]{:S(2)}, u32[]{:S(2)}) collective-permute-start(f32[8,512]{1,0:T(8,128)S(1)} %get-tuple-element.63), channel_id=1, source_target_pairs={{0,1},{1,0},{2,3},{3,2},{4,5},{5,4},{6,7},{7,6},{8,9},{9,8},{10,11... | collective-permute-start | bytes 49160 | tf_op jit(solution)/shard_map/ppermute | solution.py:587
  55.6 7.0 %collective-permute-start.14 = (f32[16,512]{1,0:T(8,128)S(1)}, f32[16,512]{1,0:T(8,128)S(1)}, u32[]{:S(2)}, u32[]{:S(2)}) collective-permute-start(f32[16,512]{1,0:T(8,128)S(1)} %get-tuple-element.64), channel_id=1, source_target_pairs={{0,1},{1,0},{2,3},{3,2},{4,5},{5,4},{6,7},{7,6},{8,16},{9,17},{10,... | collective-permute-start | bytes 98312 | tf_op jit(solution)/shard_map/ppermute | solution.py:603
  58.6 4.1 %collective-permute-start.15 = (f32[16,512]{1,0:T(8,128)S(1)}, f32[16,512]{1,0:T(8,128)S(1)}, u32[]{:S(2)}, u32[]{:S(2)}) collective-permute-start(f32[16,512]{1,0:T(8,128)S(1)} %get-tuple-element.65), channel_id=1, source_target_pairs={{0,8},{8,0},{16,24},{24,16},{32,40},{40,32},{48,56},{56,48},{64,72... | collective-permute-start | bytes 98312 | tf_op jit(solution)/shard_map/ppermute | solution.py:592
